TPU v7x, 128 devices: a whole 4x4x4 slice. The times are simulated.
128 devices in a mesh: batch: 64 (over z, y, x), head: 2 (over core).
Axes of the slice: x: 4, y: 4, z: 4, core: 2. Of those that a mesh axis runs over, the one named last changes fastest.
Arguments:
- q_nope: bfloat16 [4, 64, 16384], P(None, 'batch', 'head'), may hold values from -6 to 6
- q_rope: bfloat16 [4, 64, 8192], P(None, 'batch', 'head'), may hold values from -180 to 180
- up_key: bfloat16 [128, 128, 512], P('head'), may hold values from -0.5 to 0.5
- up_value: bfloat16 [128, 512, 128], P('head'), may hold values from -2 to 2
- pool_latent: bfloat16 [6144, 64, 512], P('batch'), may hold values from -6 to 6
- pool_rope: bfloat16 [6144, 4096], P('batch'), may hold values from -6 to 6
- new_latent: bfloat16 [4, 64, 512], P(None, 'batch'), may hold values from -6 to 6
- new_rope: bfloat16 [64, 256], P('batch'), may hold values from -7 to 7
- page_shard: int32 [64, 352, 1], P('batch'), may hold values from 0 to 63; in each aligned block of 176 rows (0 to 175, 176 to 351, ..., all dimensions but the last counted through in order) at most 5 rows name the same one
- page_slot: int32 [64, 352], P('batch'), may hold values from 0 to 95
Outputs:
- attended: bfloat16 [4, 64, 16384], P(None, 'batch', 'head')
Inputs may be any that keep to these rules, and one draw needn't show every extreme that they name: `page_shard`: in each aligned block of 176 consecutive kept pages of a row, no context shard is named more than 5 times, a bound that some block reaches.
All inputs are finite; a program needn't handle non-finite values.
Results may differ from a plain program's by a relative error of at most 0.038.
Values may be sent and summed in bfloat16 or wider, within the bound.
No kernel may reach another device: no remote copies, remote signals or barrier semaphores. Data moves between devices by JAX's collectives and lax.ppermute only.
A program may use at most 192 MiB of HBM per device.

v0:
```python
import math

import jax
import jax.numpy as jnp
from jax import lax
from jax.sharding import PartitionSpec as P


def placement(sources, capacity, rows_dev):
    row_count, block_len = sources.shape
    matches = sources[:, :, None] == sources[:, None, :]
    earlier = jnp.arange(block_len)[None, :] < jnp.arange(block_len)[:, None]
    rank_of = jnp.sum(matches & earlier[None], axis=2)
    local_row = jnp.arange(row_count, dtype=jnp.int32)[:, None] % rows_dev
    return local_row * capacity + rank_of


def partial_attend(query_lat, query_rope, lat_pages, rope_pages, score_scale):
    row_count = lat_pages.shape[0]
    token_count = lat_pages.shape[1] * lat_pages.shape[2]
    key_rows = lat_pages.reshape(row_count, token_count, lat_pages.shape[3])
    rope_rows = rope_pages.reshape(row_count, token_count, query_rope.shape[2])
    scores = (
        jnp.einsum("rql,rtl->rqt", query_lat, key_rows, preferred_element_type=jnp.float32)
        + jnp.einsum("rqe,rte->rqt", query_rope, rope_rows, preferred_element_type=jnp.float32)
    ) * score_scale
    row_max = jnp.max(scores, axis=2)
    weights = jnp.exp(scores - row_max[..., None])
    total = jnp.sum(weights, axis=2)
    mixed = jnp.einsum(
        "rqt,rtl->rql", weights.astype(jnp.bfloat16), key_rows, preferred_element_type=jnp.float32
    )
    return (row_max, total, mixed)


def combine(first, second):
    row_max = jnp.maximum(first[0], second[0])
    second_scale = jnp.exp(second[0] - row_max)
    total = second_scale * second[1]
    mixed = second_scale[..., None] * second[2]
    return (row_max, total, mixed)


def per_device(
    q_nope,
    q_rope,
    up_key,
    up_value,
    pool_latent,
    pool_rope,
    new_latent,
    new_rope,
    page_shard,
    page_slot,
):
    batch_count = lax.axis_size("batch")
    head_count = lax.axis_size("head")
    head_at = lax.axis_index("head")
    step_count, rows_dev = (q_nope.shape[0], q_nope.shape[1])
    heads_dev, nope_dim, latent = up_key.shape
    value_dim = up_value.shape[2]
    page_len = pool_latent.shape[1]
    rope_dim = pool_rope.shape[1] // page_len
    block_len = page_slot.shape[1] // head_count
    capacity = max(2, 2 * block_len // batch_count)
    slot_count = rows_dev * capacity
    score_scale = 1.0 / math.sqrt(nope_dim + rope_dim)
    sources = lax.dynamic_slice_in_dim(page_shard[:, :, 0], head_at * block_len, block_len, 1)
    slot_ids = lax.dynamic_slice_in_dim(page_slot, head_at * block_len, block_len, 1)
    places = placement(sources, capacity, rows_dev)
    wanted = jnp.zeros((batch_count, slot_count), jnp.int32).at[sources, places].set(slot_ids)
    incoming = lax.all_to_all(wanted, "batch", split_axis=0, concat_axis=0, tiled=True)
    outgoing_lat = pool_latent[incoming]
    outgoing_rope = pool_rope[incoming]
    arrived_lat, arrived_rope = (
        lax.all_to_all(outgoing_lat, "batch", split_axis=0, concat_axis=0, tiled=True),
        lax.all_to_all(outgoing_rope, "batch", split_axis=0, concat_axis=0, tiled=True),
    )
    flat_index = (sources * slot_count + places).reshape(-1)
    kept_lat = arrived_lat.reshape(batch_count * slot_count, page_len, latent)[flat_index]
    kept_lat = kept_lat.reshape(rows_dev, block_len, page_len, latent)
    kept_rope = arrived_rope.reshape(batch_count * slot_count, page_len * rope_dim)[flat_index]
    kept_rope = kept_rope.reshape(rows_dev, block_len, page_len * rope_dim)
    q_heads = q_nope.reshape(step_count, rows_dev, heads_dev, nope_dim)
    absorbed = jnp.einsum(
        "srhn,hnl->rshl", q_heads, up_key, preferred_element_type=jnp.float32
    ).astype(jnp.bfloat16)
    rotated = q_rope.reshape(step_count, rows_dev, heads_dev, rope_dim).transpose(1, 0, 2, 3)
    own_lat = absorbed.reshape(rows_dev, step_count * heads_dev, latent)
    own_rope = rotated.reshape(rows_dev, step_count * heads_dev, rope_dim)
    query_total = step_count * heads_dev
    start_state = (
        jnp.full((rows_dev, query_total), -1e30, jnp.float32),
        jnp.zeros((rows_dev, query_total), jnp.float32),
        jnp.zeros((rows_dev, query_total, latent), jnp.float32),
    )
    state = combine(
        start_state,
        partial_attend(
            own_lat,
            own_rope,
            lax.all_gather(kept_lat, "head", axis=1, tiled=True),
            lax.all_gather(kept_rope, "head", axis=1, tiled=True),
            score_scale,
        ),
    )
    fresh_lat = new_latent.transpose(1, 0, 2)
    fresh_rope = new_rope.reshape(rows_dev, step_count, rope_dim)
    fresh_scores = (
        jnp.einsum("rql,rtl->rqt", own_lat, fresh_lat, preferred_element_type=jnp.float32)
        + jnp.einsum("rqe,rte->rqt", own_rope, fresh_rope, preferred_element_type=jnp.float32)
    ) * score_scale
    step_of = jnp.arange(step_count * heads_dev, dtype=jnp.int32) // heads_dev
    allowed = jnp.arange(step_count, dtype=jnp.int32)[None, :] <= step_of[:, None]
    fresh_scores = jnp.where(allowed[None], fresh_scores, -jnp.inf)
    row_max = jnp.maximum(state[0], jnp.max(fresh_scores, axis=2))
    carried = jnp.exp(state[0] - row_max)
    fresh_weights = jnp.exp(fresh_scores - row_max[..., None])
    total = carried * state[1] + jnp.sum(fresh_weights, axis=2)
    mixed = carried[..., None] * state[2] + jnp.einsum(
        "rqt,rtl->rql",
        fresh_weights.astype(jnp.bfloat16),
        fresh_lat,
        preferred_element_type=jnp.float32,
    )
    latent_out = (
        (mixed / total[..., None])
        .astype(jnp.bfloat16)
        .reshape(rows_dev, step_count, heads_dev, latent)
    )
    projected = jnp.einsum(
        "rshl,hlv->srhv", latent_out, up_value, preferred_element_type=jnp.float32
    )
    return projected.astype(jnp.bfloat16).reshape(step_count, rows_dev, heads_dev * value_dim)


def solution(mesh):
    placed = (
        P(None, "batch", "head"),
        P(None, "batch", "head"),
        P("head", None, None),
        P("head", None, None),
        P("batch", None, None),
        P("batch", None),
        P(None, "batch", None),
        P("batch", None),
        P("batch", None, None),
        P("batch", None),
    )
    return jax.shard_map(
        per_device, mesh=mesh, in_specs=placed, out_specs=P(None, "batch", "head"), check_vma=False
    )
```

profile of v0, /device:TPU:1, one launch (start us, length us, event | category | flops | bytes accessed | tf_op | source)
XLA Modules:
  0.0 601.7 jit_solution(12115419873602420703)
XLA Ops:
  6.5 0.8 compare_select_fusion.3
  7.4 0.2 convert_reduce_fusion
  7.6 0.8 constant_dynamic-slice_fusion
  8.4 8.6 %scatter_fusion = s32[64,5]{0,1:T(8,128)S(1)} fusion(s32[64,5]{0,1:T(8,128)S(1)} %broadcast.193, s32[176]{0:T(256)S(1)} %bitcast.59, s32[176]{0:T(256)S(1)} %bitcast.67), kind=kCustom, calls=%fused_computation.4 | custom fusion | bytes 3520 | tf_op jit(solution)/shard_map/scatter | solution.py:71
  17.0 0.1 copy.26
  17.1 20.2 %all_to_all.22 = s32[64,1,5]{2,1,0:T(1,128)S(1)} all-to-all(s32[64,1,5]{2,1,0:T(1,128)S(1)} %copy.26), channel_id=1, replica_groups=mesh['batch'=64,'head'=2] {'batch'}, dimensions={0} | all-to-all | bytes 2560 | tf_op jit(solution)/shard_map/all_to_all | solution.py:72
  37.3 0.1 reshape.371
  37.4 3.3 gather_fusion.2
  40.7 2.9 reshape.386
  43.6 5.7 all-to-all-start.2
  49.2 14.1 %gather_fusion = bf16[320,64,512]{2,1,0:T(8,128)(2,1)} fusion(bf16[96,64,512]{2,1,0:T(8,128)(2,1)} %param.14, s32[1024]{0:T(1024)S(1)} %pad_clamp_fusion.1), kind=kCustom, calls=%fused_computation | custom fusion | bytes 41944320 | tf_op jit(solution)/shard_map/gather | solution.py:73
  63.4 36.4 %all-to-all-done.2 = bf16[64,5,4096]{2,1,0:T(8,128)(2,1)} async-done(((bf16[64,5,4096]{2,1,0:T(8,128)(2,1)}), bf16[64,5,4096]{2,1,0:T(8,128)(2,1)}, u32[]{:S(2)}, u32[]{:S(2)}) %all-to-all-start.2) | async-done | bytes 2621472 | tf_op jit(solution)/shard_map/all_to_all | solution.py:77
  99.8 11.2 %all-to-all-start.1 = ((bf16[64,5,64,512]{3,2,1,0:T(8,128)(2,1)}), bf16[64,5,64,512]{3,2,1,0:T(8,128)(2,1)}, u32[]{:S(2)}, u32[]{:S(2)}) async-start(bf16[64,5,64,512]{3,2,1,0:T(8,128)(2,1)} %bitcast.56), calls=%async_computation.1 | async-start | bytes 41943040 | tf_op jit(solution)/shard_map/all_to_all | solution.py:76
  111.1 3.4 reshape.361
  114.5 2.6 gather_fusion.3
  117.2 0.2 all-gather.5.cloned.1.call-start
  117.4 360.4 %all-to-all-done.1 = bf16[64,5,64,512]{3,2,1,0:T(8,128)(2,1)} async-done(((bf16[64,5,64,512]{3,2,1,0:T(8,128)(2,1)}), bf16[64,5,64,512]{3,2,1,0:T(8,128)(2,1)}, u32[]{:S(2)}, u32[]{:S(2)}) %all-to-all-start.1) | async-done | bytes 20971552 | tf_op jit(solution)/shard_map/all_to_all | solution.py:76
  477.8 14.8 %gather_fusion.1 = bf16[176,64,512]{2,1,0:T(8,128)(2,1)} fusion(bf16[320,64,512]{2,1,0:T(8,128)(2,1)} %bitcast.12, s32[1024]{0:T(1024)S(1)} %pad_clamp_fusion), kind=kCustom, calls=%fused_computation.1 | custom fusion | bytes 23069376 | tf_op jit(solution)/shard_map/gather | solution.py:80
  492.7 0.7 copy-done.3
  493.4 0.1 reshape.364
  493.6 4.6 fusion.14
  498.2 0.1 reshape.366
  498.3 0.1 fusion.22
  498.5 0.2 fusion.33
  498.7 9.0 %reshape.363 = bf16[22528,64]{1,0:T(8,128)(2,1)} reshape(bf16[352,4096]{1,0:T(8,128)(2,1)} %all-gather.7.cloned.1.call-done) | data formatting | bytes 5767168 | tf_op jit(solution)/shard_map/reshape.24
  507.7 19.5 %convolution_bitcast_fusion = f32[256,22528]{1,0:T(8,128)} fusion(bf16[22528,64]{1,0:T(8,128)(2,1)} %reshape.363, bf16[256,64]{1,0:T(8,128)(2,1)S(1)} %reshape.364), kind=kOutput, calls=%fused_computation.5 | convolution fusion | flops 738197504 | bytes 25985024 | tf_op jit(solution)/shard_map/rqe,rte->rqt/dot_general | solution.py:25
  527.2 9.1 %all-gather.5.cloned.1.call-done = bf16[352,64,512]{2,1,0:T(8,128)(2,1)} async-done(((bf16[176,64,512]{2,1,0:T(8,128)(2,1)}), bf16[352,64,512]{2,1,0:T(8,128)(2,1)}) %all-gather.5.cloned.1.call-update) | async-done | bytes 23068688 | tf_op jit(solution)/shard_map/all_gather | solution.py:102
  536.3 25.2 %fusion.32 = (f32[256]{0:T(256)S(1)}, f32[256,22528]{1,0:T(8,128)}) fusion(f32[256,22528]{1,0:T(8,128)} %convolution_bitcast_fusion, bf16[256,512]{1,0:T(8,128)(2,1)S(1)} %bitcast.61, bf16[22528,512]{1,0:T(8,128)(2,1)} %bitcast.57), kind=kOutput, calls=%fused_computation.62 | convolution fusion | flops 5922881536 | bytes 69469184 | tf_op jit(solution)/shard_map/rql,rtl->rqt/dot_general | solution.py:24
  561.5 10.0 %fusion.1 = f32[256]{0:T(256)S(1)} fusion(f32[256,22528]{1,0:T(8,128)} %get-tuple-element.11, f32[256]{0:T(256)S(1)} %get-tuple-element.10), kind=kLoop, calls=%fused_computation.9 | loop fusion | flops 11534080 | bytes 23070720 | tf_op jit(solution)/shard_map/reduce_sum | solution.py:29
  571.5 17.8 %fusion.10 = f32[256,512]{1,0:T(8,128)S(1)} fusion(bf16[22528,512]{1,0:T(8,128)(2,1)} %bitcast.58, f32[256,22528]{1,0:T(8,128)} %get-tuple-element.11, f32[256]{0:T(256)S(1)} %get-tuple-element.10, f32[256]{0:T(256)S(1)} %get-tuple-element.9, f32[256]{0:T(256)S(1)} %get-tuple-element.6), kind=kOutput, calls=%fused_computation.16 | convolution fusion | flops 5917376512 | bytes 46664704 | tf_op jit(solution)/shard_map/rqt,rtl->rql/dot_general | solution.py:30
  589.3 0.3 fusion.13
  589.6 5.2 fusion.15
  (29 shorter events, 0.3 us)
Async XLA Ops:
  6.5 30.9 %copy-start = (bf16[96,4096]{1,0:T(8,128)(2,1)S(1)}, bf16[96,4096]{1,0:T(8,128)(2,1)}, u32[]{:S(2)}) copy-start(bf16[96,4096]{1,0:T(8,128)(2,1)} %param.15) | copy-start | bytes 2359300
  43.6 56.2 %all-to-all-start.2 = ((bf16[64,5,4096]{2,1,0:T(8,128)(2,1)}), bf16[64,5,4096]{2,1,0:T(8,128)(2,1)}, u32[]{:S(2)}, u32[]{:S(2)}) async-start(bf16[64,5,4096]{2,1,0:T(8,128)(2,1)} %reshape.386), calls=%async_computation.2 | async-start | bytes 8388608 | tf_op jit(solution)/shard_map/all_to_all | solution.py:77
  99.8 378.0 %all-to-all-start.1 = ((bf16[64,5,64,512]{3,2,1,0:T(8,128)(2,1)}), bf16[64,5,64,512]{3,2,1,0:T(8,128)(2,1)}, u32[]{:S(2)}, u32[]{:S(2)}) async-start(bf16[64,5,64,512]{3,2,1,0:T(8,128)(2,1)} %bitcast.56), calls=%async_computation.1 | async-start | bytes 41943040 | tf_op jit(solution)/shard_map/all_to_all | solution.py:76
  111.0 387.7 %all-gather.7.cloned.1.call-start = ((), (), s32[]{:S(2)}) async-start(), calls=%async_computation.4 | async-start | bytes 4325376 | tf_op jit(solution)/shard_map/all_gather | solution.py:103
  117.2 419.1 %all-gather.5.cloned.1.call-start = ((), (), s32[]{:S(2)}) async-start(), calls=%async_computation.3 | async-start | bytes 34603008 | tf_op jit(solution)/shard_map/all_gather | solution.py:102
  492.7 0.8 copy-start.3
  492.7 0.9 copy-start.2
  492.7 5.5 copy-start.5
  492.7 5.6 copy-start.4
  571.5 23.3 %copy-start.1 = (bf16[96,4096]{1,0:T(8,128)(2,1)S(1)}, bf16[96,4096]{1,0:T(8,128)(2,1)}, u32[]{:S(2)}) copy-start(bf16[96,4096]{1,0:T(8,128)(2,1)} %param.15) | copy-start | bytes 2359300
Sparse Core Ops, SparseCore 0:
  117.3 16.1 all-gather.6
  492.8 43.4 all-gather.4
where the time goes:
time: 603 us; the launch traced here: 602 us
  waiting for transfers between devices  406 us (67%)
  matrix products  72.9 us (12%)
  local copies, waits for them, and re-layouts  60.8 us (10%)
  blocking collectives  20.2 us (3%)
  starting transfers between devices  17.1 us (3%)
  between operations  13.6 us (2%)
  other arithmetic  11.1 us (2%)
    all_to_all x1, waiting for transfers between devices, per_device(): lax.all_to_all(outgoing_lat, 'batch', split_axis=0, concat_axis=0, tiled=...  360 us
    all_to_all x1, waiting for transfers between devices, per_device(): lax.all_to_all(outgoing_rope, 'batch', split_axis=0, concat_axis=0, tiled...  36.4 us
    dot_general x1, matrix products, partial_attend(): jnp.einsum('rql,rtl->rqt', query_lat, key_rows, preferred_element_type=jn...  25.2 us
    all_to_all x1, blocking collectives, per_device(): lax.all_to_all(wanted, 'batch', split_axis=0, concat_axis=0, tiled=True)  20.2 us
    dot_general x1, matrix products, partial_attend(): jnp.einsum('rqe,rte->rqt', query_rope, rope_rows, preferred_element_type=...  19.5 us
    dot_general x1, matrix products, partial_attend(): jnp.einsum('rqt,rtl->rql', weights.astype(jnp.bfloat16), key_rows, prefer...  17.8 us
    gather x1, local copies, waits for them, and re-layouts, per_device(): arrived_lat.reshape(batch_count * slot_count, page_len, latent)[flat_index]  14.8 us
    gather x1, local copies, waits for them, and re-layouts, per_device(): outgoing_lat = pool_latent[incoming]  14.1 us
  transfers between devices with their start and end apart: 4, of which 3 were waited for; matrix products, arithmetic and copies ran while one was open for 11% of the time, Pallas kernels for 0%

commit v1 on v0

v1 whole, which is shorter than its diff:
```python
import math

import jax
import jax.numpy as jnp
from jax import lax
from jax.experimental import pallas as pl
from jax.experimental.pallas import tpu as pltpu
from jax.sharding import PartitionSpec as P

MAX_PAGES = 10
NEG = -1e30
VMEM_BYTES = 48 * 1024 * 1024


def absorb_kernel(q_ref, up_ref, out_ref):
    rows, _, nope = q_ref.shape
    latent = up_ref.shape[2]
    q = q_ref[...].astype(jnp.float32).reshape(rows, 2, 8, nope)
    first = lax.broadcasted_iota(jnp.int32, (rows, 8, nope), 1) < 4
    halves = []
    for pair in range(2):
        part = q[:, pair]
        wide = jnp.concatenate(
            [jnp.where(first, part, 0.0), jnp.where(first, 0.0, part)], axis=2
        )
        wide = wide.reshape(rows * 8, 2 * nope).astype(jnp.bfloat16)
        weight = up_ref[2 * pair : 2 * pair + 2].reshape(2 * nope, latent)
        out = jnp.dot(wide, weight, preferred_element_type=jnp.float32)
        halves.append(out.reshape(rows, 8, latent))
    out_ref[...] = jnp.concatenate(halves, axis=1).astype(jnp.bfloat16)


def absorb(packed, up_key):
    rows = packed.shape[0]
    heads, nope, latent = up_key.shape
    groups = heads // 4
    return pl.pallas_call(
        absorb_kernel,
        out_shape=jax.ShapeDtypeStruct((rows, heads * 4, latent), jnp.bfloat16),
        grid=(groups,),
        in_specs=[
            pl.BlockSpec((rows, 16, nope), lambda j: (0, j, 0)),
            pl.BlockSpec((4, nope, latent), lambda j: (j, 0, 0)),
        ],
        out_specs=pl.BlockSpec((rows, 16, latent), lambda j: (0, j, 0)),
        compiler_params=pltpu.CompilerParams(vmem_limit_bytes=VMEM_BYTES),
        name="absorb",
    )(packed, up_key)


def attend_kernel(
    scale, counts_ref, slots_ref, q_ref, rope_ref, lat_ref, keyrope_ref, out_ref, lse_ref,
    keys, rotated
):
    r = pl.program_id(0)
    queries = q_ref.shape[1]
    latent = q_ref.shape[2]
    page = lat_ref.shape[1]
    count = counts_ref[r]

    def run(pages):
        tokens = pages * page
        for k in range(pages):
            slot = slots_ref[r, k]
            keys[k * page : (k + 1) * page, :] = lat_ref[slot]
            rotated[k * page : (k + 1) * page, :] = keyrope_ref[slot]
        key = keys[0:tokens, :]
        key_rope = rotated[0:tokens, :]
        packed = rope_ref[0]
        half = packed.shape[1] // 2
        q_rope = jnp.concatenate([packed[:, :half], packed[:, half:]], axis=0)
        nt = (((1,), (1,)), ((), ()))
        scores = lax.dot_general(q_ref[0], key, nt, preferred_element_type=jnp.float32)
        scores += lax.dot_general(q_rope, key_rope, nt, preferred_element_type=jnp.float32)
        scores *= scale
        token = lax.broadcasted_iota(jnp.int32, (queries, tokens), 1)
        scores = jnp.where(token < count * page, scores, NEG)
        top = jnp.max(scores, axis=1, keepdims=True)
        weights = jnp.exp(scores - top)
        total = jnp.sum(weights, axis=1, keepdims=True)
        mixed = jnp.dot(weights.astype(jnp.bfloat16), key, preferred_element_type=jnp.float32)
        out_ref[0] = (mixed / total).astype(jnp.bfloat16)
        lse = jnp.broadcast_to(top + jnp.log(total), (queries, 128))
        lse_ref[0] = lse.T[0:1, :]

    pl.when(count <= 4)(lambda: run(4))
    pl.when((count > 4) & (count <= 6))(lambda: run(6))
    pl.when((count > 6) & (count <= 8))(lambda: run(8))
    pl.when(count > 8)(lambda: run(10))


def attend(counts, slots, absorbed, packed, pool_latent, pool_rope, scale):
    rows, queries, latent = absorbed.shape
    slots_total, page, _ = pool_latent.shape
    rope = pool_rope.shape[2]
    grid_spec = pltpu.PrefetchScalarGridSpec(
        num_scalar_prefetch=2,
        grid=(rows,),
        in_specs=[
            pl.BlockSpec((1, queries, latent), lambda r, *_: (r, 0, 0)),
            pl.BlockSpec((1, queries // 2, 128), lambda r, *_: (r, 2, 0)),
            pl.BlockSpec((slots_total, page, latent), lambda r, *_: (0, 0, 0)),
            pl.BlockSpec((slots_total, page, rope), lambda r, *_: (0, 0, 0)),
        ],
        out_specs=[
            pl.BlockSpec((1, queries, latent), lambda r, *_: (r, 0, 0)),
            pl.BlockSpec((1, 1, queries), lambda r, *_: (r, 0, 0)),
        ],
        scratch_shapes=[
            pltpu.VMEM((MAX_PAGES * page, latent), jnp.bfloat16),
            pltpu.VMEM((MAX_PAGES * page, rope), jnp.bfloat16),
        ],
    )
    return pl.pallas_call(
        lambda *refs: attend_kernel(scale, *refs),
        out_shape=[
            jax.ShapeDtypeStruct((rows, queries, latent), jnp.bfloat16),
            jax.ShapeDtypeStruct((rows, 1, queries), jnp.float32),
        ],
        grid_spec=grid_spec,
        compiler_params=pltpu.CompilerParams(vmem_limit_bytes=VMEM_BYTES),
        name="attend",
    )(counts, slots, absorbed, packed, pool_latent, pool_rope)


def project_kernel(mixed_ref, up_ref, out_ref):
    rows, _, latent = mixed_ref.shape
    value = up_ref.shape[2]
    mixed = mixed_ref[...].astype(jnp.float32).reshape(rows, 2, 8, latent)
    first = lax.broadcasted_iota(jnp.int32, (rows, 8, value), 1) < 4
    halves = []
    for pair in range(2):
        part = mixed[:, pair].reshape(rows * 8, latent).astype(jnp.bfloat16)
        weight = jnp.concatenate([up_ref[2 * pair], up_ref[2 * pair + 1]], axis=1)
        out = jnp.dot(part, weight, preferred_element_type=jnp.float32)
        out = out.reshape(rows, 8, 2 * value)
        halves.append(jnp.where(first, out[:, :, :value], out[:, :, value:]))
    out_ref[...] = jnp.concatenate(halves, axis=1).astype(jnp.bfloat16)


def project(mixed, up_value):
    rows, queries, latent = mixed.shape
    heads, _, value = up_value.shape
    return pl.pallas_call(
        project_kernel,
        out_shape=jax.ShapeDtypeStruct((rows, queries, value), jnp.bfloat16),
        grid=(heads // 4,),
        in_specs=[
            pl.BlockSpec((rows, 16, latent), lambda j: (0, j, 0)),
            pl.BlockSpec((4, latent, value), lambda j: (j, 0, 0)),
        ],
        out_specs=pl.BlockSpec((rows, 16, value), lambda j: (0, j, 0)),
        compiler_params=pltpu.CompilerParams(vmem_limit_bytes=VMEM_BYTES),
        name="project",
    )(mixed, up_value)


def fresh_part(q_nope, q_rope, up_key, up_value, new_latent, new_rope, scale):
    steps, heads, _ = q_nope.shape
    latent = up_key.shape[2]
    absorbed = jnp.einsum(
        "shn,hnl->hsl", q_nope, up_key, preferred_element_type=jnp.float32
    ).astype(jnp.bfloat16)
    scores = (
        jnp.einsum("hsl,tl->hst", absorbed, new_latent, preferred_element_type=jnp.float32)
        + jnp.einsum("she,te->hst", q_rope, new_rope, preferred_element_type=jnp.float32)
    ) * scale
    at = jnp.arange(steps, dtype=jnp.int32)
    allowed = at[None, None, :] <= at[None, :, None]
    scores = jnp.where(allowed, scores, NEG)
    top = jnp.max(scores, axis=2, keepdims=True)
    weights = jnp.where(allowed, jnp.exp(scores - top), 0.0)
    total = jnp.sum(weights, axis=2, keepdims=True)
    mixed = jnp.einsum(
        "hst,tl->hsl", weights.astype(jnp.bfloat16), new_latent, preferred_element_type=jnp.float32
    )
    mixed = (mixed / total).astype(jnp.bfloat16)
    out = jnp.einsum("hsl,hlv->hsv", mixed, up_value, preferred_element_type=jnp.float32)
    return out, (top + jnp.log(total))[:, :, 0]


def page_lists(page_shard, page_slot, shards):
    kept = page_shard.shape[0]
    rank = jnp.sum(
        (page_shard[:, None] == page_shard[None, :])
        & (jnp.arange(kept)[None, :] < jnp.arange(kept)[:, None]),
        axis=1,
    )
    here = page_shard[None, :] == jnp.arange(shards, dtype=jnp.int32)[:, None]
    counts = jnp.sum(here, axis=1).astype(jnp.int32)
    at = jnp.arange(MAX_PAGES)[None, :, None]
    slots = jnp.sum(
        jnp.where(here[:, None, :] & (rank[None, None, :] == at), page_slot[None, None, :], 0),
        axis=2,
    ).astype(jnp.int32)
    return jnp.concatenate(
        [counts[:, None], slots, jnp.zeros((shards, 15 - MAX_PAGES), jnp.int32)], axis=1
    )


def exchange(x):
    return lax.all_to_all(x, "batch", split_axis=0, concat_axis=0, tiled=True)


def per_device(
    q_nope, q_rope, up_key, up_value, pool_latent, pool_rope,
    new_latent, new_rope, page_shard, page_slot
):
    shards = lax.axis_size("batch")
    steps = q_nope.shape[0]
    heads, nope, latent = up_key.shape
    value = up_value.shape[2]
    slots_total, page, _ = pool_latent.shape
    rope = pool_rope.shape[1] // page
    scale = 1.0 / math.sqrt(nope + rope)
    q_nope = q_nope.reshape(steps, heads, nope)
    q_rope = q_rope.reshape(steps, heads, rope)

    nope_rows = q_nope.transpose(1, 0, 2).reshape(heads * steps, nope)
    rope_rows = q_rope.transpose(1, 0, 2).reshape(2, heads * steps // 2, rope)
    rope_rows = rope_rows.transpose(1, 0, 2).reshape(heads * steps // 2, 2 * rope)
    own = jnp.concatenate([nope_rows, rope_rows], axis=0)
    packed = exchange(jnp.broadcast_to(own[None], (shards,) + own.shape))

    lists = exchange(page_lists(page_shard[0, :, 0], page_slot[0], shards))
    fresh_out, fresh_lse = fresh_part(
        q_nope, q_rope, up_key, up_value, new_latent[:, 0], new_rope.reshape(steps, rope), scale
    )
    pool_rope = pool_rope.reshape(slots_total, page, rope)

    absorbed = absorb(packed, up_key)
    mixed, lse = attend(
        lists[:, 0], lists[:, 1 : 1 + MAX_PAGES], absorbed, packed, pool_latent, pool_rope, scale
    )
    lse = exchange(lse[:, 0, :])
    parts = exchange(project(mixed, up_value))

    fresh_lse = fresh_lse.reshape(1, heads * steps)
    top = jnp.maximum(jnp.max(lse, axis=0, keepdims=True), fresh_lse)
    share = jnp.exp(lse - top)
    fresh_share = jnp.exp(fresh_lse - top)
    total = jnp.sum(share, axis=0, keepdims=True) + fresh_share
    share = share / total
    fresh_share = (fresh_share / total).reshape(heads * steps, 1)
    out = jnp.sum(parts.astype(jnp.float32) * share[:, :, None], axis=0)
    out = out + fresh_share * fresh_out.reshape(heads * steps, value)
    out = out.astype(jnp.bfloat16).reshape(heads, steps, value).transpose(1, 0, 2)
    return out.reshape(steps, 1, heads * value)


def solution(mesh):
    placed = (
        P(None, "batch", "head"),
        P(None, "batch", "head"),
        P("head", None, None),
        P("head", None, None),
        P("batch", None, None),
        P("batch", None),
        P(None, "batch", None),
        P("batch", None),
        P("batch", None, None),
        P("batch", None),
    )
    return jax.shard_map(
        per_device, mesh=mesh, in_specs=placed, out_specs=P(None, "batch", "head"), check_vma=False
    )
```

time: 603 us -> 300 us (0.50)
  waiting for transfers between devices: 406 us -> 126 us
  Pallas kernels: 0 us -> 94.6 us
  matrix products: 72.9 us -> 10.6 us
  local copies, waits for them, and re-layouts: 60.8 us -> 12.9 us
  starting transfers between devices: 17.1 us -> 45.5 us
  blocking collectives: 20.2 us -> 0 us
  between operations: 13.6 us -> 0.24 us
    all_to_all x2 -> x4, waiting for transfers between devices: 397 us -> 126 us  [exchange(): return lax.all_to_all(x, 'batch', split_axis=0, concat_axis=0, tiled=True)]
    pallas_call x0 -> x3, Pallas kernels: none -> 94.6 us  [the longest x1 60.4 us: attend(): pl.pallas_call(lambda *refs: attend_kernel(scale, *refs), out_shape=[jax....]
    dot_general x8 -> x5, matrix products: 72.9 us -> 10.6 us  [the longest x1 5.26 us: fresh_part(): jnp.einsum('hsl,hlv->hsv', mixed, up_value, preferred_element_type=jnp.fl...]
    gather x5 -> x0, local copies, waits for them, and re-layouts: 37.7 us -> none  [the longest x1 14.8 us: per_device(): arrived_lat.reshape(batch_count * slot_count, page_len, latent)[flat_index]]
    all_to_all x2 -> x4, starting transfers between devices: 16.9 us -> 45.5 us  [exchange(): return lax.all_to_all(x, 'batch', split_axis=0, concat_axis=0, tiled=True)]
    all_to_all x1 -> x0, blocking collectives: 20.2 us -> none  [per_device(): lax.all_to_all(wanted, 'batch', split_axis=0, concat_axis=0, tiled=True)]
    another operation x4 -> x0, local copies, waits for them, and re-layouts: 9.22 us -> none
    all_gather x2 -> x0, waiting for transfers between devices: 9.1 us -> none  [the longest x1 9.08 us: per_device(): lax.all_gather(kept_lat, 'head', axis=1, tiled=True)]
  transfers between devices with their start and end apart: 4 -> 4, of which waited for: 3 -> 3; matrix products, arithmetic and copies ran while one was open for 11% -> 4% of each run, Pallas kernels for 0% -> 5%
where the time goes in v1:
time: 300 us; the launch traced here: 297 us
  waiting for transfers between devices  126 us (42%)
  Pallas kernels  94.6 us (32%)
  starting transfers between devices  45.5 us (15%)
  local copies, waits for them, and re-layouts  12.9 us (4%)
  matrix products  10.6 us (4%)
  other arithmetic  6.88 us (2%)
    all_to_all x4, waiting for transfers between devices, exchange(): return lax.all_to_all(x, 'batch', split_axis=0, concat_axis=0, tiled=True)  126 us
    pallas_call x1, Pallas kernels, attend(): pl.pallas_call(lambda *refs: attend_kernel(scale, *refs), out_shape=[jax....  60.4 us
    all_to_all x4, starting transfers between devices, exchange(): return lax.all_to_all(x, 'batch', split_axis=0, concat_axis=0, tiled=True)  45.5 us
    pallas_call x1, Pallas kernels, absorb(): pl.pallas_call(absorb_kernel, out_shape=jax.ShapeDtypeStruct((rows, heads...  18.2 us
    pallas_call x1, Pallas kernels, project(): pl.pallas_call(project_kernel, out_shape=jax.ShapeDtypeStruct((rows, quer...  15.9 us
  transfers between devices with their start and end apart: 4, of which 3 were waited for; matrix products, arithmetic and copies ran while one was open for 4% of the time, Pallas kernels for 5%

profile of v1, /device:TPU:1, one launch (start us, length us, event | category | flops | bytes accessed | tf_op | source)
XLA Modules:
  0.0 296.8 jit_solution(13142411050847987599)
XLA Ops:
  0.0 0.7 reduce.1
  0.7 0.2 convert_reduce_fusion
  1.0 0.1 convert_reduce_fusion.1
  1.1 0.7 reduce.2
  1.9 0.3 select_reduce_fusion
  2.2 0.7 copy.37
  2.9 12.0 %all-to-all-start = ((s32[64,1,16]{2,1,0:T(1,128)}), s32[64,1,16]{2,1,0:T(1,128)S(1)}, u32[]{:S(2)}, u32[]{:S(2)}) async-start(s32[64,1,16]{2,1,0:T(1,128)} %bitcast.1), calls=%async_computation | async-start | bytes 65536 | tf_op jit(solution)/shard_map/all_to_all | solution.py:202
  14.9 0.9 reshape.208
  15.9 0.1 copy.41
  16.1 0.9 copy.63
  17.0 6.2 %all-to-all-done = s32[64,1,16]{2,1,0:T(1,128)S(1)} async-done(((s32[64,1,16]{2,1,0:T(1,128)}), s32[64,1,16]{2,1,0:T(1,128)S(1)}, u32[]{:S(2)}, u32[]{:S(2)}) %all-to-all-start) | async-done | bytes 4128 | tf_op jit(solution)/shard_map/all_to_all | solution.py:202
  23.2 4.2 %broadcast_in_dim.64 = bf16[64,384,128]{2,1,0:T(8,128)(2,1)} broadcast(bf16[384,128]{1,0:T(8,128)(2,1)S(1)} %pad_maximum_fusion), dimensions={1,2} | broadcast | bytes 6389760 | tf_op jit(solution)/shard_map/broadcast_in_dim | solution.py:223
  27.4 5.7 %all-to-all-start.1 = ((bf16[64,384,128]{2,1,0:T(8,128)(2,1)}), bf16[64,384,128]{2,1,0:T(8,128)(2,1)}, u32[]{:S(2)}, u32[]{:S(2)}) async-start(bf16[64,384,128]{2,1,0:T(8,128)(2,1)} %broadcast_in_dim.64), calls=%async_computation.1 | async-start | bytes 12582912 | tf_op jit(solution)/shard_map/all_to_all | solution.py:202
  33.1 0.7 copy.42
  33.8 2.4 copy.43.refs_5_
  36.2 0.1 slice_reduce_fusion.refs_0_
  36.3 75.7 %all-to-all-done.1.q_ref.refs_3_ = bf16[64,384,128]{2,1,0:T(8,128)(2,1)} async-done(((bf16[64,384,128]{2,1,0:T(8,128)(2,1)}), bf16[64,384,128]{2,1,0:T(8,128)(2,1)}, u32[]{:S(2)}, u32[]{:S(2)}) %all-to-all-start.1) | async-done | bytes 6291488 | tf_op jit(solution)/shard_map/all_to_all | solution.py:202
  112.0 18.2 %absorb.1.refs_2_ = bf16[64,256,512]{2,1,0:T(8,128)(2,1)} custom-call(bf16[64,384,128]{2,1,0:T(8,128)(2,1)} %all-to-all-done.1.q_ref.refs_3_, bf16[64,128,512]{2,1,0:T(8,128)(2,1)} %up_ref.2), custom_call_target="tpu_custom_call" | custom-call | tf_op jit(solution)/shard_map/absorb/pallas_call | solution.py:37
  130.3 60.4 %attend.1 = (bf16[64,256,512]{2,1,0:T(8,128)(2,1)}, f32[64,1,256]{2,1,0:T(1,128)}) custom-call(s32[64]{0:T(128)S(1)} %slice_reduce_fusion.refs_0_, s32[64,10]{1,0:T(8,128)S(1)} %slice.9.refs_1_, bf16[64,256,512]{2,1,0:T(8,128)(2,1)} %absorb.1.refs_2_, bf16[64,384,128]{2,1,0:T(8,128)(2,1)} %all-to-all-done.1.q_ref.refs_3_, bf16[96,64,512]{2,1,0:T(8,128)(2,1)} %refs_4_.1, ...), custom_call_target="tpu_custom_call" | custom-call | tf_op jit(solution)/shard_map/attend/pallas_call | solution.py:114
  190.7 17.5 %all-to-all-start.3 = ((f32[64,1,256]{2,1,0:T(1,128)}), f32[64,1,256]{2,1,0:T(1,128)S(1)}, u32[]{:S(2)}, u32[]{:S(2)}) async-start(f32[64,1,256]{2,1,0:T(1,128)} %get-tuple-element.8), calls=%async_computation.3 | async-start | bytes 131072 | tf_op jit(solution)/shard_map/all_to_all | solution.py:202
  208.2 15.9 %project.1 = bf16[64,256,128]{2,1,0:T(8,128)(2,1)S(1)} custom-call(bf16[64,256,512]{2,1,0:T(8,128)(2,1)} %get-tuple-element.7.mixed_ref, bf16[64,512,128]{2,1,0:T(8,128)(2,1)} %up_ref.3), custom_call_target="tpu_custom_call" | custom-call | tf_op jit(solution)/shard_map/project/pallas_call | solution.py:144
  224.2 2.0 copy-done.1
  226.2 10.4 %all-to-all-start.2 = ((bf16[64,256,128]{2,1,0:T(8,128)(2,1)}), bf16[64,256,128]{2,1,0:T(8,128)(2,1)}, u32[]{:S(2)}, u32[]{:S(2)}) async-start(bf16[64,256,128]{2,1,0:T(8,128)(2,1)} %copy-done.1), calls=%async_computation.2 | async-start | bytes 8388608 | tf_op jit(solution)/shard_map/all_to_all | solution.py:202
  236.6 4.6 %convolution_convert_fusion = bf16[64,4,512]{2,1,0:T(4,128)(2,1)S(1)} fusion(bf16[64,128,512]{2,1,0:T(8,128)(2,1)} %up_ref.2, bf16[4,1,8192]{2,0,1:T(4,128)(2,1)S(1)} %copy-done.3), kind=kOutput, calls=%fused_computation.3 | convolution fusion | flops 33685504 | bytes 8716288 | tf_op jit(solution)/shard_map/shn,hnl->hsl/dot_general | solution.py:161
  241.2 0.2 fusion.9
  241.4 0.2 fusion.25
  241.8 0.1 add.49
  241.9 0.3 fusion
  242.4 0.1 reduce_max.22
  243.0 44.1 %all-to-all-done.2 = bf16[64,256,128]{2,1,0:T(8,128)(2,1)} async-done(((bf16[64,256,128]{2,1,0:T(8,128)(2,1)}), bf16[64,256,128]{2,1,0:T(8,128)(2,1)}, u32[]{:S(2)}, u32[]{:S(2)}) %all-to-all-start.2) | async-done | bytes 4194336 | tf_op jit(solution)/shard_map/all_to_all | solution.py:202
  287.1 4.4 %multiply_reduce_fusion = f32[256,128]{1,0:T(8,128)S(1)} fusion(bf16[64,256,128]{2,1,0:T(8,128)(2,1)} %all-to-all-done.2, f32[64,256]{1,0:T(8,128)S(1)} %fusion.13), kind=kLoop, calls=%fused_computation | loop fusion | flops 6258688 | bytes 4390912 | tf_op jit(solution)/shard_map/reduce_sum | solution.py:245
  291.6 5.3 %fusion.3 = bf16[4,1,8192]{2,0,1:T(4,128)(2,1)} fusion(f32[64,4,128]{2,1,0:T(4,128)S(1)} %bitcast.58, bf16[64,512,128]{2,1,0:T(8,128)(2,1)} %up_ref.3, bf16[64,4,512]{2,0,1:T(8,128)(2,1)S(1)} %fusion, f32[64,4]{1,0:T(8,128)S(1)} %copy.49), kind=kOutput, calls=%fused_computation.7 | convolution fusion | flops 33652736 | bytes 8848384 | tf_op jit(solution)/shard_map/hsl,hlv->hsv/dot_general | solution.py:178
  (36 shorter events, 1.3 us)
Async XLA Ops:
  0.0 241.2 %copy-start = (bf16[4,1,512]{2,0,1:T(4,128)(2,1)S(1)}, bf16[4,1,512]{2,0,1:T(4,128)(2,1)}, u32[]{:S(2)}) copy-start(bf16[4,1,512]{2,0,1:T(4,128)(2,1)} %param.16) | copy-start | bytes 12292
  2.9 20.3 %all-to-all-start = ((s32[64,1,16]{2,1,0:T(1,128)}), s32[64,1,16]{2,1,0:T(1,128)S(1)}, u32[]{:S(2)}, u32[]{:S(2)}) async-start(s32[64,1,16]{2,1,0:T(1,128)} %bitcast.1), calls=%async_computation | async-start | bytes 65536 | tf_op jit(solution)/shard_map/all_to_all | solution.py:202
  17.0 16.1 %copy-start.2 = (bf16[96,4096]{1,0:T(8,128)(2,1)S(1)}, bf16[96,4096]{1,0:T(8,128)(2,1)}, u32[]{:S(2)}) copy-start(bf16[96,4096]{1,0:T(8,128)(2,1)} %param.15) | copy-start | bytes 2359300
  27.4 84.6 %all-to-all-start.1 = ((bf16[64,384,128]{2,1,0:T(8,128)(2,1)}), bf16[64,384,128]{2,1,0:T(8,128)(2,1)}, u32[]{:S(2)}, u32[]{:S(2)}) async-start(bf16[64,384,128]{2,1,0:T(8,128)(2,1)} %broadcast_in_dim.64), calls=%async_computation.1 | async-start | bytes 12582912 | tf_op jit(solution)/shard_map/all_to_all | solution.py:202
  190.7 35.5 %all-to-all-start.3 = ((f32[64,1,256]{2,1,0:T(1,128)}), f32[64,1,256]{2,1,0:T(1,128)S(1)}, u32[]{:S(2)}, u32[]{:S(2)}) async-start(f32[64,1,256]{2,1,0:T(1,128)} %get-tuple-element.8), calls=%async_computation.3 | async-start | bytes 131072 | tf_op jit(solution)/shard_map/all_to_all | solution.py:202
  224.2 2.0 copy-start.1
  226.1 10.4 %copy-start.4 = (bf16[1,256]{1,0:T(2,128)(2,1)S(1)}, bf16[1,256]{1,0:T(2,128)(2,1)}, u32[]{:S(2)}) copy-start(bf16[1,256]{1,0:T(2,128)(2,1)} %param.17) | copy-start | bytes 1540
  226.1 10.5 %copy-start.3 = (bf16[4,1,8192]{2,0,1:T(4,128)(2,1)S(1)}, bf16[4,1,8192]{2,0,1:T(4,128)(2,1)}, u32[]{:S(2)}) copy-start(bf16[4,1,8192]{2,0,1:T(4,128)(2,1)} %param.10) | copy-start | bytes 196612
  226.2 61.0 %all-to-all-start.2 = ((bf16[64,256,128]{2,1,0:T(8,128)(2,1)}), bf16[64,256,128]{2,1,0:T(8,128)(2,1)}, u32[]{:S(2)}, u32[]{:S(2)}) async-start(bf16[64,256,128]{2,1,0:T(8,128)(2,1)} %copy-done.1), calls=%async_computation.2 | async-start | bytes 8388608 | tf_op jit(solution)/shard_map/all_to_all | solution.py:202

commit v2 on v1

v2 whole, which is shorter than its diff:
```python
import functools
import math

import jax
import jax.numpy as jnp
from jax import lax
from jax.experimental import pallas as pl
from jax.experimental.pallas import tpu as pltpu
from jax.sharding import PartitionSpec as P

MAX_PAGES = 10
NEG = -1e30
VMEM_BYTES = 62 * 1024 * 1024
PER = 2
PIECES = 4
NT = (((1,), (1,)), ((), ()))


def sixteen(at):
    return pl.ds(pl.multiple_of(at * 16, 16), 16)

def absorb_step(at, packed, up_ref, held):
    rows, _, nope = packed.shape
    latent = up_ref.shape[2]
    q = packed[:, sixteen(at), :].astype(jnp.float32).reshape(rows, 2, 8, nope)
    first = lax.broadcasted_iota(jnp.int32, (rows, 8, nope), 1) < 4
    halves = []
    for pair in range(2):
        part = q[:, pair]
        wide = jnp.concatenate([jnp.where(first, part, 0.0), jnp.where(first, 0.0, part)], axis=2)
        wide = wide.reshape(rows * 8, 2 * nope).astype(jnp.bfloat16)
        weight = up_ref[pl.ds(at * 4 + 2 * pair, 2)].reshape(2 * nope, latent)
        out = jnp.dot(wide, weight, preferred_element_type=jnp.float32)
        halves.append(out.reshape(rows, 8, latent))
    held[:, sixteen(at), :] = jnp.concatenate(halves, axis=1).astype(jnp.bfloat16)

def project_step(at, held, up_ref, packed):
    rows, _, latent = held.shape
    value = up_ref.shape[2]
    mixed = held[:, sixteen(at), :].astype(jnp.float32).reshape(rows, 2, 8, latent)
    first = lax.broadcasted_iota(jnp.int32, (rows, 8, value), 1) < 4
    halves = []
    for pair in range(2):
        part = mixed[:, pair].reshape(rows * 8, latent).astype(jnp.bfloat16)
        at_head = at * 4 + 2 * pair
        weight = jnp.concatenate([up_ref[at_head], up_ref[at_head + 1]], axis=1)
        out = jnp.dot(part, weight, preferred_element_type=jnp.float32)
        out = out.reshape(rows, 8, 2 * value)
        halves.append(jnp.where(first, out[:, :, :value], out[:, :, value:]))
    packed[:, sixteen(at), :] = jnp.concatenate(halves, axis=1).astype(jnp.bfloat16)

def attend_step(scale, at, counts_ref, slots_ref, packed_ref, lat_ref, keyrope_ref, held, keys, rotated, tops, totals):
    queries, latent = held.shape[1:]
    page = lat_ref.shape[1]
    counts = [counts_ref[at * PER + i] for i in range(PER)]
    most = functools.reduce(jnp.maximum, counts)

    def run(pages):
        tokens = pages * page
        lanes = lax.broadcasted_iota(jnp.int32, (queries, 128), 1)
        token = lax.broadcasted_iota(jnp.int32, (1, tokens), 1)
        all_scores = []
        for i in range(PER):
            r = at * PER + i
            for k in range(pages):
                slot = slots_ref[r, k]
                keys[i, k * page : (k + 1) * page, :] = lat_ref[slot]
                rotated[i, k * page : (k + 1) * page, :] = keyrope_ref[slot]
            packed = packed_ref[r, queries : queries + queries // 2, :]
            half = packed.shape[1] // 2
            q_rope = jnp.concatenate([packed[:, :half], packed[:, half:]], axis=0)
            bias = jnp.where(token < counts[i] * page, 0.0, NEG)
            scores = lax.dot_general(held[r], keys[i, 0:tokens, :], NT, preferred_element_type=jnp.float32)
            scores += lax.dot_general(q_rope, rotated[i, 0:tokens, :], NT, preferred_element_type=jnp.float32)
            all_scores.append(scores + bias)
        for i in range(PER):
            r = at * PER + i
            scores = all_scores[i]
            top = jnp.max(scores, axis=1, keepdims=True)
            weights = jnp.exp2((scores - top) * (scale * math.log2(math.e)))
            total = jnp.sum(weights, axis=1, keepdims=True)
            mixed = jnp.dot(weights.astype(jnp.bfloat16), keys[i, 0:tokens, :], preferred_element_type=jnp.float32)
            held[r] = (mixed * (1.0 / total)).astype(jnp.bfloat16)
            tops[...] = jnp.where(lanes == r, top, tops[...])
            totals[...] = jnp.where(lanes == r, total, totals[...])

    pl.when(most <= 4)(lambda: run(4))
    pl.when((most > 4) & (most <= 6))(lambda: run(6))
    pl.when((most > 6) & (most <= 8))(lambda: run(8))
    pl.when(most > 8)(lambda: run(10))

def share_step(scale, tops, totals, packed):
    rows, _, width = packed.shape
    queries = tops.shape[0]
    lse = tops[...] * scale + jnp.log(jnp.maximum(totals[...], 1e-30))
    lse = lse.T[:rows]
    row = lax.broadcasted_iota(jnp.int32, (rows, 8, width), 1)
    out = jnp.zeros((rows, 8, width), jnp.float32)
    left = lse
    per = queries // width
    for level in range(3):
        piece = left.astype(jnp.bfloat16).astype(jnp.float32)
        left = left - piece
        for c in range(per):
            part = piece[:, c * width : (c + 1) * width].reshape(rows, 1, width)
            out = jnp.where(row == level * per + c, part, out)
    packed[:, queries : queries + 16, :] = jnp.concatenate([out, jnp.zeros_like(out)], axis=1).astype(jnp.bfloat16)

def body(scale, counts_ref, slots_ref, packed_hbm, upk_hbm, lat_hbm, keyrope_hbm, upv_hbm, out_hbm,
         packed, upk, lat, keyrope, upv, held, keys, rotated, tops, totals, in_sems, key_sems, value_sems, out_sems):
    heads = upk.shape[0]
    queries = held.shape[1]
    groups = heads // 4
    chunk = heads // PIECES

    def piece(hbm, vmem, sems, k):
        span = pl.ds(k * chunk, chunk)
        return pltpu.make_async_copy(hbm.at[span], vmem.at[span], sems.at[k])

    def out_copy(at):
        return pltpu.make_async_copy(packed.at[:, sixteen(at), :], out_hbm.at[:, sixteen(at), :], out_sems.at[at])

    load_packed = pltpu.make_async_copy(packed_hbm, packed, in_sems.at[0])
    load_lat = pltpu.make_async_copy(lat_hbm, lat, in_sems.at[1])
    load_rope = pltpu.make_async_copy(keyrope_hbm, keyrope, in_sems.at[2])
    load_packed.start()
    for k in range(PIECES):
        piece(upk_hbm, upk, key_sems, k).start()
    load_lat.start()
    load_rope.start()
    for k in range(PIECES):
        piece(upv_hbm, upv, value_sems, k).start()
    tops[...] = jnp.zeros_like(tops)
    totals[...] = jnp.ones_like(totals)
    load_packed.wait()

    def absorb(at, _):
        @pl.when(at % (groups // PIECES) == 0)
        def _():
            piece(upk_hbm, upk, key_sems, at // (groups // PIECES)).wait()
        absorb_step(at, packed, upk, held)
        return 0
    lax.fori_loop(0, groups, absorb, 0)

    load_lat.wait()
    load_rope.wait()

    def attend(at, _):
        attend_step(scale, at, counts_ref, slots_ref, packed, lat, keyrope, held, keys, rotated, tops, totals)
        return 0
    lax.fori_loop(0, held.shape[0] // PER, attend, 0)

    share_step(scale, tops, totals, packed)
    out_copy(groups).start()
    def project(at, _):
        @pl.when(at % (groups // PIECES) == 0)
        def _():
            piece(upv_hbm, upv, value_sems, at // (groups // PIECES)).wait()
        project_step(at, held, upv, packed)
        out_copy(at).start()
        return 0
    lax.fori_loop(0, groups, project, 0)
    def drain(at, _):
        out_copy(at).wait()
        return 0
    lax.fori_loop(0, groups + 1, drain, 0)

def attention(counts, slots, packed, up_key, up_value, pool_latent, pool_rope, scale):
    rows = packed.shape[0]
    heads, nope, latent = up_key.shape
    value = up_value.shape[2]
    queries = heads * 4
    page = pool_latent.shape[1]
    rope = pool_rope.shape[2]
    anywhere = pl.BlockSpec(memory_space=pl.ANY)
    scalars = pl.BlockSpec(memory_space=pltpu.SMEM)
    return pl.pallas_call(
        functools.partial(body, scale),
        out_shape=jax.ShapeDtypeStruct((rows, queries + 16, value), jnp.bfloat16),
        in_specs=[scalars] * 2 + [anywhere] * 5,
        out_specs=anywhere,
        scratch_shapes=[
            pltpu.VMEM(packed.shape, jnp.bfloat16),
            pltpu.VMEM(up_key.shape, jnp.bfloat16),
            pltpu.VMEM(pool_latent.shape, jnp.bfloat16),
            pltpu.VMEM(pool_rope.shape, jnp.bfloat16),
            pltpu.VMEM(up_value.shape, jnp.bfloat16),
            pltpu.VMEM((rows, queries, latent), jnp.bfloat16),
            pltpu.VMEM((PER, MAX_PAGES * page, latent), jnp.bfloat16),
            pltpu.VMEM((PER, MAX_PAGES * page, rope), jnp.bfloat16),
            pltpu.VMEM((queries, 128), jnp.float32),
            pltpu.VMEM((queries, 128), jnp.float32),
            pltpu.SemaphoreType.DMA((3,)),
            pltpu.SemaphoreType.DMA((PIECES,)),
            pltpu.SemaphoreType.DMA((PIECES,)),
            pltpu.SemaphoreType.DMA((heads // 4 + 1,)),
        ],
        compiler_params=pltpu.CompilerParams(vmem_limit_bytes=VMEM_BYTES),
        name="attention",
    )(counts, slots, packed, up_key, pool_latent, pool_rope, up_value)

def fresh_part(q_nope, q_rope, up_key, up_value, new_latent, new_rope, scale):
    steps, heads, _ = q_nope.shape
    latent = up_key.shape[2]
    absorbed = jnp.einsum(
        "shn,hnl->hsl", q_nope, up_key, preferred_element_type=jnp.float32
    ).astype(jnp.bfloat16)
    scores = (
        jnp.einsum("hsl,tl->hst", absorbed, new_latent, preferred_element_type=jnp.float32)
        + jnp.einsum("she,te->hst", q_rope, new_rope, preferred_element_type=jnp.float32)
    ) * scale
    at = jnp.arange(steps, dtype=jnp.int32)
    allowed = at[None, None, :] <= at[None, :, None]
    scores = jnp.where(allowed, scores, NEG)
    top = jnp.max(scores, axis=2, keepdims=True)
    weights = jnp.where(allowed, jnp.exp(scores - top), 0.0)
    total = jnp.sum(weights, axis=2, keepdims=True)
    mixed = jnp.einsum(
        "hst,tl->hsl", weights.astype(jnp.bfloat16), new_latent, preferred_element_type=jnp.float32
    )
    mixed = (mixed / total).astype(jnp.bfloat16)
    out = jnp.einsum("hsl,hlv->hsv", mixed, up_value, preferred_element_type=jnp.float32)
    return out, (top + jnp.log(total))[:, :, 0]


def page_lists(page_shard, page_slot, shards):
    kept = page_shard.shape[0]
    rank = jnp.sum(
        (page_shard[:, None] == page_shard[None, :])
        & (jnp.arange(kept)[None, :] < jnp.arange(kept)[:, None]),
        axis=1,
    )
    here = page_shard[None, :] == jnp.arange(shards, dtype=jnp.int32)[:, None]
    counts = jnp.sum(here, axis=1).astype(jnp.int32)
    at = jnp.arange(MAX_PAGES)[None, :, None]
    slots = jnp.sum(
        jnp.where(here[:, None, :] & (rank[None, None, :] == at), page_slot[None, None, :], 0),
        axis=2,
    ).astype(jnp.int32)
    return jnp.concatenate(
        [counts[:, None], slots, jnp.zeros((shards, 15 - MAX_PAGES), jnp.int32)], axis=1
    )


def exchange(x):
    return lax.all_to_all(x, "batch", split_axis=0, concat_axis=0, tiled=True)


def per_device(
    q_nope, q_rope, up_key, up_value, pool_latent, pool_rope,
    new_latent, new_rope, page_shard, page_slot
):
    shards = lax.axis_size("batch")
    steps = q_nope.shape[0]
    heads, nope, latent = up_key.shape
    value = up_value.shape[2]
    slots_total, page, _ = pool_latent.shape
    rope = pool_rope.shape[1] // page
    scale = 1.0 / math.sqrt(nope + rope)
    q_nope = q_nope.reshape(steps, heads, nope)
    q_rope = q_rope.reshape(steps, heads, rope)

    nope_rows = q_nope.transpose(1, 0, 2).reshape(heads * steps, nope)
    rope_rows = q_rope.transpose(1, 0, 2).reshape(2, heads * steps // 2, rope)
    rope_rows = rope_rows.transpose(1, 0, 2).reshape(heads * steps // 2, 2 * rope)
    own = jnp.concatenate([nope_rows, rope_rows], axis=0)
    packed = lax.all_gather(own, "batch", axis=0, tiled=False)

    lists = exchange(page_lists(page_shard[0, :, 0], page_slot[0], shards))
    fresh_out, fresh_lse = fresh_part(
        q_nope, q_rope, up_key, up_value, new_latent[:, 0], new_rope.reshape(steps, rope), scale
    )
    pool_rope = pool_rope.reshape(slots_total, page, rope)
    packed, lists, fresh_out, fresh_lse, pool_rope = lax.optimization_barrier(
        (packed, lists, fresh_out, fresh_lse, pool_rope)
    )
    parts = exchange(
        attention(
            lists[:, 0], lists[:, 1 : 1 + MAX_PAGES], packed, up_key, up_value,
            pool_latent, pool_rope, scale,
        )
    )
    queries = heads * steps
    extra = queries // value
    lse = parts[:, queries : queries + 3 * extra].astype(jnp.float32)
    lse = jnp.sum(lse.reshape(shards, 3, queries), axis=1)
    parts = parts[:, :queries]

    fresh_lse = fresh_lse.reshape(1, heads * steps)
    top = jnp.maximum(jnp.max(lse, axis=0, keepdims=True), fresh_lse)
    share = jnp.exp(lse - top)
    fresh_share = jnp.exp(fresh_lse - top)
    total = jnp.sum(share, axis=0, keepdims=True) + fresh_share
    share = share / total
    fresh_share = (fresh_share / total).reshape(heads * steps, 1)
    out = jnp.sum(parts.astype(jnp.float32) * share[:, :, None], axis=0)
    out = out + fresh_share * fresh_out.reshape(heads * steps, value)
    out = out.astype(jnp.bfloat16).reshape(heads, steps, value).transpose(1, 0, 2)
    return out.reshape(steps, 1, heads * value)


def solution(mesh):
    placed = (
        P(None, "batch", "head"),
        P(None, "batch", "head"),
        P("head", None, None),
        P("head", None, None),
        P("batch", None, None),
        P("batch", None),
        P(None, "batch", None),
        P("batch", None),
        P("batch", None, None),
        P("batch", None),
    )
    return jax.shard_map(
        per_device, mesh=mesh, in_specs=placed, out_specs=P(None, "batch", "head"), check_vma=False
    )
```

time: 300 us -> 233 us (0.78)
  Pallas kernels: 94.6 us -> 49.3 us
  waiting for transfers between devices: 126 us -> 107 us
  between operations: 0.24 us -> 13.6 us
  starting transfers between devices: 45.5 us -> 33.5 us
  local copies, waits for them, and re-layouts: 12.9 us -> 8.79 us
  other arithmetic: 6.88 us -> 9.97 us
    all_to_all x4 -> x2, waiting for transfers between devices: 126 us -> 57.2 us  [exchange(): return lax.all_to_all(x, 'batch', split_axis=0, concat_axis=0, tiled=True)]
    all_gather x0 -> x1, waiting for transfers between devices: none -> 49.4 us  [per_device(): packed = lax.all_gather(own, 'batch', axis=0, tiled=False)]
    pallas_call x3 -> x1, Pallas kernels: 94.6 us -> 49.3 us  [attention(): pl.pallas_call(functools.partial(body, scale), out_shape=jax.ShapeDtypeSt...]
    all_to_all x4 -> x2, starting transfers between devices: 45.5 us -> 33.5 us  [exchange(): return lax.all_to_all(x, 'batch', split_axis=0, concat_axis=0, tiled=True)]
    broadcast_in_dim x1 -> x0, local copies, waits for them, and re-layouts: 4.18 us -> none  [per_device(): packed = exchange(jnp.broadcast_to(own[None], (shards,) + own.shape))]
    optimization_barrier x0 -> x2, local copies, waits for them, and re-layouts: none -> 3.15 us  [per_device(): lax.optimization_barrier((packed, lists, fresh_out, fresh_lse, pool_rope))]
  transfers between devices with their start and end apart: 4 -> 3, of which waited for: 3 -> 2; matrix products, arithmetic and copies ran while one was open for 4% -> 6% of each run, Pallas kernels for 5% -> 0%
where the time goes in v2:
time: 233 us; the launch traced here: 232 us
  waiting for transfers between devices  107 us (46%)
  Pallas kernels  49.3 us (21%)
  starting transfers between devices  33.5 us (14%)
  between operations  13.6 us (6%)
  matrix products  10.1 us (4%)
  other arithmetic  9.97 us (4%)
  local copies, waits for them, and re-layouts  8.79 us (4%)
    all_to_all x2, waiting for transfers between devices, exchange(): return lax.all_to_all(x, 'batch', split_axis=0, concat_axis=0, tiled=True)  57.2 us
    all_gather x1, waiting for transfers between devices, per_device(): packed = lax.all_gather(own, 'batch', axis=0, tiled=False)  49.4 us
    pallas_call x1, Pallas kernels, attention(): pl.pallas_call(functools.partial(body, scale), out_shape=jax.ShapeDtypeSt...  49.3 us
    all_to_all x2, starting transfers between devices, exchange(): return lax.all_to_all(x, 'batch', split_axis=0, concat_axis=0, tiled=True)  33.5 us
    dot_general x1, matrix products, fresh_part(): jnp.einsum('hsl,hlv->hsv', mixed, up_value, preferred_element_type=jnp.fl...  4.72 us
  transfers between devices with their start and end apart: 3, of which 2 were waited for; matrix products, arithmetic and copies ran while one was open for 6% of the time, Pallas kernels for 0%

profile of v2, /device:TPU:1, one launch (start us, length us, event | category | flops | bytes accessed | tf_op | source)
XLA Modules:
  0.0 231.8 jit_solution(18182417094255247503)
XLA Ops:
  6.5 0.9 reshape.192
  7.6 0.1 copy.40
  7.7 0.9 copy.57
  8.6 0.6 pad_maximum_fusion
  9.3 0.7 reduce
  10.0 0.7 reduce.1
  10.8 0.1 convert_reduce_fusion.1
  10.9 0.2 convert_reduce_fusion
  11.2 0.3 select_reduce_fusion
  11.5 0.7 copy.41
  12.2 12.0 %all-to-all-start = ((s32[64,1,16]{2,1,0:T(1,128)}), s32[64,1,16]{2,1,0:T(1,128)S(1)}, u32[]{:S(2)}, u32[]{:S(2)}) async-start(s32[64,1,16]{2,1,0:T(1,128)} %bitcast.8), calls=%async_computation | async-start | bytes 65536 | tf_op jit(solution)/shard_map/all_to_all | solution.py:246
  24.2 0.7 reduce.2
  25.0 4.6 %convolution_convert_fusion = bf16[64,4,512]{2,1,0:T(4,128)(2,1)S(1)} fusion(bf16[64,128,512]{2,1,0:T(8,128)(2,1)} %upk_hbm.1, bf16[4,1,8192]{2,0,1:T(4,128)(2,1)} %param.10), kind=kOutput, calls=%fused_computation.3 | convolution fusion | flops 33685504 | bytes 8716288 | tf_op jit(solution)/shard_map/shn,hnl->hsl/dot_general | solution.py:205
  29.6 0.2 fusion.7
  29.8 0.2 fusion.23
  30.1 0.3 fusion
  30.5 4.7 %fusion.5 = f32[64,4,128]{2,1,0:T(4,128)S(1)} fusion(bf16[64,512,128]{2,1,0:T(8,128)(2,1)} %upv_hbm.1, bf16[64,4,512]{2,0,1:T(8,128)(2,1)S(1)} %fusion), kind=kOutput, calls=%fused_computation.12 | convolution fusion | flops 33554432 | bytes 8781824 | tf_op jit(solution)/shard_map/hsl,hlv->hsv/dot_general | solution.py:222
  35.2 0.7 copy.45
  35.9 49.4 %all-gather.3.cloned.1.call-done = bf16[24576,128]{1,0:T(8,128)(2,1)} async-done(((bf16[384,128]{1,0:T(8,128)(2,1)}), bf16[24576,128]{1,0:T(8,128)(2,1)}) %all-gather.3.cloned.1.call-update) | async-done | bytes 6291472 | tf_op jit(solution)/shard_map/all_gather | solution.py:267
  85.2 0.7 slice.13.slots_ref
  85.9 0.7 slice_reduce_fusion.counts_ref
  86.6 3.1 %copy.46.keyrope_hbm = bf16[96,64,64]{2,1,0:T(8,128)(2,1)} copy(bf16[96,64,64]{0,2,1:T(8,128)(2,1)S(1)} %bitcast.50) | data formatting | bytes 1572864 | tf_op jit(solution)/shard_map/optimization_barrier | solution.py:274
  89.7 49.3 %attention.1 = bf16[64,272,128]{2,1,0:T(8,128)(2,1)} custom-call(s32[64]{0:T(128)} %slice_reduce_fusion.counts_ref, s32[64,10]{1,0:T(8,128)} %slice.13.slots_ref, bf16[64,384,128]{2,1,0:T(8,128)(2,1)} %bitcast.49, bf16[64,128,512]{2,1,0:T(8,128)(2,1)} %upk_hbm.1, bf16[96,64,512]{2,1,0:T(8,128)(2,1)} %lat_hbm.1, bf16[96,64,64]{2,1,0:T(8,128)(2,1)} %copy.46.keyrope_hbm, ...), custom_call_target="tpu_custom_call" | custom-call | tf_op jit(solution)/shard_map/attention/pallas_call | solution.py:177
  139.0 21.5 %all-to-all-start.1 = ((bf16[64,272,128]{2,1,0:T(8,128)(2,1)}), bf16[64,272,128]{2,1,0:T(8,128)(2,1)}, u32[]{:S(2)}, u32[]{:S(2)}) async-start(bf16[64,272,128]{2,1,0:T(8,128)(2,1)} %attention.1), calls=%async_computation.1 | async-start | bytes 8912896 | tf_op jit(solution)/shard_map/all_to_all | solution.py:246
  160.7 0.1 reshape.199
  160.8 57.2 %all-to-all-done.1 = bf16[64,272,128]{2,1,0:T(8,128)(2,1)} async-done(((bf16[64,272,128]{2,1,0:T(8,128)(2,1)}), bf16[64,272,128]{2,1,0:T(8,128)(2,1)}, u32[]{:S(2)}, u32[]{:S(2)}) %all-to-all-start.1) | async-done | bytes 4456480 | tf_op jit(solution)/shard_map/all_to_all | solution.py:246
  217.9 0.9 slice_convert_fusion
  218.9 0.1 reshape.202
  219.0 0.2 reduce_sum.71
  219.3 0.1 reduce_sum.75
  219.8 4.4 %multiply_reduce_fusion = f32[256,128]{1,0:T(8,128)S(1)} fusion(bf16[64,272,128]{2,1,0:T(8,128)(2,1)} %all-to-all-done.1, f32[64,256]{1,0:T(8,128)S(1)} %fusion.11), kind=kLoop, calls=%fused_computation | loop fusion | flops 6258688 | bytes 4390912 | tf_op jit(solution)/shard_map/reduce_sum | solution.py:296
  224.2 0.8 fusion.9
  (30 shorter events, 1.2 us)
Async XLA Ops:
  6.5 23.1 %copy-start = (bf16[4,1,512]{2,0,1:T(4,128)(2,1)S(1)}, bf16[4,1,512]{2,0,1:T(4,128)(2,1)}, u32[]{:S(2)}) copy-start(bf16[4,1,512]{2,0,1:T(4,128)(2,1)} %param.16) | copy-start | bytes 12292
  6.5 78.7 %all-gather.3.cloned.1.call-start = ((), (), s32[]{:S(2)}) async-start(), calls=%async_computation.2 | async-start | bytes 6389760 | tf_op jit(solution)/shard_map/all_gather | solution.py:267
  12.2 23.6 %all-to-all-start = ((s32[64,1,16]{2,1,0:T(1,128)}), s32[64,1,16]{2,1,0:T(1,128)S(1)}, u32[]{:S(2)}, u32[]{:S(2)}) async-start(s32[64,1,16]{2,1,0:T(1,128)} %bitcast.8), calls=%async_computation | async-start | bytes 65536 | tf_op jit(solution)/shard_map/all_to_all | solution.py:246
  30.4 4.7 %copy-start.1 = (bf16[96,4096]{1,0:T(8,128)(2,1)S(1)}, bf16[96,4096]{1,0:T(8,128)(2,1)}, u32[]{:S(2)}) copy-start(bf16[96,4096]{1,0:T(8,128)(2,1)} %param.15) | copy-start | bytes 2359300
  139.0 78.9 %all-to-all-start.1 = ((bf16[64,272,128]{2,1,0:T(8,128)(2,1)}), bf16[64,272,128]{2,1,0:T(8,128)(2,1)}, u32[]{:S(2)}, u32[]{:S(2)}) async-start(bf16[64,272,128]{2,1,0:T(8,128)(2,1)} %attention.1), calls=%async_computation.1 | async-start | bytes 8912896 | tf_op jit(solution)/shard_map/all_to_all | solution.py:246
Sparse Core Ops, SparseCore 0:
  10.1 75.0 all-gather.2

commit v3 on v2

--- a/solution.py
+++ b/solution.py
@@ -49,10 +49,11 @@
         halves.append(jnp.where(first, out[:, :, :value], out[:, :, value:]))
     packed[:, sixteen(at), :] = jnp.concatenate(halves, axis=1).astype(jnp.bfloat16)
 
-def attend_step(scale, at, counts_ref, slots_ref, packed_ref, lat_ref, keyrope_ref, held, keys, rotated, tops, totals):
+def attend_step(scale, at, counts_ref, slots_ref, order_ref, packed_ref, lat_ref, keyrope_ref, held, keys, rotated, tops, totals):
     queries, latent = held.shape[1:]
     page = lat_ref.shape[1]
-    counts = [counts_ref[at * PER + i] for i in range(PER)]
+    owners = [order_ref[at * PER + i] for i in range(PER)]
+    counts = [counts_ref[owners[i]] for i in range(PER)]
     most = functools.reduce(jnp.maximum, counts)
 
     def run(pages):
@@ -63,7 +64,7 @@
         for i in range(PER):
             r = at * PER + i
             for k in range(pages):
-                slot = slots_ref[r, k]
+                slot = slots_ref[owners[i], k]
                 keys[i, k * page : (k + 1) * page, :] = lat_ref[slot]
                 rotated[i, k * page : (k + 1) * page, :] = keyrope_ref[slot]
             packed = packed_ref[r, queries : queries + queries // 2, :]
@@ -106,24 +107,39 @@
             out = jnp.where(row == level * per + c, part, out)
     packed[:, queries : queries + 16, :] = jnp.concatenate([out, jnp.zeros_like(out)], axis=1).astype(jnp.bfloat16)
 
-def body(scale, counts_ref, slots_ref, packed_hbm, upk_hbm, lat_hbm, keyrope_hbm, upv_hbm, out_hbm,
-         packed, upk, lat, keyrope, upv, held, keys, rotated, tops, totals, in_sems, key_sems, value_sems, out_sems):
+def body(scale, members, counts_ref, slots_ref, order_ref, *refs):
+    packed_hbm, refs = refs[:members], refs[members:]
+    upk_hbm, lat_hbm, keyrope_hbm, upv_hbm, refs = refs[:4] + (refs[4:],)
+    out_hbm, refs = refs[:members], refs[members:]
+    packed, upk, lat, keyrope, upv, held, keys, rotated, tops, totals = refs[:10]
+    packed_sems, in_sems, key_sems, value_sems, out_sems = refs[10:]
     heads = upk.shape[0]
     queries = held.shape[1]
     groups = heads // 4
     chunk = heads // PIECES
+    each = packed.shape[0] // members
+    span = queries // PIECES
 
     def piece(hbm, vmem, sems, k):
-        span = pl.ds(k * chunk, chunk)
-        return pltpu.make_async_copy(hbm.at[span], vmem.at[span], sems.at[k])
-
-    def out_copy(at):
-        return pltpu.make_async_copy(packed.at[:, sixteen(at), :], out_hbm.at[:, sixteen(at), :], out_sems.at[at])
-
-    load_packed = pltpu.make_async_copy(packed_hbm, packed, in_sems.at[0])
-    load_lat = pltpu.make_async_copy(lat_hbm, lat, in_sems.at[1])
-    load_rope = pltpu.make_async_copy(keyrope_hbm, keyrope, in_sems.at[2])
-    load_packed.start()
+        at = pl.ds(k * chunk, chunk)
+        return pltpu.make_async_copy(hbm.at[at], vmem.at[at], sems.at[k])
+
+    def packed_copy(m):
+        return pltpu.make_async_copy(packed_hbm[m], packed.at[pl.ds(m * each, each)], packed_sems.at[m])
+
+    def out_copy(k, m):
+        if k < PIECES:
+            at = pl.ds(k * span, span)
+        else:
+            at = pl.ds(queries, 16)
+        return pltpu.make_async_copy(
+            packed.at[pl.ds(m * each, each), at, :], out_hbm[m].at[:, at, :], out_sems.at[k, m]
+        )
+
+    load_lat = pltpu.make_async_copy(lat_hbm, lat, in_sems.at[0])
+    load_rope = pltpu.make_async_copy(keyrope_hbm, keyrope, in_sems.at[1])
+    for m in range(members):
+        packed_copy(m).start()
     for k in range(PIECES):
         piece(upk_hbm, upk, key_sems, k).start()
     load_lat.start()
@@ -132,42 +148,49 @@
         piece(upv_hbm, upv, value_sems, k).start()
     tops[...] = jnp.zeros_like(tops)
     totals[...] = jnp.ones_like(totals)
-    load_packed.wait()
+    for m in range(members):
+        packed_copy(m).wait()
 
     def absorb(at, _):
-        @pl.when(at % (groups // PIECES) == 0)
-        def _():
-            piece(upk_hbm, upk, key_sems, at // (groups // PIECES)).wait()
         absorb_step(at, packed, upk, held)
         return 0
-    lax.fori_loop(0, groups, absorb, 0)
+    for k in range(PIECES):
+        piece(upk_hbm, upk, key_sems, k).wait()
+        lax.fori_loop(k * groups // PIECES, (k + 1) * groups // PIECES, absorb, 0)
 
     load_lat.wait()
     load_rope.wait()
 
     def attend(at, _):
-        attend_step(scale, at, counts_ref, slots_ref, packed, lat, keyrope, held, keys, rotated, tops, totals)
+        attend_step(
+            scale, at, counts_ref, slots_ref, order_ref, packed, lat, keyrope, held, keys, rotated,
+            tops, totals
+        )
         return 0
     lax.fori_loop(0, held.shape[0] // PER, attend, 0)
 
     share_step(scale, tops, totals, packed)
-    out_copy(groups).start()
+    for m in range(members):
+        out_copy(PIECES, m).start()
+
     def project(at, _):
-        @pl.when(at % (groups // PIECES) == 0)
-        def _():
-            piece(upv_hbm, upv, value_sems, at // (groups // PIECES)).wait()
         project_step(at, held, upv, packed)
-        out_copy(at).start()
         return 0
-    lax.fori_loop(0, groups, project, 0)
-    def drain(at, _):
-        out_copy(at).wait()
-        return 0
-    lax.fori_loop(0, groups + 1, drain, 0)
-
-def attention(counts, slots, packed, up_key, up_value, pool_latent, pool_rope, scale):
-    rows = packed.shape[0]
-    heads, nope, latent = up_key.shape
+    for k in range(PIECES):
+        piece(upv_hbm, upv, value_sems, k).wait()
+        lax.fori_loop(k * groups // PIECES, (k + 1) * groups // PIECES, project, 0)
+        for m in range(members):
+            out_copy(k, m).start()
+    for k in range(PIECES + 1):
+        for m in range(members):
+            out_copy(k, m).wait()
+
+
+def attention(lists, order, packed, up_key, up_value, pool_latent, pool_rope, scale):
+    members = len(packed)
+    each, length, _ = packed[0].shape
+    rows = members * each
+    heads, _, latent = up_key.shape
     value = up_value.shape[2]
     queries = heads * 4
     page = pool_latent.shape[1]
@@ -175,12 +198,12 @@
     anywhere = pl.BlockSpec(memory_space=pl.ANY)
     scalars = pl.BlockSpec(memory_space=pltpu.SMEM)
     return pl.pallas_call(
-        functools.partial(body, scale),
-        out_shape=jax.ShapeDtypeStruct((rows, queries + 16, value), jnp.bfloat16),
-        in_specs=[scalars] * 2 + [anywhere] * 5,
-        out_specs=anywhere,
+        functools.partial(body, scale, members),
+        out_shape=[jax.ShapeDtypeStruct((each, queries + 16, value), jnp.bfloat16)] * members,
+        in_specs=[scalars] * 3 + [anywhere] * (members + 4),
+        out_specs=[anywhere] * members,
         scratch_shapes=[
-            pltpu.VMEM(packed.shape, jnp.bfloat16),
+            pltpu.VMEM((rows, length, value), jnp.bfloat16),
             pltpu.VMEM(up_key.shape, jnp.bfloat16),
             pltpu.VMEM(pool_latent.shape, jnp.bfloat16),
             pltpu.VMEM(pool_rope.shape, jnp.bfloat16),
@@ -190,14 +213,16 @@
             pltpu.VMEM((PER, MAX_PAGES * page, rope), jnp.bfloat16),
             pltpu.VMEM((queries, 128), jnp.float32),
             pltpu.VMEM((queries, 128), jnp.float32),
-            pltpu.SemaphoreType.DMA((3,)),
+            pltpu.SemaphoreType.DMA((members,)),
+            pltpu.SemaphoreType.DMA((2,)),
             pltpu.SemaphoreType.DMA((PIECES,)),
             pltpu.SemaphoreType.DMA((PIECES,)),
-            pltpu.SemaphoreType.DMA((heads // 4 + 1,)),
+            pltpu.SemaphoreType.DMA((PIECES + 1, members)),
         ],
         compiler_params=pltpu.CompilerParams(vmem_limit_bytes=VMEM_BYTES),
         name="attention",
-    )(counts, slots, packed, up_key, pool_latent, pool_rope, up_value)
+    )(lists[0], lists[1], order, *packed, up_key, pool_latent, pool_rope, up_value)
+
 
 def fresh_part(q_nope, q_rope, up_key, up_value, new_latent, new_rope, scale):
     steps, heads, _ = q_nope.shape
@@ -246,6 +271,84 @@
     return lax.all_to_all(x, "batch", split_axis=0, concat_axis=0, tiled=True)
 
 
+SIDE = 4
+CORNERS = [(a, b, c) for a in range(2) for b in range(2) for c in range(2)]
+
+
+def place(index):
+    return (index // (SIDE * SIDE), index // SIDE % SIDE, index % SIDE)
+
+
+def index_of(at):
+    return (at[0] * SIDE + at[1]) * SIDE + at[2]
+
+
+def flipped(v, core):
+    return (v + 1 - 2 * ((v - core) % 2)) % SIDE
+
+
+def across(at, core, corner):
+    return tuple(flipped(v, core) if f else v for v, f in zip(at, corner))
+
+
+def strided(at, corner):
+    return tuple((v + 2 * f) % SIDE for v, f in zip(at, corner))
+
+
+def block_pairs(corner, cores):
+    pairs = []
+    for i in range(SIDE**3):
+        for core in range(cores):
+            j = index_of(across(place(i), core, corner))
+            pairs.append((i * cores + core, j * cores + core))
+    return pairs
+
+
+def stride_pairs(corner):
+    return [(i, index_of(strided(place(i), corner))) for i in range(SIDE**3)]
+
+
+def to_block(x, corner):
+    return lax.ppermute(x, ("batch", "head"), block_pairs(corner, lax.axis_size("head")))
+
+
+def to_stride(x, corner):
+    return lax.ppermute(x, "batch", stride_pairs(corner))
+
+
+def row_order():
+    at, core = place(lax.axis_index("batch")), lax.axis_index("head")
+    order = [index_of(strided(across(at, core, m), e)) for m in CORNERS for e in CORNERS]
+    return jnp.stack(order).astype(jnp.int32)
+
+
+def unpack(part, queries):
+    extra = queries // part.shape[2]
+    lse = part[:, queries : queries + 3 * extra].astype(jnp.float32)
+    lse = jnp.sum(lse.reshape(part.shape[0], 3, queries), axis=1)
+    return part[:, :queries].astype(jnp.float32), lse
+
+
+def mix(outs, lses):
+    top = functools.reduce(jnp.maximum, lses)
+    shares = [jnp.exp(lse - top) for lse in lses]
+    total = sum(shares)
+    out = sum(out * (share / total)[:, :, None] for out, share in zip(outs, shares))
+    return out, top + jnp.log(total)
+
+
+def pack(out, lse):
+    rows, queries, value = out.shape
+    pieces, left = [], lse
+    for _ in range(3):
+        piece = lax.reduce_precision(left, 8, 7)
+        left = left - piece
+        pieces.append(piece.reshape(rows, queries // value, value))
+    extra = 16 - 3 * queries // value
+    pieces.append(jnp.zeros((rows, extra, value), jnp.float32))
+    return jnp.concatenate([out] + pieces, axis=1).astype(jnp.bfloat16)
+
+
 def per_device(
     q_nope, q_rope, up_key, up_value, pool_latent, pool_rope,
     new_latent, new_rope, page_shard, page_slot
@@ -264,37 +367,31 @@
     rope_rows = q_rope.transpose(1, 0, 2).reshape(2, heads * steps // 2, rope)
     rope_rows = rope_rows.transpose(1, 0, 2).reshape(heads * steps // 2, 2 * rope)
     own = jnp.concatenate([nope_rows, rope_rows], axis=0)
-    packed = lax.all_gather(own, "batch", axis=0, tiled=False)
+    near = jnp.stack([own] + [to_stride(own, e) for e in CORNERS[1:]])
+    packed = [near] + [to_block(near, m) for m in CORNERS[1:]]
 
     lists = exchange(page_lists(page_shard[0, :, 0], page_slot[0], shards))
     fresh_out, fresh_lse = fresh_part(
         q_nope, q_rope, up_key, up_value, new_latent[:, 0], new_rope.reshape(steps, rope), scale
     )
     pool_rope = pool_rope.reshape(slots_total, page, rope)
-    packed, lists, fresh_out, fresh_lse, pool_rope = lax.optimization_barrier(
-        (packed, lists, fresh_out, fresh_lse, pool_rope)
-    )
-    parts = exchange(
-        attention(
-            lists[:, 0], lists[:, 1 : 1 + MAX_PAGES], packed, up_key, up_value,
-            pool_latent, pool_rope, scale,
-        )
-    )
+    counts, slots = lists[:, 0], lists[:, 1 : 1 + MAX_PAGES]
+    packed, counts, slots, fresh_out, fresh_lse, pool_rope = lax.optimization_barrier(
+        (packed, counts, slots, fresh_out, fresh_lse, pool_rope)
+    )
+    parts = attention(
+        (counts, slots), row_order(), packed, up_key, up_value, pool_latent, pool_rope, scale
+    )
+
     queries = heads * steps
-    extra = queries // value
-    lse = parts[:, queries : queries + 3 * extra].astype(jnp.float32)
-    lse = jnp.sum(lse.reshape(shards, 3, queries), axis=1)
-    parts = parts[:, :queries]
-
-    fresh_lse = fresh_lse.reshape(1, heads * steps)
-    top = jnp.maximum(jnp.max(lse, axis=0, keepdims=True), fresh_lse)
-    share = jnp.exp(lse - top)
-    fresh_share = jnp.exp(fresh_lse - top)
-    total = jnp.sum(share, axis=0, keepdims=True) + fresh_share
-    share = share / total
-    fresh_share = (fresh_share / total).reshape(heads * steps, 1)
-    out = jnp.sum(parts.astype(jnp.float32) * share[:, :, None], axis=0)
-    out = out + fresh_share * fresh_out.reshape(heads * steps, value)
+    parts = [parts[0]] + [to_block(part, m) for part, m in zip(parts[1:], CORNERS[1:])]
+    outs, lses = zip(*(unpack(part, queries) for part in parts))
+    mixed = pack(*mix(outs, lses))
+    rows = [mixed[:1]] + [to_stride(mixed[k : k + 1], CORNERS[k]) for k in range(1, len(CORNERS))]
+    outs, lses = zip(*(unpack(row, queries) for row in rows))
+    outs += (fresh_out.reshape(1, queries, value),)
+    lses += (fresh_lse.reshape(1, queries),)
+    out, _ = mix(outs, lses)
     out = out.astype(jnp.bfloat16).reshape(heads, steps, value).transpose(1, 0, 2)
     return out.reshape(steps, 1, heads * value)
 

time: 233 us -> 245 us (1.052)
  the two profiles are of different devices: /device:TPU:1 before, /device:TPU:0 now
where the time goes in v3:
time: 245 us; the launch traced here: 244 us
  starting transfers between devices  88.7 us (36%)
  waiting for transfers between devices  73 us (30%)
  Pallas kernels  50.3 us (21%)
  other arithmetic  12.6 us (5%)
  matrix products  9.98 us (4%)
  local copies, waits for them, and re-layouts  8.94 us (4%)
    ppermute x14, waiting for transfers between devices, to_block(): lax.ppermute(x, ('batch', 'head'), block_pairs(corner, lax.axis_size('hea...  57.8 us
    ppermute x14, starting transfers between devices, to_stride(): return lax.ppermute(x, 'batch', stride_pairs(corner))  52 us
    pallas_call x1, Pallas kernels, attention(): pl.pallas_call(functools.partial(body, scale, members), out_shape=[jax.Sh...  50.3 us
    ppermute x14, starting transfers between devices, to_block(): lax.ppermute(x, ('batch', 'head'), block_pairs(corner, lax.axis_size('hea...  27.5 us
    ppermute x14, waiting for transfers between devices, to_stride(): return lax.ppermute(x, 'batch', stride_pairs(corner))  15.2 us
    all_to_all x1, starting transfers between devices, exchange(): return lax.all_to_all(x, 'batch', split_axis=0, concat_axis=0, tiled=True)  9.18 us
  transfers between devices with their start and end apart: 29, of which 9 were waited for; matrix products, arithmetic and copies ran while one was open for 8% of the time, Pallas kernels for 0%

profile of v3, /device:TPU:0, one launch (start us, length us, event | category | flops | bytes accessed | tf_op | source)
XLA Modules:
  0.0 244.4 jit_solution(10460816405891333170)
XLA Ops:
  2.0 3.1 %collective-permute-start = (bf16[384,128]{1,0:T(8,128)(2,1)S(1)}, bf16[384,128]{1,0:T(8,128)(2,1)S(1)}, u32[]{:S(2)}, u32[]{:S(2)}) collective-permute-start(bf16[384,128]{1,0:T(8,128)(2,1)S(1)} %pad_maximum_fusion), channel_id=1, source_target_pairs={{0,4},{2,6},{4,0},{6,2},{8,12},{10,14},{12,8},{14,10},{16,20},{18,... | collective-permute-start | bytes 294920 | tf_op jit(solution)/shard_map/ppermute | solution.py:316
  5.1 3.2 %collective-permute-start.1 = (bf16[384,128]{1,0:T(8,128)(2,1)S(1)}, bf16[384,128]{1,0:T(8,128)(2,1)S(1)}, u32[]{:S(2)}, u32[]{:S(2)}) collective-permute-start(bf16[384,128]{1,0:T(8,128)(2,1)S(1)} %pad_maximum_fusion), channel_id=1, source_target_pairs={{0,16},{2,18},{4,20},{6,22},{8,24},{10,26},{12,28},{14,30},{16,0},... | collective-permute-start | bytes 294920 | tf_op jit(solution)/shard_map/ppermute | solution.py:316
  8.5 4.0 %collective-permute-start.3 = (bf16[384,128]{1,0:T(8,128)(2,1)S(1)}, bf16[384,128]{1,0:T(8,128)(2,1)S(1)}, u32[]{:S(2)}, u32[]{:S(2)}) collective-permute-start(bf16[384,128]{1,0:T(8,128)(2,1)S(1)} %pad_maximum_fusion), channel_id=1, source_target_pairs={{0,64},{2,66},{4,68},{6,70},{8,72},{10,74},{12,76},{14,78},{16,80}... | collective-permute-start | bytes 294920 | tf_op jit(solution)/shard_map/ppermute | solution.py:316
  12.5 2.5 %collective-permute-start.4 = (bf16[384,128]{1,0:T(8,128)(2,1)S(1)}, bf16[384,128]{1,0:T(8,128)(2,1)S(1)}, u32[]{:S(2)}, u32[]{:S(2)}) collective-permute-start(bf16[384,128]{1,0:T(8,128)(2,1)S(1)} %pad_maximum_fusion), channel_id=1, source_target_pairs={{0,68},{2,70},{4,64},{6,66},{8,76},{10,78},{12,72},{14,74},{16,84}... | collective-permute-start | bytes 294920 | tf_op jit(solution)/shard_map/ppermute | solution.py:316
  17.9 9.2 %all-to-all-start = ((s32[64,1,16]{2,1,0:T(1,128)}), s32[64,1,16]{2,1,0:T(1,128)S(1)}, u32[]{:S(2)}, u32[]{:S(2)}) async-start(s32[64,1,16]{2,1,0:T(1,128)} %bitcast.16), calls=%async_computation | async-start | bytes 65536 | tf_op jit(solution)/shard_map/all_to_all | solution.py:271
  28.3 4.6 %convolution_convert_fusion = bf16[64,4,512]{2,1,0:T(4,128)(2,1)S(1)} fusion(bf16[64,128,512]{2,1,0:T(8,128)(2,1)} %refs_8_.1, bf16[4,1,8192]{2,0,1:T(4,128)(2,1)} %param.10), kind=kOutput, calls=%fused_computation.2 | convolution fusion | flops 33685504 | bytes 8716288 | tf_op jit(solution)/shard_map/shn,hnl->hsl/dot_general | solution.py:230
  33.0 5.7 %collective-permute-start.5 = (bf16[384,128]{1,0:T(8,128)(2,1)S(1)}, bf16[384,128]{1,0:T(8,128)(2,1)S(1)}, u32[]{:S(2)}, u32[]{:S(2)}) collective-permute-start(bf16[384,128]{1,0:T(8,128)(2,1)S(1)} %pad_maximum_fusion), channel_id=1, source_target_pairs={{0,80},{2,82},{4,84},{6,86},{8,88},{10,90},{12,92},{14,94},{16,64}... | collective-permute-start | bytes 294920 | tf_op jit(solution)/shard_map/ppermute | solution.py:316
  38.7 2.9 %collective-permute-start.6 = (bf16[384,128]{1,0:T(8,128)(2,1)S(1)}, bf16[384,128]{1,0:T(8,128)(2,1)S(1)}, u32[]{:S(2)}, u32[]{:S(2)}) collective-permute-start(bf16[384,128]{1,0:T(8,128)(2,1)S(1)} %pad_maximum_fusion), channel_id=1, source_target_pairs={{0,84},{2,86},{4,80},{6,82},{8,92},{10,94},{12,88},{14,90},{16,68}... | collective-permute-start | bytes 294920 | tf_op jit(solution)/shard_map/ppermute | solution.py:316
  41.8 8.0 %collective-permute-done.6 = bf16[384,128]{1,0:T(8,128)(2,1)S(1)} collective-permute-done((bf16[384,128]{1,0:T(8,128)(2,1)S(1)}, bf16[384,128]{1,0:T(8,128)(2,1)S(1)}, u32[]{:S(2)}, u32[]{:S(2)}) %collective-permute-start.6) | collective-permute-done | bytes 98336 | tf_op jit(solution)/shard_map/ppermute | solution.py:316
  50.6 2.2 collective-permute-start.11
  58.1 29.0 %collective-permute-done.10.refs_4_ = bf16[8,384,128]{2,1,0:T(8,128)(2,1)S(1)} collective-permute-done((bf16[8,384,128]{2,1,0:T(8,128)(2,1)S(1)}, bf16[8,384,128]{2,1,0:T(8,128)(2,1)S(1)}, u32[]{:S(2)}, u32[]{:S(2)}) %collective-permute-start.10) | collective-permute-done | bytes 786464 | tf_op jit(solution)/shard_map/ppermute | solution.py:312
  87.7 2.3 collective-permute-start.9
  90.1 4.6 %fusion.5 = f32[64,4,128]{2,1,0:T(4,128)S(1)} fusion(bf16[64,512,128]{2,1,0:T(8,128)(2,1)} %refs_11_.1, bf16[64,4,512]{2,0,1:T(8,128)(2,1)S(1)} %fusion), kind=kOutput, calls=%fused_computation.12 | convolution fusion | flops 33554432 | bytes 8781824 | tf_op jit(solution)/shard_map/hsl,hlv->hsv/dot_general | solution.py:247
  97.5 10.1 %collective-permute-done.8.refs_2_ = bf16[8,384,128]{2,1,0:T(8,128)(2,1)} collective-permute-done((bf16[8,384,128]{2,1,0:T(8,128)(2,1)S(1)}, bf16[8,384,128]{2,1,0:T(8,128)(2,1)}, u32[]{:S(2)}, u32[]{:S(2)}) %collective-permute-start.8) | collective-permute-done | bytes 786464 | tf_op jit(solution)/shard_map/ppermute | solution.py:312
  107.7 3.1 %copy.57.refs_10_ = bf16[96,64,64]{2,1,0:T(8,128)(2,1)} copy(bf16[96,64,64]{0,2,1:T(8,128)(2,1)S(1)} %bitcast.130) | data formatting | bytes 1572864 | tf_op jit(solution)/shard_map/optimization_barrier | solution.py:379
  110.7 50.3 %attention.1 = (bf16[8,272,128]{2,1,0:T(8,128)(2,1)}, bf16[8,272,128]{2,1,0:T(8,128)(2,1)}, bf16[8,272,128]{2,1,0:T(8,128)(2,1)}, bf16[8,272,128]{2,1,0:T(8,128)...) custom-call(s32[64]{0:T(128)} %slice_reduce_fusion.counts_ref, ...), custom_call_target="tpu_custom_call" | custom-call | tf_op jit(solution)/shard_map/attention/pallas_call | solution.py:200
  162.6 4.2 %collective-permute-start.15 = (bf16[8,272,128]{2,1,0:T(8,128)(2,1)}, bf16[8,272,128]{2,1,0:T(8,128)(2,1)S(1)}, u32[]{:S(2)}, u32[]{:S(2)}) collective-permute-start(bf16[8,272,128]{2,1,0:T(8,128)(2,1)} %get-tuple-element.39), channel_id=1, source_target_pairs={{0,8},{1,25},{2,10},{3,27},{4,12},{5,29},{6,14},{7,31},{8,0},{9,17... | collective-permute-start | bytes 1671176 | tf_op jit(solution)/shard_map/ppermute | solution.py:312
  166.8 2.4 collective-permute-start.17
  170.9 5.2 %collective-permute-start.19 = (bf16[8,272,128]{2,1,0:T(8,128)(2,1)}, bf16[8,272,128]{2,1,0:T(8,128)(2,1)}, u32[]{:S(2)}, u32[]{:S(2)}) collective-permute-start(bf16[8,272,128]{2,1,0:T(8,128)(2,1)} %get-tuple-element.43), channel_id=1, source_target_pairs={{0,40},{1,121},{2,42},{3,123},{4,44},{5,125},{6,46},{7,127},{8,32}... | collective-permute-start | bytes 1671176 | tf_op jit(solution)/shard_map/ppermute | solution.py:312
  176.1 4.4 %collective-permute-done.15 = bf16[8,272,128]{2,1,0:T(8,128)(2,1)S(1)} collective-permute-done((bf16[8,272,128]{2,1,0:T(8,128)(2,1)}, bf16[8,272,128]{2,1,0:T(8,128)(2,1)S(1)}, u32[]{:S(2)}, u32[]{:S(2)}) %collective-permute-start.15) | collective-permute-done | bytes 557088 | tf_op jit(solution)/shard_map/ppermute | solution.py:312
  180.5 3.1 %collective-permute-start.20 = (bf16[8,272,128]{2,1,0:T(8,128)(2,1)}, bf16[8,272,128]{2,1,0:T(8,128)(2,1)}, u32[]{:S(2)}, u32[]{:S(2)}) collective-permute-start(bf16[8,272,128]{2,1,0:T(8,128)(2,1)} %get-tuple-element.44), channel_id=1, source_target_pairs={{0,42},{1,127},{2,40},{3,125},{4,46},{5,123},{6,44},{7,121},{8,34}... | collective-permute-start | bytes 1671176 | tf_op jit(solution)/shard_map/ppermute | solution.py:312
  183.6 10.9 %collective-permute-done.17 = bf16[8,272,128]{2,1,0:T(8,128)(2,1)S(1)} collective-permute-done((bf16[8,272,128]{2,1,0:T(8,128)(2,1)}, bf16[8,272,128]{2,1,0:T(8,128)(2,1)S(1)}, u32[]{:S(2)}, u32[]{:S(2)}) %collective-permute-start.17) | collective-permute-done | bytes 557088 | tf_op jit(solution)/shard_map/ppermute | solution.py:312
  195.6 3.3 %collective-permute-done.19 = bf16[8,272,128]{2,1,0:T(8,128)(2,1)} collective-permute-done((bf16[8,272,128]{2,1,0:T(8,128)(2,1)}, bf16[8,272,128]{2,1,0:T(8,128)(2,1)}, u32[]{:S(2)}, u32[]{:S(2)}) %collective-permute-start.19) | collective-permute-done | bytes 557088 | tf_op jit(solution)/shard_map/ppermute | solution.py:312
  200.7 4.2 %add_convert_fusion = bf16[8,256,128]{2,1,0:T(8,128)(2,1)S(1)} fusion(bf16[8,272,128]{2,1,0:T(8,128)(2,1)} %collective-permute-done.20, bf16[8,272,128]{2,1,0:T(8,128)(2,1)} %collective-permute-done.19, bf16[8,272,128]{2,1,0:T(8,128)(2,1)} %collective-permute-done.18, bf16[8,272,128]{2,1,0:T(8,128)(2,1)S(1)} %collective-permute-done.17, ...), kind=kLoop, calls=%fused_computation.7 | loop fusion | flops 6291456 | bytes 4784128 | tf_op jit(solution)/shard_map/convert.16
  205.3 15.6 %collective-permute-start.21 = (bf16[1,272,128]{2,1,0:T(8,128)(2,1)S(1)}, bf16[1,272,128]{2,1,0:T(8,128)(2,1)S(1)}, u32[]{:S(2)}, u32[]{:S(2)}) collective-permute-start(bf16[1,272,128]{2,1,0:T(8,128)(2,1)S(1)} %get-tuple-element.55), channel_id=1, source_target_pairs={{0,4},{2,6},{4,0},{6,2},{8,12},{10,14},{12,8},{14,10},{16,20},{18,... | collective-permute-start | bytes 208904 | tf_op jit(solution)/shard_map/ppermute | solution.py:316
  221.0 3.0 %collective-permute-start.23 = (bf16[1,272,128]{2,1,0:T(8,128)(2,1)S(1)}, bf16[1,272,128]{2,1,0:T(8,128)(2,1)S(1)}, u32[]{:S(2)}, u32[]{:S(2)}) collective-permute-start(bf16[1,272,128]{2,1,0:T(8,128)(2,1)S(1)} %get-tuple-element.60), channel_id=1, source_target_pairs={{0,20},{2,22},{4,16},{6,18},{8,28},{10,30},{12,24},{14,26},{16,4},... | collective-permute-start | bytes 208904 | tf_op jit(solution)/shard_map/ppermute | solution.py:316
  224.0 3.0 %collective-permute-start.24 = (bf16[1,272,128]{2,1,0:T(8,128)(2,1)S(1)}, bf16[1,272,128]{2,1,0:T(8,128)(2,1)S(1)}, u32[]{:S(2)}, u32[]{:S(2)}) collective-permute-start(bf16[1,272,128]{2,1,0:T(8,128)(2,1)S(1)} %get-tuple-element.59), channel_id=1, source_target_pairs={{0,64},{2,66},{4,68},{6,70},{8,72},{10,74},{12,76},{14,78},{16,80}... | collective-permute-start | bytes 208904 | tf_op jit(solution)/shard_map/ppermute | solution.py:316
  227.0 3.4 %collective-permute-start.25 = (bf16[1,272,128]{2,1,0:T(8,128)(2,1)S(1)}, bf16[1,272,128]{2,1,0:T(8,128)(2,1)S(1)}, u32[]{:S(2)}, u32[]{:S(2)}) collective-permute-start(bf16[1,272,128]{2,1,0:T(8,128)(2,1)S(1)} %get-tuple-element.58), channel_id=1, source_target_pairs={{0,68},{2,70},{4,64},{6,66},{8,76},{10,78},{12,72},{14,74},{16,84}... | collective-permute-start | bytes 208904 | tf_op jit(solution)/shard_map/ppermute | solution.py:316
  230.4 2.2 collective-permute-start.26
  232.7 3.2 %collective-permute-start.27 = (bf16[1,272,128]{2,1,0:T(8,128)(2,1)S(1)}, bf16[1,272,128]{2,1,0:T(8,128)(2,1)S(1)}, u32[]{:S(2)}, u32[]{:S(2)}) collective-permute-start(bf16[1,272,128]{2,1,0:T(8,128)(2,1)S(1)} %get-tuple-element.56), channel_id=1, source_target_pairs={{0,84},{2,86},{4,80},{6,82},{8,92},{10,94},{12,88},{14,90},{16,68}... | collective-permute-start | bytes 208904 | tf_op jit(solution)/shard_map/ppermute | solution.py:316
  235.9 2.8 %collective-permute-done.26 = bf16[1,272,128]{2,1,0:T(8,128)(2,1)S(1)} collective-permute-done((bf16[1,272,128]{2,1,0:T(8,128)(2,1)S(1)}, bf16[1,272,128]{2,1,0:T(8,128)(2,1)S(1)}, u32[]{:S(2)}, u32[]{:S(2)}) %collective-permute-start.26) | collective-permute-done | bytes 69664 | tf_op jit(solution)/shard_map/ppermute | solution.py:316
  238.8 4.4 %collective-permute-done.27 = bf16[1,272,128]{2,1,0:T(8,128)(2,1)S(1)} collective-permute-done((bf16[1,272,128]{2,1,0:T(8,128)(2,1)S(1)}, bf16[1,272,128]{2,1,0:T(8,128)(2,1)S(1)}, u32[]{:S(2)}, u32[]{:S(2)}) %collective-permute-start.27) | collective-permute-done | bytes 69664 | tf_op jit(solution)/shard_map/ppermute | solution.py:316
  (147 shorter events, 23.5 us)
Async XLA Ops:
  0.0 52.8 %copy-start = (bf16[4,1,512]{2,0,1:T(4,128)(2,1)S(1)}, bf16[4,1,512]{2,0,1:T(4,128)(2,1)}, u32[]{:S(2)}) copy-start(bf16[4,1,512]{2,0,1:T(4,128)(2,1)} %param.16) | copy-start | bytes 12292
  2.0 31.0 %collective-permute-start = (bf16[384,128]{1,0:T(8,128)(2,1)S(1)}, bf16[384,128]{1,0:T(8,128)(2,1)S(1)}, u32[]{:S(2)}, u32[]{:S(2)}) collective-permute-start(bf16[384,128]{1,0:T(8,128)(2,1)S(1)} %pad_maximum_fusion), channel_id=1, source_target_pairs={{0,4},{2,6},{4,0},{6,2},{8,12},{10,14},{12,8},{14,10},{16,20},{18,... | collective-permute-start | bytes 294920 | tf_op jit(solution)/shard_map/ppermute | solution.py:316
  5.1 33.6 %collective-permute-start.1 = (bf16[384,128]{1,0:T(8,128)(2,1)S(1)}, bf16[384,128]{1,0:T(8,128)(2,1)S(1)}, u32[]{:S(2)}, u32[]{:S(2)}) collective-permute-start(bf16[384,128]{1,0:T(8,128)(2,1)S(1)} %pad_maximum_fusion), channel_id=1, source_target_pairs={{0,16},{2,18},{4,20},{6,22},{8,24},{10,26},{12,28},{14,30},{16,0},... | collective-permute-start | bytes 294920 | tf_op jit(solution)/shard_map/ppermute | solution.py:316
  8.3 33.3 %collective-permute-start.2 = (bf16[384,128]{1,0:T(8,128)(2,1)S(1)}, bf16[384,128]{1,0:T(8,128)(2,1)S(1)}, u32[]{:S(2)}, u32[]{:S(2)}) collective-permute-start(bf16[384,128]{1,0:T(8,128)(2,1)S(1)} %pad_maximum_fusion), channel_id=1, source_target_pairs={{0,20},{2,22},{4,16},{6,18},{8,28},{10,30},{12,24},{14,26},{16,4},... | collective-permute-start | bytes 294920 | tf_op jit(solution)/shard_map/ppermute | solution.py:316
  8.5 33.2 %collective-permute-start.3 = (bf16[384,128]{1,0:T(8,128)(2,1)S(1)}, bf16[384,128]{1,0:T(8,128)(2,1)S(1)}, u32[]{:S(2)}, u32[]{:S(2)}) collective-permute-start(bf16[384,128]{1,0:T(8,128)(2,1)S(1)} %pad_maximum_fusion), channel_id=1, source_target_pairs={{0,64},{2,66},{4,68},{6,70},{8,72},{10,74},{12,76},{14,78},{16,80}... | collective-permute-start | bytes 294920 | tf_op jit(solution)/shard_map/ppermute | solution.py:316
  12.5 29.2 %collective-permute-start.4 = (bf16[384,128]{1,0:T(8,128)(2,1)S(1)}, bf16[384,128]{1,0:T(8,128)(2,1)S(1)}, u32[]{:S(2)}, u32[]{:S(2)}) collective-permute-start(bf16[384,128]{1,0:T(8,128)(2,1)S(1)} %pad_maximum_fusion), channel_id=1, source_target_pairs={{0,68},{2,70},{4,64},{6,66},{8,76},{10,78},{12,72},{14,74},{16,84}... | collective-permute-start | bytes 294920 | tf_op jit(solution)/shard_map/ppermute | solution.py:316
  17.9 78.3 %all-to-all-start = ((s32[64,1,16]{2,1,0:T(1,128)}), s32[64,1,16]{2,1,0:T(1,128)S(1)}, u32[]{:S(2)}, u32[]{:S(2)}) async-start(s32[64,1,16]{2,1,0:T(1,128)} %bitcast.16), calls=%async_computation | async-start | bytes 65536 | tf_op jit(solution)/shard_map/all_to_all | solution.py:271
  33.0 8.8 %collective-permute-start.5 = (bf16[384,128]{1,0:T(8,128)(2,1)S(1)}, bf16[384,128]{1,0:T(8,128)(2,1)S(1)}, u32[]{:S(2)}, u32[]{:S(2)}) collective-permute-start(bf16[384,128]{1,0:T(8,128)(2,1)S(1)} %pad_maximum_fusion), channel_id=1, source_target_pairs={{0,80},{2,82},{4,84},{6,86},{8,88},{10,90},{12,92},{14,94},{16,64}... | collective-permute-start | bytes 294920 | tf_op jit(solution)/shard_map/ppermute | solution.py:316
  38.7 11.0 %collective-permute-start.6 = (bf16[384,128]{1,0:T(8,128)(2,1)S(1)}, bf16[384,128]{1,0:T(8,128)(2,1)S(1)}, u32[]{:S(2)}, u32[]{:S(2)}) collective-permute-start(bf16[384,128]{1,0:T(8,128)(2,1)S(1)} %pad_maximum_fusion), channel_id=1, source_target_pairs={{0,84},{2,86},{4,80},{6,82},{8,92},{10,94},{12,88},{14,90},{16,68}... | collective-permute-start | bytes 294920 | tf_op jit(solution)/shard_map/ppermute | solution.py:316
  49.8 44.9 %copy-start.1 = (bf16[8,384,128]{2,1,0:T(8,128)(2,1)}, bf16[8,384,128]{2,1,0:T(8,128)(2,1)S(1)}, u32[]{:S(2)}) copy-start(bf16[8,384,128]{2,1,0:T(8,128)(2,1)S(1)} %bitcast_dynamic-update-slice_fusion.refs_0_) | copy-start | bytes 2359300
  49.8 37.3 %collective-permute-start.10 = (bf16[8,384,128]{2,1,0:T(8,128)(2,1)S(1)}, bf16[8,384,128]{2,1,0:T(8,128)(2,1)S(1)}, u32[]{:S(2)}, u32[]{:S(2)}) collective-permute-start(bf16[8,384,128]{2,1,0:T(8,128)(2,1)S(1)} %bitcast_dynamic-update-slice_fusion.refs_0_), channel_id=1, source_target_pairs={{0,32},{1,97},{2,34},{3,99},{4,36},{5,101},{6,38},{7,103},{8,40},{... | collective-permute-start | bytes 2359304 | tf_op jit(solution)/shard_map/ppermute | solution.py:312
  50.6 37.1 %collective-permute-start.11 = (bf16[8,384,128]{2,1,0:T(8,128)(2,1)S(1)}, bf16[8,384,128]{2,1,0:T(8,128)(2,1)S(1)}, u32[]{:S(2)}, u32[]{:S(2)}) collective-permute-start(bf16[8,384,128]{2,1,0:T(8,128)(2,1)S(1)} %bitcast_dynamic-update-slice_fusion.refs_0_), channel_id=1, source_target_pairs={{0,34},{1,103},{2,32},{3,101},{4,38},{5,99},{6,36},{7,97},{8,42},{... | collective-permute-start | bytes 2359304 | tf_op jit(solution)/shard_map/ppermute | solution.py:312
  53.6 41.1 %copy-start.2 = (bf16[96,4096]{1,0:T(8,128)(2,1)S(1)}, bf16[96,4096]{1,0:T(8,128)(2,1)}, u32[]{:S(2)}) copy-start(bf16[96,4096]{1,0:T(8,128)(2,1)} %param.15) | copy-start | bytes 2359300
  53.6 43.9 %collective-permute-start.12 = (bf16[8,384,128]{2,1,0:T(8,128)(2,1)S(1)}, bf16[8,384,128]{2,1,0:T(8,128)(2,1)}, u32[]{:S(2)}, u32[]{:S(2)}) collective-permute-start(bf16[8,384,128]{2,1,0:T(8,128)(2,1)S(1)} %bitcast_dynamic-update-slice_fusion.refs_0_), channel_id=1, source_target_pairs={{0,40},{1,121},{2,42},{3,123},{4,44},{5,125},{6,46},{7,127},{8,32}... | collective-permute-start | bytes 2359304 | tf_op jit(solution)/shard_map/ppermute | solution.py:312
  54.5 43.0 %collective-permute-start.13 = (bf16[8,384,128]{2,1,0:T(8,128)(2,1)S(1)}, bf16[8,384,128]{2,1,0:T(8,128)(2,1)}, u32[]{:S(2)}, u32[]{:S(2)}) collective-permute-start(bf16[8,384,128]{2,1,0:T(8,128)(2,1)S(1)} %bitcast_dynamic-update-slice_fusion.refs_0_), channel_id=1, source_target_pairs={{0,42},{1,127},{2,40},{3,125},{4,46},{5,123},{6,44},{7,121},{8,34}... | collective-permute-start | bytes 2359304 | tf_op jit(solution)/shard_map/ppermute | solution.py:312
  56.6 40.9 %collective-permute-start.7 = (bf16[8,384,128]{2,1,0:T(8,128)(2,1)S(1)}, bf16[8,384,128]{2,1,0:T(8,128)(2,1)}, u32[]{:S(2)}, u32[]{:S(2)}) collective-permute-start(bf16[8,384,128]{2,1,0:T(8,128)(2,1)S(1)} %bitcast_dynamic-update-slice_fusion.refs_0_), channel_id=1, source_target_pairs={{0,2},{1,7},{2,0},{3,5},{4,6},{5,3},{6,4},{7,1},{8,10},{9,15},{10,... | collective-permute-start | bytes 2359304 | tf_op jit(solution)/shard_map/ppermute | solution.py:312
  87.1 20.5 %collective-permute-start.8 = (bf16[8,384,128]{2,1,0:T(8,128)(2,1)S(1)}, bf16[8,384,128]{2,1,0:T(8,128)(2,1)}, u32[]{:S(2)}, u32[]{:S(2)}) collective-permute-start(bf16[8,384,128]{2,1,0:T(8,128)(2,1)S(1)} %bitcast_dynamic-update-slice_fusion.refs_0_), channel_id=1, source_target_pairs={{0,8},{1,25},{2,10},{3,27},{4,12},{5,29},{6,14},{7,31},{8,0},{9,17... | collective-permute-start | bytes 2359304 | tf_op jit(solution)/shard_map/ppermute | solution.py:312
  87.7 19.9 %collective-permute-start.9 = (bf16[8,384,128]{2,1,0:T(8,128)(2,1)S(1)}, bf16[8,384,128]{2,1,0:T(8,128)(2,1)}, u32[]{:S(2)}, u32[]{:S(2)}) collective-permute-start(bf16[8,384,128]{2,1,0:T(8,128)(2,1)S(1)} %bitcast_dynamic-update-slice_fusion.refs_0_), channel_id=1, source_target_pairs={{0,10},{1,31},{2,8},{3,29},{4,14},{5,27},{6,12},{7,25},{8,2},{9,23... | collective-permute-start | bytes 2359304 | tf_op jit(solution)/shard_map/ppermute | solution.py:312
  161.1 9.8 %collective-permute-start.14 = (bf16[8,272,128]{2,1,0:T(8,128)(2,1)}, bf16[8,272,128]{2,1,0:T(8,128)(2,1)S(1)}, u32[]{:S(2)}, u32[]{:S(2)}) collective-permute-start(bf16[8,272,128]{2,1,0:T(8,128)(2,1)} %get-tuple-element.38), channel_id=1, source_target_pairs={{0,2},{1,7},{2,0},{3,5},{4,6},{5,3},{6,4},{7,1},{8,10},{9,15},{10,... | collective-permute-start | bytes 1671176 | tf_op jit(solution)/shard_map/ppermute | solution.py:312
  162.6 17.9 %collective-permute-start.15 = (bf16[8,272,128]{2,1,0:T(8,128)(2,1)}, bf16[8,272,128]{2,1,0:T(8,128)(2,1)S(1)}, u32[]{:S(2)}, u32[]{:S(2)}) collective-permute-start(bf16[8,272,128]{2,1,0:T(8,128)(2,1)} %get-tuple-element.39), channel_id=1, source_target_pairs={{0,8},{1,25},{2,10},{3,27},{4,12},{5,29},{6,14},{7,31},{8,0},{9,17... | collective-permute-start | bytes 1671176 | tf_op jit(solution)/shard_map/ppermute | solution.py:312
  166.8 16.8 %collective-permute-start.16 = (bf16[8,272,128]{2,1,0:T(8,128)(2,1)}, bf16[8,272,128]{2,1,0:T(8,128)(2,1)S(1)}, u32[]{:S(2)}, u32[]{:S(2)}) collective-permute-start(bf16[8,272,128]{2,1,0:T(8,128)(2,1)} %get-tuple-element.40), channel_id=1, source_target_pairs={{0,10},{1,31},{2,8},{3,29},{4,14},{5,27},{6,12},{7,25},{8,2},{9,23... | collective-permute-start | bytes 1671176 | tf_op jit(solution)/shard_map/ppermute | solution.py:312
  166.8 27.7 %collective-permute-start.17 = (bf16[8,272,128]{2,1,0:T(8,128)(2,1)}, bf16[8,272,128]{2,1,0:T(8,128)(2,1)S(1)}, u32[]{:S(2)}, u32[]{:S(2)}) collective-permute-start(bf16[8,272,128]{2,1,0:T(8,128)(2,1)} %get-tuple-element.41), channel_id=1, source_target_pairs={{0,32},{1,97},{2,34},{3,99},{4,36},{5,101},{6,38},{7,103},{8,40},{... | collective-permute-start | bytes 1671176 | tf_op jit(solution)/shard_map/ppermute | solution.py:312
  169.2 25.6 %collective-permute-start.18 = (bf16[8,272,128]{2,1,0:T(8,128)(2,1)}, bf16[8,272,128]{2,1,0:T(8,128)(2,1)}, u32[]{:S(2)}, u32[]{:S(2)}) collective-permute-start(bf16[8,272,128]{2,1,0:T(8,128)(2,1)} %get-tuple-element.42), channel_id=1, source_target_pairs={{0,34},{1,103},{2,32},{3,101},{4,38},{5,99},{6,36},{7,97},{8,42},{... | collective-permute-start | bytes 1671176 | tf_op jit(solution)/shard_map/ppermute | solution.py:312
  170.9 28.0 %collective-permute-start.19 = (bf16[8,272,128]{2,1,0:T(8,128)(2,1)}, bf16[8,272,128]{2,1,0:T(8,128)(2,1)}, u32[]{:S(2)}, u32[]{:S(2)}) collective-permute-start(bf16[8,272,128]{2,1,0:T(8,128)(2,1)} %get-tuple-element.43), channel_id=1, source_target_pairs={{0,40},{1,121},{2,42},{3,123},{4,44},{5,125},{6,46},{7,127},{8,32}... | collective-permute-start | bytes 1671176 | tf_op jit(solution)/shard_map/ppermute | solution.py:312
  180.5 19.2 %collective-permute-start.20 = (bf16[8,272,128]{2,1,0:T(8,128)(2,1)}, bf16[8,272,128]{2,1,0:T(8,128)(2,1)}, u32[]{:S(2)}, u32[]{:S(2)}) collective-permute-start(bf16[8,272,128]{2,1,0:T(8,128)(2,1)} %get-tuple-element.44), channel_id=1, source_target_pairs={{0,42},{1,127},{2,40},{3,125},{4,46},{5,123},{6,44},{7,121},{8,34}... | collective-permute-start | bytes 1671176 | tf_op jit(solution)/shard_map/ppermute | solution.py:312
  205.3 25.2 %collective-permute-start.21 = (bf16[1,272,128]{2,1,0:T(8,128)(2,1)S(1)}, bf16[1,272,128]{2,1,0:T(8,128)(2,1)S(1)}, u32[]{:S(2)}, u32[]{:S(2)}) collective-permute-start(bf16[1,272,128]{2,1,0:T(8,128)(2,1)S(1)} %get-tuple-element.55), channel_id=1, source_target_pairs={{0,4},{2,6},{4,0},{6,2},{8,12},{10,14},{12,8},{14,10},{16,20},{18,... | collective-permute-start | bytes 208904 | tf_op jit(solution)/shard_map/ppermute | solution.py:316
  220.9 11.8 %collective-permute-start.22 = (bf16[1,272,128]{2,1,0:T(8,128)(2,1)S(1)}, bf16[1,272,128]{2,1,0:T(8,128)(2,1)S(1)}, u32[]{:S(2)}, u32[]{:S(2)}) collective-permute-start(bf16[1,272,128]{2,1,0:T(8,128)(2,1)S(1)} %get-tuple-element.61), channel_id=1, source_target_pairs={{0,16},{2,18},{4,20},{6,22},{8,24},{10,26},{12,28},{14,30},{16,0},... | collective-permute-start | bytes 208904 | tf_op jit(solution)/shard_map/ppermute | solution.py:316
  221.0 14.9 %collective-permute-start.23 = (bf16[1,272,128]{2,1,0:T(8,128)(2,1)S(1)}, bf16[1,272,128]{2,1,0:T(8,128)(2,1)S(1)}, u32[]{:S(2)}, u32[]{:S(2)}) collective-permute-start(bf16[1,272,128]{2,1,0:T(8,128)(2,1)S(1)} %get-tuple-element.60), channel_id=1, source_target_pairs={{0,20},{2,22},{4,16},{6,18},{8,28},{10,30},{12,24},{14,26},{16,4},... | collective-permute-start | bytes 208904 | tf_op jit(solution)/shard_map/ppermute | solution.py:316
  224.0 11.9 %collective-permute-start.24 = (bf16[1,272,128]{2,1,0:T(8,128)(2,1)S(1)}, bf16[1,272,128]{2,1,0:T(8,128)(2,1)S(1)}, u32[]{:S(2)}, u32[]{:S(2)}) collective-permute-start(bf16[1,272,128]{2,1,0:T(8,128)(2,1)S(1)} %get-tuple-element.59), channel_id=1, source_target_pairs={{0,64},{2,66},{4,68},{6,70},{8,72},{10,74},{12,76},{14,78},{16,80}... | collective-permute-start | bytes 208904 | tf_op jit(solution)/shard_map/ppermute | solution.py:316
  227.0 8.9 %collective-permute-start.25 = (bf16[1,272,128]{2,1,0:T(8,128)(2,1)S(1)}, bf16[1,272,128]{2,1,0:T(8,128)(2,1)S(1)}, u32[]{:S(2)}, u32[]{:S(2)}) collective-permute-start(bf16[1,272,128]{2,1,0:T(8,128)(2,1)S(1)} %get-tuple-element.58), channel_id=1, source_target_pairs={{0,68},{2,70},{4,64},{6,66},{8,76},{10,78},{12,72},{14,74},{16,84}... | collective-permute-start | bytes 208904 | tf_op jit(solution)/shard_map/ppermute | solution.py:316
  230.4 8.2 %collective-permute-start.26 = (bf16[1,272,128]{2,1,0:T(8,128)(2,1)S(1)}, bf16[1,272,128]{2,1,0:T(8,128)(2,1)S(1)}, u32[]{:S(2)}, u32[]{:S(2)}) collective-permute-start(bf16[1,272,128]{2,1,0:T(8,128)(2,1)S(1)} %get-tuple-element.57), channel_id=1, source_target_pairs={{0,80},{2,82},{4,84},{6,86},{8,88},{10,90},{12,92},{14,94},{16,64}... | collective-permute-start | bytes 208904 | tf_op jit(solution)/shard_map/ppermute | solution.py:316
  232.7 10.6 %collective-permute-start.27 = (bf16[1,272,128]{2,1,0:T(8,128)(2,1)S(1)}, bf16[1,272,128]{2,1,0:T(8,128)(2,1)S(1)}, u32[]{:S(2)}, u32[]{:S(2)}) collective-permute-start(bf16[1,272,128]{2,1,0:T(8,128)(2,1)S(1)} %get-tuple-element.56), channel_id=1, source_target_pairs={{0,84},{2,86},{4,80},{6,82},{8,92},{10,94},{12,88},{14,90},{16,68}... | collective-permute-start | bytes 208904 | tf_op jit(solution)/shard_map/ppermute | solution.py:316
  (3 other events, 15.5 us)

commit v4 on v2

--- a/solution.py
+++ b/solution.py
@@ -10,7 +10,7 @@
 
 MAX_PAGES = 10
 NEG = -1e30
-VMEM_BYTES = 62 * 1024 * 1024
+VMEM_BYTES = 52 * 1024 * 1024
 PER = 2
 PIECES = 4
 NT = (((1,), (1,)), ((), ()))
@@ -49,10 +49,10 @@
         halves.append(jnp.where(first, out[:, :, :value], out[:, :, value:]))
     packed[:, sixteen(at), :] = jnp.concatenate(halves, axis=1).astype(jnp.bfloat16)
 
-def attend_step(scale, at, counts_ref, slots_ref, packed_ref, lat_ref, keyrope_ref, held, keys, rotated, tops, totals):
+def attend_step(scale, at, lists_ref, packed_ref, lat_ref, keyrope_ref, held, keys, rotated, tops, totals):
     queries, latent = held.shape[1:]
     page = lat_ref.shape[1]
-    counts = [counts_ref[at * PER + i] for i in range(PER)]
+    counts = [lists_ref[at * PER + i, 0] for i in range(PER)]
     most = functools.reduce(jnp.maximum, counts)
 
     def run(pages):
@@ -63,7 +63,7 @@
         for i in range(PER):
             r = at * PER + i
             for k in range(pages):
-                slot = slots_ref[r, k]
+                slot = lists_ref[r, 1 + k]
                 keys[i, k * page : (k + 1) * page, :] = lat_ref[slot]
                 rotated[i, k * page : (k + 1) * page, :] = keyrope_ref[slot]
             packed = packed_ref[r, queries : queries + queries // 2, :]
@@ -106,7 +106,7 @@
             out = jnp.where(row == level * per + c, part, out)
     packed[:, queries : queries + 16, :] = jnp.concatenate([out, jnp.zeros_like(out)], axis=1).astype(jnp.bfloat16)
 
-def body(scale, counts_ref, slots_ref, packed_hbm, upk_hbm, lat_hbm, keyrope_hbm, upv_hbm, out_hbm,
+def body(scale, lists_ref, packed_hbm, upk_hbm, lat_hbm, keyrope_hbm, upv_hbm, out_hbm,
          packed, upk, lat, keyrope, upv, held, keys, rotated, tops, totals, in_sems, key_sems, value_sems, out_sems):
     heads = upk.shape[0]
     queries = held.shape[1]
@@ -120,7 +120,9 @@
     def out_copy(at):
         return pltpu.make_async_copy(packed.at[:, sixteen(at), :], out_hbm.at[:, sixteen(at), :], out_sems.at[at])
 
-    load_packed = pltpu.make_async_copy(packed_hbm, packed, in_sems.at[0])
+    load_packed = pltpu.make_async_copy(
+        packed_hbm.at[:, pl.ds(0, packed.shape[1]), :], packed, in_sems.at[0]
+    )
     load_lat = pltpu.make_async_copy(lat_hbm, lat, in_sems.at[1])
     load_rope = pltpu.make_async_copy(keyrope_hbm, keyrope, in_sems.at[2])
     load_packed.start()
@@ -146,7 +148,7 @@
     load_rope.wait()
 
     def attend(at, _):
-        attend_step(scale, at, counts_ref, slots_ref, packed, lat, keyrope, held, keys, rotated, tops, totals)
+        attend_step(scale, at, lists_ref, packed, lat, keyrope, held, keys, rotated, tops, totals)
         return 0
     lax.fori_loop(0, held.shape[0] // PER, attend, 0)
 
@@ -165,7 +167,7 @@
         return 0
     lax.fori_loop(0, groups + 1, drain, 0)
 
-def attention(counts, slots, packed, up_key, up_value, pool_latent, pool_rope, scale):
+def attention(lists, packed, up_key, up_value, pool_latent, pool_rope, scale):
     rows = packed.shape[0]
     heads, nope, latent = up_key.shape
     value = up_value.shape[2]
@@ -177,10 +179,10 @@
     return pl.pallas_call(
         functools.partial(body, scale),
         out_shape=jax.ShapeDtypeStruct((rows, queries + 16, value), jnp.bfloat16),
-        in_specs=[scalars] * 2 + [anywhere] * 5,
+        in_specs=[scalars] + [anywhere] * 5,
         out_specs=anywhere,
         scratch_shapes=[
-            pltpu.VMEM(packed.shape, jnp.bfloat16),
+            pltpu.VMEM((rows, queries + queries // 2, nope), jnp.bfloat16),
             pltpu.VMEM(up_key.shape, jnp.bfloat16),
             pltpu.VMEM(pool_latent.shape, jnp.bfloat16),
             pltpu.VMEM(pool_rope.shape, jnp.bfloat16),
@@ -196,8 +198,11 @@
             pltpu.SemaphoreType.DMA((heads // 4 + 1,)),
         ],
         compiler_params=pltpu.CompilerParams(vmem_limit_bytes=VMEM_BYTES),
+        cost_estimate=pl.CostEstimate(
+            flops=rows * queries * 640 * 4 * latent, bytes_accessed=1 << 27, transcendentals=0
+        ),
         name="attention",
-    )(counts, slots, packed, up_key, pool_latent, pool_rope, up_value)
+    )(lists, packed, up_key, pool_latent, pool_rope, up_value)
 
 def fresh_part(q_nope, q_rope, up_key, up_value, new_latent, new_rope, scale):
     steps, heads, _ = q_nope.shape
@@ -242,8 +247,74 @@
     )
 
 
-def exchange(x):
-    return lax.all_to_all(x, "batch", split_axis=0, concat_axis=0, tiled=True)
+SIDE = 4
+HALVES = 2
+
+
+def corner_index(bits):
+    return (bits[0] * 2 + bits[1]) * 2 + bits[2]
+
+
+def grouped(cores, key):
+    groups = {}
+    for i in range(SIDE**3):
+        at = (i // (SIDE * SIDE), i // SIDE % SIDE, i % SIDE)
+        for core in range(cores):
+            group, position = key(at, core)
+            groups.setdefault((core,) + group, {})[corner_index(position)] = i * cores + core
+    return [[group[p] for p in sorted(group)] for _, group in sorted(groups.items())]
+
+
+def sublattice(at, core):
+    return tuple(v % 2 for v in at), tuple(v // 2 for v in at)
+
+
+def block(at, core):
+    return tuple((v - core) % SIDE // 2 for v in at), tuple((v - core) % 2 for v in at)
+
+
+def exchange(x, key):
+    groups = grouped(lax.axis_size("head"), key)
+    return lax.all_to_all(
+        x, ("batch", "head"), split_axis=0, concat_axis=0, tiled=True, axis_index_groups=groups
+    )
+
+
+def spread(x, key):
+    return exchange(jnp.broadcast_to(x[None], (8,) + x.shape), key)
+
+
+def mix(parts, queries, fresh=None):
+    count, rows, _, value = parts.shape
+    extra = queries // value
+    lse = parts[:, :, queries : queries + 3 * extra].astype(jnp.float32)
+    lse = jnp.sum(lse.reshape(count, rows, 3, queries), axis=2)
+    top = jnp.max(lse, axis=0)
+    if fresh is not None:
+        top = jnp.maximum(top, fresh[1])
+    share = jnp.exp(lse - top)
+    total = jnp.sum(share, axis=0)
+    if fresh is not None:
+        fresh_share = jnp.exp(fresh[1] - top)
+        total = total + fresh_share
+    out = jnp.sum(
+        parts[:, :, :queries].astype(jnp.float32) * (share / total)[..., None], axis=0
+    )
+    if fresh is not None:
+        out = out + fresh[0] * (fresh_share / total)[..., None]
+    return out, top + jnp.log(total)
+
+
+def pack(out, lse):
+    rows, queries, value = out.shape
+    pieces, left = [], lse
+    for _ in range(3):
+        piece = lax.reduce_precision(left, 8, 7)
+        left = left - piece
+        pieces.append(piece.reshape(rows, queries // value, value))
+    extra = 16 - 3 * queries // value
+    pieces.append(jnp.zeros((rows, extra, value), jnp.float32))
+    return jnp.concatenate([out] + pieces, axis=1).astype(jnp.bfloat16)
 
 
 def per_device(
@@ -263,38 +334,38 @@
     nope_rows = q_nope.transpose(1, 0, 2).reshape(heads * steps, nope)
     rope_rows = q_rope.transpose(1, 0, 2).reshape(2, heads * steps // 2, rope)
     rope_rows = rope_rows.transpose(1, 0, 2).reshape(heads * steps // 2, 2 * rope)
-    own = jnp.concatenate([nope_rows, rope_rows], axis=0)
-    packed = lax.all_gather(own, "batch", axis=0, tiled=False)
-
-    lists = exchange(page_lists(page_shard[0, :, 0], page_slot[0], shards))
-    fresh_out, fresh_lse = fresh_part(
+    lists = page_lists(page_shard[0, :, 0], page_slot[0], shards)
+    wide = lists.shape[1]
+    list_rows = lists.astype(jnp.bfloat16).reshape(shards * wide // nope, nope)
+    list_rows = jnp.pad(list_rows, ((0, 16 - list_rows.shape[0]), (0, 0)))
+    own = jnp.concatenate([nope_rows, rope_rows, list_rows], axis=0)
+    queries = heads * steps
+    length = queries + queries // 2
+
+    near = spread(own, sublattice)
+    count = near.shape[0] // HALVES
+    pool_rope = pool_rope.reshape(slots_total, page, rope)
+    me = lax.axis_index("batch")
+    gathered = [
+        spread(near[k * count : (k + 1) * count], block) for k in range(HALVES)
+    ]
+    fresh = fresh_part(
         q_nope, q_rope, up_key, up_value, new_latent[:, 0], new_rope.reshape(steps, rope), scale
     )
-    pool_rope = pool_rope.reshape(slots_total, page, rope)
-    packed, lists, fresh_out, fresh_lse, pool_rope = lax.optimization_barrier(
-        (packed, lists, fresh_out, fresh_lse, pool_rope)
-    )
-    parts = exchange(
-        attention(
-            lists[:, 0], lists[:, 1 : 1 + MAX_PAGES], packed, up_key, up_value,
-            pool_latent, pool_rope, scale,
-        )
-    )
-    queries = heads * steps
-    extra = queries // value
-    lse = parts[:, queries : queries + 3 * extra].astype(jnp.float32)
-    lse = jnp.sum(lse.reshape(shards, 3, queries), axis=1)
-    parts = parts[:, :queries]
-
-    fresh_lse = fresh_lse.reshape(1, heads * steps)
-    top = jnp.maximum(jnp.max(lse, axis=0, keepdims=True), fresh_lse)
-    share = jnp.exp(lse - top)
-    fresh_share = jnp.exp(fresh_lse - top)
-    total = jnp.sum(share, axis=0, keepdims=True) + fresh_share
-    share = share / total
-    fresh_share = (fresh_share / total).reshape(heads * steps, 1)
-    out = jnp.sum(parts.astype(jnp.float32) * share[:, :, None], axis=0)
-    out = out + fresh_share * fresh_out.reshape(heads * steps, value)
+    returned = []
+    for k in range(HALVES):
+        packed = gathered[k].reshape(8 * count, own.shape[0], nope)
+        lists = packed[:, length : length + shards * wide // nope]
+        lists = lists.reshape(8 * count, shards, wide)
+        lists = lax.dynamic_index_in_dim(lists, me, 1, keepdims=False).astype(jnp.int32)
+        parts = attention(lists, packed, up_key, up_value, pool_latent, pool_rope, scale)
+        if k + 1 < HALVES:
+            parts, gathered[k + 1] = lax.optimization_barrier((parts, gathered[k + 1]))
+        parts = exchange(parts.reshape(8, count, queries + 16, value), block)
+        returned.append(pack(*mix(parts, queries)))
+    rows = exchange(jnp.concatenate(returned, axis=0), sublattice)
+    fresh = (fresh[0].reshape(1, queries, value), fresh[1].reshape(1, queries))
+    out, _ = mix(rows[:, None], queries, fresh)
     out = out.astype(jnp.bfloat16).reshape(heads, steps, value).transpose(1, 0, 2)
     return out.reshape(steps, 1, heads * value)
 

time: 233 us -> 205 us (0.88)
  waiting for transfers between devices: 107 us -> 19.2 us
  blocking collectives: 0 us -> 54.2 us
  between operations: 13.6 us -> 0.38 us
  Pallas kernels: 49.3 us -> 58.4 us
  starting transfers between devices: 33.5 us -> 40.6 us
    all_to_all x0 -> x2, blocking collectives: none -> 54.2 us  [exchange(): lax.all_to_all(x, ('batch', 'head'), split_axis=0, concat_axis=0, tiled=T...]
    all_gather x1 -> x0, waiting for transfers between devices: 49.4 us -> none  [per_device(): packed = lax.all_gather(own, 'batch', axis=0, tiled=False)]
    all_to_all x2 -> x4, waiting for transfers between devices: 57.2 us -> 19.2 us  [exchange(): lax.all_to_all(x, ('batch', 'head'), split_axis=0, concat_axis=0, tiled=T...]
    pallas_call x1 -> x2, Pallas kernels: 49.3 us -> 58.4 us  [attention(): pl.pallas_call(functools.partial(body, scale), out_shape=jax.ShapeDtypeSt...]
    all_to_all x2 -> x4, starting transfers between devices: 33.5 us -> 40.6 us  [exchange(): lax.all_to_all(x, ('batch', 'head'), split_axis=0, concat_axis=0, tiled=T...]
    optimization_barrier x2 -> x0, local copies, waits for them, and re-layouts: 3.15 us -> none  [per_device(): lax.optimization_barrier((packed, lists, fresh_out, fresh_lse, pool_rope))]
    broadcast_in_dim x0 -> x3, local copies, waits for them, and re-layouts: none -> 2.67 us  [spread(): return exchange(jnp.broadcast_to(x[None], (8,) + x.shape), key)]
    reduce_sum x3 -> x9, other arithmetic: 4.64 us -> 5.17 us  [the longest x3 4.86 us: mix(): jnp.sum(parts[:, :, :queries].astype(jnp.float32) * (share / total)[...,...]
  transfers between devices with their start and end apart: 3 -> 4, of which waited for: 2 -> 2; matrix products, arithmetic and copies ran while one was open for 6% -> 6% of each run, Pallas kernels for 0% -> 29%
where the time goes in v4:
time: 205 us; the launch traced here: 204 us
  Pallas kernels  58.4 us (28%)
  blocking collectives  54.2 us (26%)
  starting transfers between devices  40.6 us (20%)
  waiting for transfers between devices  19.2 us (9%)
  local copies, waits for them, and re-layouts  10.9 us (5%)
  matrix products  10.6 us (5%)
  other arithmetic  10.2 us (5%)
    pallas_call x2, Pallas kernels, attention(): pl.pallas_call(functools.partial(body, scale), out_shape=jax.ShapeDtypeSt...  58.4 us
    all_to_all x2, blocking collectives, exchange(): lax.all_to_all(x, ('batch', 'head'), split_axis=0, concat_axis=0, tiled=T...  54.2 us
    all_to_all x4, starting transfers between devices, exchange(): lax.all_to_all(x, ('batch', 'head'), split_axis=0, concat_axis=0, tiled=T...  40.6 us
    all_to_all x4, waiting for transfers between devices, exchange(): lax.all_to_all(x, ('batch', 'head'), split_axis=0, concat_axis=0, tiled=T...  19.2 us
    dot_general x1, matrix products, fresh_part(): jnp.einsum('hsl,hlv->hsv', mixed, up_value, preferred_element_type=jnp.fl...  5.26 us
    reduce_sum x3, other arithmetic, mix(): jnp.sum(parts[:, :, :queries].astype(jnp.float32) * (share / total)[...,...  4.86 us
    dot_general x1, matrix products, fresh_part(): jnp.einsum('shn,hnl->hsl', q_nope, up_key, preferred_element_type=jnp.flo...  4.57 us
  transfers between devices with their start and end apart: 4, of which 2 were waited for; matrix products, arithmetic and copies ran while one was open for 6% of the time, Pallas kernels for 29%

profile of v4, /device:TPU:1, one launch (start us, length us, event | category | flops | bytes accessed | tf_op | source)
XLA Modules:
  0.0 204.5 jit_solution(7168535966124240963)
XLA Ops:
  0.0 0.7 reduce.6
  0.7 0.2 convert_reduce_fusion
  1.1 0.7 reduce.7
  1.8 0.3 select_reduce_fusion
  2.5 0.9 reshape.334
  3.6 0.9 fusion.12
  4.6 26.9 %all_to_all.30 = bf16[8,400,128]{2,1,0:T(8,128)(2,1)S(1)} all-to-all(bf16[8,400,128]{2,1,0:T(8,128)(2,1)S(1)} %broadcast_in_dim.87), channel_id=1, replica_groups={{0,4,16,20,64,68,80,84},{2,6,18,22,66,70,82,86},{8,12,24,28,72,76,88,92..., dimensions={0} | all-to-all | bytes 1638400 | tf_op jit(solution)/shard_map/all_to_all | solution.py:278
  31.5 0.4 broadcast_in_dim.88
  32.0 27.4 %all_to_all.31 = bf16[8,4,400,128]{3,2,1,0:T(8,128)(2,1)} all-to-all(bf16[8,4,400,128]{3,2,1,0:T(8,128)(2,1)S(1)} %broadcast_in_dim.88), channel_id=1, replica_groups={{0,2,8,10,32,34,40,42},{4,6,12,14,36,38,44,46},{16,18,24,26,48,50,56,58..., dimensions={0} | all-to-all | bytes 6553600 | tf_op jit(solution)/shard_map/all_to_all | solution.py:278
  59.3 2.1 %broadcast_in_dim.89 = bf16[8,4,400,128]{3,2,1,0:T(8,128)(2,1)} broadcast(bf16[4,400,128]{2,1,0:T(8,128)(2,1)S(1)} %get-tuple-element.9), dimensions={1,2,3} | broadcast | bytes 3686400 | tf_op jit(solution)/shard_map/broadcast_in_dim | solution.py:284
  61.5 10.8 %all-to-all-start.2 = ((bf16[8,4,400,128]{3,2,1,0:T(8,128)(2,1)}), bf16[8,4,400,128]{3,2,1,0:T(8,128)(2,1)}, u32[]{:S(2)}, u32[]{:S(2)}) async-start(bf16[8,4,400,128]{3,2,1,0:T(8,128)(2,1)} %broadcast_in_dim.89), calls=%async_computation.2 | async-start | bytes 6553600 | tf_op jit(solution)/shard_map/all_to_all | solution.py:278
  72.3 0.6 copy.55
  72.9 2.4 %copy.56.keyrope_hbm = bf16[96,64,64]{2,1,0:T(8,128)(2,1)S(1)} copy(bf16[96,64,64]{0,2,1:T(8,128)(2,1)S(1)} %bitcast.65) | data formatting | bytes 1572864 | tf_op jit(solution)/shard_map/reshape | solution.py:347
  75.3 0.8 slice.41
  76.5 29.1 %attention.2 = bf16[32,272,128]{2,1,0:T(8,128)(2,1)} custom-call(s32[32,16]{1,0:T(8,128)S(1)} %bitcast_convert_fusion.1.lists_ref, bf16[32,400,128]{2,1,0:T(8,128)(2,1)} %bitcast.67, bf16[64,128,512]{2,1,0:T(8,128)(2,1)} %upk_hbm.3, bf16[96,64,512]{2,1,0:T(8,128)(2,1)} %lat_hbm.3, bf16[96,64,64]{2,1,0:T(8,128)(2,1)S(1)} %copy.56.keyrope_hbm, ...), custom_call_target="tpu_custom_call" | custom-call | flops 10737418240 | bytes 134217728 | tf_op jit(solution)/shard_map/attention/pallas_call | solution.py:179
  105.6 8.2 %all-to-all-start.3 = ((bf16[8,4,272,128]{3,2,1,0:T(8,128)(2,1)}), bf16[8,4,272,128]{3,2,1,0:T(8,128)(2,1)}, u32[]{:S(2)}, u32[]{:S(2)}) async-start(bf16[8,4,272,128]{3,2,1,0:T(8,128)(2,1)} %bitcast.69), calls=%async_computation.3 | async-start | bytes 4456448 | tf_op jit(solution)/shard_map/all_to_all | solution.py:278
  113.7 0.8 slice.45
  114.9 29.3 %attention.3 = bf16[32,272,128]{2,1,0:T(8,128)(2,1)} custom-call(s32[32,16]{1,0:T(8,128)S(1)} %bitcast_convert_fusion.lists_ref, bf16[32,400,128]{2,1,0:T(8,128)(2,1)} %bitcast.13.packed_hbm, bf16[64,128,512]{2,1,0:T(8,128)(2,1)} %upk_hbm.3, bf16[96,64,512]{2,1,0:T(8,128)(2,1)} %lat_hbm.3, bf16[96,64,64]{2,1,0:T(8,128)(2,1)S(1)} %copy.56.keyrope_hbm, ...), custom_call_target="tpu_custom_call" | custom-call | flops 10737418240 | bytes 134217728 | tf_op jit(solution)/shard_map/attention/pallas_call | solution.py:179
  144.2 8.3 %all-to-all-start.4 = ((bf16[8,4,272,128]{3,2,1,0:T(8,128)(2,1)}), bf16[8,4,272,128]{3,2,1,0:T(8,128)(2,1)S(1)}, u32[]{:S(2)}, u32[]{:S(2)}) async-start(bf16[8,4,272,128]{3,2,1,0:T(8,128)(2,1)} %bitcast.68), calls=%async_computation.4 | async-start | bytes 4456448 | tf_op jit(solution)/shard_map/all_to_all | solution.py:278
  152.7 4.6 %convolution_convert_fusion = bf16[64,4,512]{2,1,0:T(4,128)(2,1)S(1)} fusion(bf16[64,128,512]{2,1,0:T(8,128)(2,1)} %upk_hbm.3, bf16[4,1,8192]{2,0,1:T(4,128)(2,1)S(1)} %copy-done.2), kind=kOutput, calls=%fused_computation.4 | convolution fusion | flops 33685504 | bytes 8716288 | tf_op jit(solution)/shard_map/shn,hnl->hsl/dot_general | solution.py:210
  157.7 0.9 slice_convert_fusion.1
  158.8 7.9 %all-to-all-done.4 = bf16[8,4,272,128]{3,2,1,0:T(8,128)(2,1)S(1)} async-done(((bf16[8,4,272,128]{3,2,1,0:T(8,128)(2,1)}), bf16[8,4,272,128]{3,2,1,0:T(8,128)(2,1)S(1)}, u32[]{:S(2)}, u32[]{:S(2)}) %all-to-all-start.4) | async-done | bytes 2228256 | tf_op jit(solution)/shard_map/all_to_all | solution.py:278
  167.1 3.2 %multiply_reduce_fusion.1 = bf16[4,256,128]{2,1,0:T(8,128)(2,1)S(1)} fusion(bf16[8,4,272,128]{3,2,1,0:T(8,128)(2,1)} %all-to-all-done.3, f32[8,4,256]{2,1,0:T(4,128)S(1)} %bitcast.80), kind=kLoop, calls=%fused_computation.1 | loop fusion | flops 3014656 | bytes 2392064 | tf_op jit(solution)/shard_map/reduce_sum | solution.py:300
  170.3 0.3 concatenate.20
  170.6 1.3 multiply_reduce_fusion
  171.9 0.3 concatenate.21
  172.2 0.8 pad_maximum_fusion
  173.0 13.3 %all-to-all-start.5 = ((bf16[8,272,128]{2,1,0:T(8,128)(2,1)}), bf16[8,272,128]{2,1,0:T(8,128)(2,1)S(1)}, u32[]{:S(2)}, u32[]{:S(2)}) async-start(bf16[8,272,128]{2,1,0:T(8,128)(2,1)} %pad_maximum_fusion), calls=%async_computation.5 | async-start | bytes 1114112 | tf_op jit(solution)/shard_map/all_to_all | solution.py:278
  186.6 0.3 fusion
  187.0 11.3 %all-to-all-done.5 = bf16[8,272,128]{2,1,0:T(8,128)(2,1)S(1)} async-done(((bf16[8,272,128]{2,1,0:T(8,128)(2,1)}), bf16[8,272,128]{2,1,0:T(8,128)(2,1)S(1)}, u32[]{:S(2)}, u32[]{:S(2)}) %all-to-all-start.5) | async-done | bytes 557088 | tf_op jit(solution)/shard_map/all_to_all | solution.py:278
  198.9 0.3 multiply_reduce_fusion.2
  199.2 5.3 %fusion.3 = bf16[4,1,8192]{2,0,1:T(4,128)(2,1)} fusion(f32[64,4,128]{2,1,0:T(4,128)S(1)} %bitcast.73, bf16[64,512,128]{2,1,0:T(8,128)(2,1)} %upv_hbm.3, bf16[64,4,512]{2,0,1:T(8,128)(2,1)S(1)} %fusion, f32[64,4]{1,0:T(8,128)S(1)} %copy.66), kind=kOutput, calls=%fused_computation.8 | convolution fusion | flops 33652736 | bytes 8848384 | tf_op jit(solution)/shard_map/hsl,hlv->hsv/dot_general | solution.py:227
  (78 shorter events, 3.5 us)
Async XLA Ops:
  0.0 157.3 %copy-start = (bf16[4,1,512]{2,0,1:T(4,128)(2,1)S(1)}, bf16[4,1,512]{2,0,1:T(4,128)(2,1)}, u32[]{:S(2)}) copy-start(bf16[4,1,512]{2,0,1:T(4,128)(2,1)} %param.16) | copy-start | bytes 12292
  61.5 10.8 %copy-start.1 = (bf16[96,4096]{1,0:T(8,128)(2,1)S(1)}, bf16[96,4096]{1,0:T(8,128)(2,1)}, u32[]{:S(2)}) copy-start(bf16[96,4096]{1,0:T(8,128)(2,1)} %param.15) | copy-start | bytes 2359300
  61.5 44.1 %all-to-all-start.2 = ((bf16[8,4,400,128]{3,2,1,0:T(8,128)(2,1)}), bf16[8,4,400,128]{3,2,1,0:T(8,128)(2,1)}, u32[]{:S(2)}, u32[]{:S(2)}) async-start(bf16[8,4,400,128]{3,2,1,0:T(8,128)(2,1)} %broadcast_in_dim.89), calls=%async_computation.2 | async-start | bytes 6553600 | tf_op jit(solution)/shard_map/all_to_all | solution.py:278
  105.6 38.7 %all-to-all-start.3 = ((bf16[8,4,272,128]{3,2,1,0:T(8,128)(2,1)}), bf16[8,4,272,128]{3,2,1,0:T(8,128)(2,1)}, u32[]{:S(2)}, u32[]{:S(2)}) async-start(bf16[8,4,272,128]{3,2,1,0:T(8,128)(2,1)} %bitcast.69), calls=%async_computation.3 | async-start | bytes 4456448 | tf_op jit(solution)/shard_map/all_to_all | solution.py:278
  144.2 8.4 %copy-start.3 = (bf16[1,256]{1,0:T(2,128)(2,1)S(1)}, bf16[1,256]{1,0:T(2,128)(2,1)}, u32[]{:S(2)}) copy-start(bf16[1,256]{1,0:T(2,128)(2,1)} %param.17) | copy-start | bytes 1540
  144.2 8.5 %copy-start.2 = (bf16[4,1,8192]{2,0,1:T(4,128)(2,1)S(1)}, bf16[4,1,8192]{2,0,1:T(4,128)(2,1)}, u32[]{:S(2)}) copy-start(bf16[4,1,8192]{2,0,1:T(4,128)(2,1)} %param.10) | copy-start | bytes 196612
  144.2 22.4 %all-to-all-start.4 = ((bf16[8,4,272,128]{3,2,1,0:T(8,128)(2,1)}), bf16[8,4,272,128]{3,2,1,0:T(8,128)(2,1)S(1)}, u32[]{:S(2)}, u32[]{:S(2)}) async-start(bf16[8,4,272,128]{3,2,1,0:T(8,128)(2,1)} %bitcast.68), calls=%async_computation.4 | async-start | bytes 4456448 | tf_op jit(solution)/shard_map/all_to_all | solution.py:278
  173.0 25.2 %all-to-all-start.5 = ((bf16[8,272,128]{2,1,0:T(8,128)(2,1)}), bf16[8,272,128]{2,1,0:T(8,128)(2,1)S(1)}, u32[]{:S(2)}, u32[]{:S(2)}) async-start(bf16[8,272,128]{2,1,0:T(8,128)(2,1)} %pad_maximum_fusion), calls=%async_computation.5 | async-start | bytes 1114112 | tf_op jit(solution)/shard_map/all_to_all | solution.py:278

commit v5 on v4

--- a/solution.py
+++ b/solution.py
@@ -71,7 +71,7 @@
             q_rope = jnp.concatenate([packed[:, :half], packed[:, half:]], axis=0)
             bias = jnp.where(token < counts[i] * page, 0.0, NEG)
             scores = lax.dot_general(held[r], keys[i, 0:tokens, :], NT, preferred_element_type=jnp.float32)
-            scores += lax.dot_general(q_rope, rotated[i, 0:tokens, :], NT, preferred_element_type=jnp.float32)
+            scores += lax.dot_general(q_rope, rotated[i, 0:tokens, :half], NT, preferred_element_type=jnp.float32)
             all_scores.append(scores + bias)
         for i in range(PER):
             r = at * PER + i
@@ -343,8 +343,10 @@
     length = queries + queries // 2
 
     near = spread(own, sublattice)
-    count = near.shape[0] // HALVES
+    count = 8 // HALVES
     pool_rope = pool_rope.reshape(slots_total, page, rope)
+    pool_rope = jnp.pad(pool_rope, ((0, 0), (0, 0), (0, 128 - rope)))
+    near, pool_rope = lax.optimization_barrier((near, pool_rope))
     me = lax.axis_index("batch")
     gathered = [
         spread(near[k * count : (k + 1) * count], block) for k in range(HALVES)
@@ -362,11 +364,15 @@
         if k + 1 < HALVES:
             parts, gathered[k + 1] = lax.optimization_barrier((parts, gathered[k + 1]))
         parts = exchange(parts.reshape(8, count, queries + 16, value), block)
-        returned.append(pack(*mix(parts, queries)))
-    rows = exchange(jnp.concatenate(returned, axis=0), sublattice)
+        returned.append(parts)
+    mixed = pack(*mix(returned[0], queries))
+    mixed, second = lax.optimization_barrier((mixed, returned[1]))
+    rows = jnp.concatenate([mixed, pack(*mix(second, queries))], axis=0)
+    rows = exchange(rows, sublattice)
     fresh = (fresh[0].reshape(1, queries, value), fresh[1].reshape(1, queries))
     out, _ = mix(rows[:, None], queries, fresh)
-    out = out.astype(jnp.bfloat16).reshape(heads, steps, value).transpose(1, 0, 2)
+    out = lax.optimization_barrier(out.astype(jnp.bfloat16))
+    out = out.reshape(heads, steps, value).transpose(1, 0, 2)
     return out.reshape(steps, 1, heads * value)
 
 

time: 205 us -> 200 us (0.976)
  blocking collectives: 54.2 us -> 27.4 us
  starting transfers between devices: 40.6 us -> 54.5 us
  waiting for transfers between devices: 19.2 us -> 28.7 us
  Pallas kernels: 58.4 us -> 55.1 us
  local copies, waits for them, and re-layouts: 10.9 us -> 13.6 us
    all_to_all x2 -> x1, blocking collectives: 54.2 us -> 27.4 us  [exchange(): lax.all_to_all(x, ('batch', 'head'), split_axis=0, concat_axis=0, tiled=T...]
    all_to_all x4 -> x5, starting transfers between devices: 40.6 us -> 54.5 us  [exchange(): lax.all_to_all(x, ('batch', 'head'), split_axis=0, concat_axis=0, tiled=T...]
    all_to_all x4 -> x5, waiting for transfers between devices: 19.2 us -> 28.7 us  [exchange(): lax.all_to_all(x, ('batch', 'head'), split_axis=0, concat_axis=0, tiled=T...]
    pallas_call x2, Pallas kernels: 58.4 us -> 55.1 us  [attention(): pl.pallas_call(functools.partial(body, scale), out_shape=jax.ShapeDtypeSt...]
  transfers between devices with their start and end apart: 4 -> 5, of which waited for: 2 -> 3; matrix products, arithmetic and copies ran while one was open for 6% -> 10% of each run, Pallas kernels for 29% -> 28%
where the time goes in v5:
time: 200 us
  Pallas kernels  55.1 us (28%)
  starting transfers between devices  54.5 us (27%)
  waiting for transfers between devices  28.7 us (14%)
  blocking collectives  27.4 us (14%)
  local copies, waits for them, and re-layouts  13.6 us (7%)
  other arithmetic  10.3 us (5%)
  matrix products  9.93 us (5%)
    pallas_call x2, Pallas kernels, attention(): pl.pallas_call(functools.partial(body, scale), out_shape=jax.ShapeDtypeSt...  55.1 us
    all_to_all x5, starting transfers between devices, exchange(): lax.all_to_all(x, ('batch', 'head'), split_axis=0, concat_axis=0, tiled=T...  54.5 us
    all_to_all x5, waiting for transfers between devices, exchange(): lax.all_to_all(x, ('batch', 'head'), split_axis=0, concat_axis=0, tiled=T...  28.7 us
    all_to_all x1, blocking collectives, exchange(): lax.all_to_all(x, ('batch', 'head'), split_axis=0, concat_axis=0, tiled=T...  27.4 us
    reduce_sum x3, other arithmetic, mix(): jnp.sum(parts[:, :, :queries].astype(jnp.float32) * (share / total)[...,...  4.86 us
    dot_general x1, matrix products, fresh_part(): jnp.einsum('hsl,hlv->hsv', mixed, up_value, preferred_element_type=jnp.fl...  4.62 us
    dot_general x1, matrix products, fresh_part(): jnp.einsum('shn,hnl->hsl', q_nope, up_key, preferred_element_type=jnp.flo...  4.57 us
  transfers between devices with their start and end apart: 5, of which 3 were waited for; matrix products, arithmetic and copies ran while one was open for 10% of the time, Pallas kernels for 28%

profile of v5, /device:TPU:1, one launch (start us, length us, event | category | flops | bytes accessed | tf_op | source)
XLA Modules:
  0.0 199.9 jit_solution(228122810558970534)
XLA Ops:
  0.0 0.8 reduce.6
  1.2 0.7 reduce.7
  2.5 0.9 reshape.367
  3.7 0.9 fusion.12
  4.5 1.0 broadcast_in_dim.87
  5.5 10.8 %all-to-all-start = ((bf16[8,400,128]{2,1,0:T(8,128)(2,1)}), bf16[8,400,128]{2,1,0:T(8,128)(2,1)}, u32[]{:S(2)}, u32[]{:S(2)}) async-start(bf16[8,400,128]{2,1,0:T(8,128)(2,1)} %broadcast_in_dim.87), calls=%async_computation | async-start | bytes 1638400 | tf_op jit(solution)/shard_map/all_to_all | solution.py:278
  16.3 0.7 copy.50
  17.0 2.4 %copy.51 = bf16[96,64,64]{2,1,0:T(8,128)(2,1)S(1)} copy(bf16[96,64,64]{0,2,1:T(8,128)(2,1)S(1)} %bitcast.73) | data formatting | bytes 1572864 | tf_op jit(solution)/shard_map/reshape | solution.py:347
  19.4 0.5 pad.9.keyrope_hbm
  19.8 12.9 %all-to-all-done = bf16[8,400,128]{2,1,0:T(8,128)(2,1)} async-done(((bf16[8,400,128]{2,1,0:T(8,128)(2,1)}), bf16[8,400,128]{2,1,0:T(8,128)(2,1)}, u32[]{:S(2)}, u32[]{:S(2)}) %all-to-all-start) | async-done | bytes 819232 | tf_op jit(solution)/shard_map/all_to_all | solution.py:278
  32.7 1.2 fusion.35
  33.9 0.4 broadcast_in_dim.88
  34.3 27.4 %all_to_all.30 = bf16[8,4,400,128]{3,2,1,0:T(8,128)(2,1)} all-to-all(bf16[8,4,400,128]{3,2,1,0:T(8,128)(2,1)S(1)} %broadcast_in_dim.88), channel_id=1, replica_groups={{0,2,8,10,32,34,40,42},{4,6,12,14,36,38,44,46},{16,18,24,26,48,50,56,58..., dimensions={0} | all-to-all | bytes 6553600 | tf_op jit(solution)/shard_map/all_to_all | solution.py:278
  61.7 2.1 %broadcast_in_dim.89 = bf16[8,4,400,128]{3,2,1,0:T(8,128)(2,1)} broadcast(bf16[4,400,128]{2,1,0:T(8,128)(2,1)S(1)} %get-tuple-element.17), dimensions={1,2,3} | broadcast | bytes 3686400 | tf_op jit(solution)/shard_map/broadcast_in_dim | solution.py:284
  63.8 10.8 %all-to-all-start.2 = ((bf16[8,4,400,128]{3,2,1,0:T(8,128)(2,1)}), bf16[8,4,400,128]{3,2,1,0:T(8,128)(2,1)}, u32[]{:S(2)}, u32[]{:S(2)}) async-start(bf16[8,4,400,128]{3,2,1,0:T(8,128)(2,1)} %broadcast_in_dim.89), calls=%async_computation.2 | async-start | bytes 6553600 | tf_op jit(solution)/shard_map/all_to_all | solution.py:278
  74.7 0.8 slice.40
  75.9 27.7 %attention.2 = bf16[32,272,128]{2,1,0:T(8,128)(2,1)} custom-call(s32[32,16]{1,0:T(8,128)S(1)} %bitcast_convert_fusion.1.lists_ref, bf16[32,400,128]{2,1,0:T(8,128)(2,1)} %bitcast.75, bf16[64,128,512]{2,1,0:T(8,128)(2,1)} %upk_hbm.3, bf16[96,64,512]{2,1,0:T(8,128)(2,1)} %lat_hbm.3, bf16[96,64,128]{2,1,0:T(8,128)(2,1)S(1)} %pad.9.keyrope_hbm, ...), custom_call_target="tpu_custom_call" | custom-call | flops 10737418240 | bytes 134217728 | tf_op jit(solution)/shard_map/attention/pallas_call | solution.py:179
  103.6 14.5 %all-to-all-start.3 = ((bf16[8,4,272,128]{3,2,1,0:T(8,128)(2,1)}), bf16[8,4,272,128]{3,2,1,0:T(8,128)(2,1)}, u32[]{:S(2)}, u32[]{:S(2)}) async-start(bf16[8,4,272,128]{3,2,1,0:T(8,128)(2,1)} %bitcast.77), calls=%async_computation.3 | async-start | bytes 4456448 | tf_op jit(solution)/shard_map/all_to_all | solution.py:278
  118.1 4.6 %convolution_convert_fusion = bf16[64,4,512]{2,1,0:T(4,128)(2,1)S(1)} fusion(bf16[64,128,512]{2,1,0:T(8,128)(2,1)} %upk_hbm.3, bf16[4,1,8192]{2,0,1:T(4,128)(2,1)S(1)} %copy-done.2), kind=kOutput, calls=%fused_computation.4 | convolution fusion | flops 33685504 | bytes 8716288 | tf_op jit(solution)/shard_map/shn,hnl->hsl/dot_general | solution.py:210
  122.9 0.9 slice.43
  124.1 27.4 %attention.3 = bf16[32,272,128]{2,1,0:T(8,128)(2,1)} custom-call(s32[32,16]{1,0:T(8,128)S(1)} %bitcast_convert_fusion.lists_ref, bf16[32,400,128]{2,1,0:T(8,128)(2,1)} %bitcast.13.packed_hbm, bf16[64,128,512]{2,1,0:T(8,128)(2,1)} %upk_hbm.3, bf16[96,64,512]{2,1,0:T(8,128)(2,1)} %lat_hbm.3, bf16[96,64,128]{2,1,0:T(8,128)(2,1)S(1)} %pad.9.keyrope_hbm, ...), custom_call_target="tpu_custom_call" | custom-call | flops 10737418240 | bytes 134217728 | tf_op jit(solution)/shard_map/attention/pallas_call | solution.py:179
  151.5 14.9 %all-to-all-start.4 = ((bf16[8,4,272,128]{3,2,1,0:T(8,128)(2,1)}), bf16[8,4,272,128]{3,2,1,0:T(8,128)(2,1)S(1)}, u32[]{:S(2)}, u32[]{:S(2)}) async-start(bf16[8,4,272,128]{3,2,1,0:T(8,128)(2,1)} %bitcast.76), calls=%async_computation.4 | async-start | bytes 4456448 | tf_op jit(solution)/shard_map/all_to_all | solution.py:278
  166.9 0.3 fusion
  167.2 0.9 slice_convert_fusion
  168.4 3.2 %multiply_reduce_fusion.1 = bf16[4,256,128]{2,1,0:T(8,128)(2,1)S(1)} fusion(bf16[8,4,272,128]{3,2,1,0:T(8,128)(2,1)} %all-to-all-done.3, f32[8,4,256]{2,1,0:T(4,128)S(1)} %bitcast.89), kind=kLoop, calls=%fused_computation.1 | loop fusion | flops 3014656 | bytes 2392064 | tf_op jit(solution)/shard_map/reduce_sum | solution.py:300
  171.9 8.6 %all-to-all-done.4 = bf16[8,4,272,128]{3,2,1,0:T(8,128)(2,1)S(1)} async-done(((bf16[8,4,272,128]{3,2,1,0:T(8,128)(2,1)}), bf16[8,4,272,128]{3,2,1,0:T(8,128)(2,1)S(1)}, u32[]{:S(2)}, u32[]{:S(2)}) %all-to-all-start.4) | async-done | bytes 2228256 | tf_op jit(solution)/shard_map/all_to_all | solution.py:278
  180.8 1.3 multiply_reduce_fusion
  182.4 0.8 pad_maximum_fusion
  183.2 3.5 %all-to-all-start.5 = ((bf16[8,272,128]{2,1,0:T(8,128)(2,1)}), bf16[8,272,128]{2,1,0:T(8,128)(2,1)S(1)}, u32[]{:S(2)}, u32[]{:S(2)}) async-start(bf16[8,272,128]{2,1,0:T(8,128)(2,1)} %pad_maximum_fusion), calls=%async_computation.5 | async-start | bytes 1114112 | tf_op jit(solution)/shard_map/all_to_all | solution.py:278
  186.8 4.6 %fusion.5 = f32[64,4,128]{2,1,0:T(4,128)S(1)} fusion(bf16[64,512,128]{2,1,0:T(8,128)(2,1)} %upv_hbm.3, bf16[64,4,512]{2,0,1:T(8,128)(2,1)S(1)} %fusion), kind=kOutput, calls=%fused_computation.15 | convolution fusion | flops 33554432 | bytes 8781824 | tf_op jit(solution)/shard_map/hsl,hlv->hsv/dot_general | solution.py:227
  191.4 7.2 %all-to-all-done.5 = bf16[8,272,128]{2,1,0:T(8,128)(2,1)S(1)} async-done(((bf16[8,272,128]{2,1,0:T(8,128)(2,1)}), bf16[8,272,128]{2,1,0:T(8,128)(2,1)S(1)}, u32[]{:S(2)}, u32[]{:S(2)}) %all-to-all-start.5) | async-done | bytes 557088 | tf_op jit(solution)/shard_map/all_to_all | solution.py:278
  199.2 0.7 reshape.386
  (77 shorter events, 4.4 us)
Async XLA Ops:
  0.0 122.7 %copy-start = (bf16[4,1,512]{2,0,1:T(4,128)(2,1)S(1)}, bf16[4,1,512]{2,0,1:T(4,128)(2,1)}, u32[]{:S(2)}) copy-start(bf16[4,1,512]{2,0,1:T(4,128)(2,1)} %param.16) | copy-start | bytes 12292
  0.0 16.3 %copy-start.1 = (bf16[96,4096]{1,0:T(8,128)(2,1)S(1)}, bf16[96,4096]{1,0:T(8,128)(2,1)}, u32[]{:S(2)}) copy-start(bf16[96,4096]{1,0:T(8,128)(2,1)} %param.15) | copy-start | bytes 2359300
  5.5 27.1 %all-to-all-start = ((bf16[8,400,128]{2,1,0:T(8,128)(2,1)}), bf16[8,400,128]{2,1,0:T(8,128)(2,1)}, u32[]{:S(2)}, u32[]{:S(2)}) async-start(bf16[8,400,128]{2,1,0:T(8,128)(2,1)} %broadcast_in_dim.87), calls=%async_computation | async-start | bytes 1638400 | tf_op jit(solution)/shard_map/all_to_all | solution.py:278
  63.8 10.8 %copy-start.3 = (bf16[1,256]{1,0:T(2,128)(2,1)S(1)}, bf16[1,256]{1,0:T(2,128)(2,1)}, u32[]{:S(2)}) copy-start(bf16[1,256]{1,0:T(2,128)(2,1)} %param.17) | copy-start | bytes 1540
  63.8 39.8 %all-to-all-start.2 = ((bf16[8,4,400,128]{3,2,1,0:T(8,128)(2,1)}), bf16[8,4,400,128]{3,2,1,0:T(8,128)(2,1)}, u32[]{:S(2)}, u32[]{:S(2)}) async-start(bf16[8,4,400,128]{3,2,1,0:T(8,128)(2,1)} %broadcast_in_dim.89), calls=%async_computation.2 | async-start | bytes 6553600 | tf_op jit(solution)/shard_map/all_to_all | solution.py:278
  103.6 14.6 %copy-start.2 = (bf16[4,1,8192]{2,0,1:T(4,128)(2,1)S(1)}, bf16[4,1,8192]{2,0,1:T(4,128)(2,1)}, u32[]{:S(2)}) copy-start(bf16[4,1,8192]{2,0,1:T(4,128)(2,1)} %param.10) | copy-start | bytes 196612
  103.6 47.9 %all-to-all-start.3 = ((bf16[8,4,272,128]{3,2,1,0:T(8,128)(2,1)}), bf16[8,4,272,128]{3,2,1,0:T(8,128)(2,1)}, u32[]{:S(2)}, u32[]{:S(2)}) async-start(bf16[8,4,272,128]{3,2,1,0:T(8,128)(2,1)} %bitcast.77), calls=%async_computation.3 | async-start | bytes 4456448 | tf_op jit(solution)/shard_map/all_to_all | solution.py:278
  151.5 29.0 %all-to-all-start.4 = ((bf16[8,4,272,128]{3,2,1,0:T(8,128)(2,1)}), bf16[8,4,272,128]{3,2,1,0:T(8,128)(2,1)S(1)}, u32[]{:S(2)}, u32[]{:S(2)}) async-start(bf16[8,4,272,128]{3,2,1,0:T(8,128)(2,1)} %bitcast.76), calls=%async_computation.4 | async-start | bytes 4456448 | tf_op jit(solution)/shard_map/all_to_all | solution.py:278
  183.2 15.4 %all-to-all-start.5 = ((bf16[8,272,128]{2,1,0:T(8,128)(2,1)}), bf16[8,272,128]{2,1,0:T(8,128)(2,1)S(1)}, u32[]{:S(2)}, u32[]{:S(2)}) async-start(bf16[8,272,128]{2,1,0:T(8,128)(2,1)} %pad_maximum_fusion), calls=%async_computation.5 | async-start | bytes 1114112 | tf_op jit(solution)/shard_map/all_to_all | solution.py:278

commit v6 on v5

--- a/solution.py
+++ b/solution.py
@@ -10,8 +10,8 @@
 
 MAX_PAGES = 10
 NEG = -1e30
-VMEM_BYTES = 52 * 1024 * 1024
-PER = 2
+VMEM_BYTES = 54 * 1024 * 1024
+PER = 4
 PIECES = 4
 NT = (((1,), (1,)), ((), ()))
 
@@ -130,22 +130,22 @@
         piece(upk_hbm, upk, key_sems, k).start()
     load_lat.start()
     load_rope.start()
-    for k in range(PIECES):
-        piece(upv_hbm, upv, value_sems, k).start()
     tops[...] = jnp.zeros_like(tops)
     totals[...] = jnp.ones_like(totals)
     load_packed.wait()
 
-    def absorb(at, _):
-        @pl.when(at % (groups // PIECES) == 0)
-        def _():
-            piece(upk_hbm, upk, key_sems, at // (groups // PIECES)).wait()
-        absorb_step(at, packed, upk, held)
+    def absorb(k, _):
+        piece(upk_hbm, upk, key_sems, k).wait()
+        for j in range(groups // PIECES):
+            absorb_step(k * (groups // PIECES) + j, packed, upk, held)
         return 0
-    lax.fori_loop(0, groups, absorb, 0)
+
+    lax.fori_loop(0, PIECES, absorb, 0)
 
     load_lat.wait()
     load_rope.wait()
+    for k in range(PIECES):
+        piece(upv_hbm, upv, value_sems, k).start()
 
     def attend(at, _):
         attend_step(scale, at, lists_ref, packed, lat, keyrope, held, keys, rotated, tops, totals)
@@ -154,14 +154,16 @@
 
     share_step(scale, tops, totals, packed)
     out_copy(groups).start()
-    def project(at, _):
-        @pl.when(at % (groups // PIECES) == 0)
-        def _():
-            piece(upv_hbm, upv, value_sems, at // (groups // PIECES)).wait()
-        project_step(at, held, upv, packed)
-        out_copy(at).start()
+    def project(k, _):
+        piece(upv_hbm, upv, value_sems, k).wait()
+        for j in range(groups // PIECES):
+            at = k * (groups // PIECES) + j
+            project_step(at, held, upv, packed)
+            out_copy(at).start()
         return 0
-    lax.fori_loop(0, groups, project, 0)
+
+    lax.fori_loop(0, PIECES, project, 0)
+
     def drain(at, _):
         out_copy(at).wait()
         return 0
@@ -204,6 +206,7 @@
         name="attention",
     )(lists, packed, up_key, pool_latent, pool_rope, up_value)
 
+
 def fresh_part(q_nope, q_rope, up_key, up_value, new_latent, new_rope, scale):
     steps, heads, _ = q_nope.shape
     latent = up_key.shape[2]
@@ -346,14 +349,14 @@
     count = 8 // HALVES
     pool_rope = pool_rope.reshape(slots_total, page, rope)
     pool_rope = jnp.pad(pool_rope, ((0, 0), (0, 0), (0, 128 - rope)))
-    near, pool_rope = lax.optimization_barrier((near, pool_rope))
+    fresh = fresh_part(
+        q_nope, q_rope, up_key, up_value, new_latent[:, 0], new_rope.reshape(steps, rope), scale
+    )
+    near, pool_rope, fresh = lax.optimization_barrier((near, pool_rope, fresh))
     me = lax.axis_index("batch")
     gathered = [
         spread(near[k * count : (k + 1) * count], block) for k in range(HALVES)
     ]
-    fresh = fresh_part(
-        q_nope, q_rope, up_key, up_value, new_latent[:, 0], new_rope.reshape(steps, rope), scale
-    )
     returned = []
     for k in range(HALVES):
         packed = gathered[k].reshape(8 * count, own.shape[0], nope)

time: 200 us -> 195 us (0.975)
  Pallas kernels: 55.1 us -> 44.5 us
  waiting for transfers between devices: 28.7 us -> 21.6 us
  local copies, waits for them, and re-layouts: 13.6 us -> 18.2 us
  blocking collectives: 27.4 us -> 29.7 us
  starting transfers between devices: 54.5 us -> 56.5 us
    pallas_call x2, Pallas kernels: 55.1 us -> 44.5 us  [attention(): pl.pallas_call(functools.partial(body, scale), out_shape=jax.ShapeDtypeSt...]
    all_to_all x5, waiting for transfers between devices: 28.7 us -> 21.6 us  [exchange(): lax.all_to_all(x, ('batch', 'head'), split_axis=0, concat_axis=0, tiled=T...]
    unnamed x15 -> x23, local copies, waits for them, and re-layouts: 0.86 us -> 3.92 us
    all_to_all x1, blocking collectives: 27.4 us -> 29.7 us  [exchange(): lax.all_to_all(x, ('batch', 'head'), split_axis=0, concat_axis=0, tiled=T...]
  transfers between devices with their start and end apart: 5 -> 5, of which waited for: 3 -> 2; matrix products, arithmetic and copies ran while one was open for 10% -> 13% of each run, Pallas kernels for 28% -> 23%
where the time goes in v6:
time: 195 us; the launch traced here: 194 us
  starting transfers between devices  56.5 us (29%)
  Pallas kernels  44.5 us (23%)
  blocking collectives  29.7 us (15%)
  waiting for transfers between devices  21.6 us (11%)
  local copies, waits for them, and re-layouts  18.2 us (9%)
  other arithmetic  11.5 us (6%)
  matrix products  11.4 us (6%)
    all_to_all x5, starting transfers between devices, exchange(): lax.all_to_all(x, ('batch', 'head'), split_axis=0, concat_axis=0, tiled=T...  56.5 us
    pallas_call x2, Pallas kernels, attention(): pl.pallas_call(functools.partial(body, scale), out_shape=jax.ShapeDtypeSt...  44.5 us
    all_to_all x1, blocking collectives, exchange(): lax.all_to_all(x, ('batch', 'head'), split_axis=0, concat_axis=0, tiled=T...  29.7 us
    all_to_all x5, waiting for transfers between devices, exchange(): lax.all_to_all(x, ('batch', 'head'), split_axis=0, concat_axis=0, tiled=T...  21.6 us
    dot_general x1, matrix products, fresh_part(): jnp.einsum('hsl,hlv->hsv', mixed, up_value, preferred_element_type=jnp.fl...  5.28 us
    reduce_sum x3, other arithmetic, mix(): jnp.sum(parts[:, :, :queries].astype(jnp.float32) * (share / total)[...,...  4.86 us
    dot_general x1, matrix products, fresh_part(): jnp.einsum('shn,hnl->hsl', q_nope, up_key, preferred_element_type=jnp.flo...  4.65 us
    unnamed x23, local copies, waits for them, and re-layouts  3.92 us
  transfers between devices with their start and end apart: 5, of which 2 were waited for; matrix products, arithmetic and copies ran while one was open for 13% of the time, Pallas kernels for 23%

profile of v6, /device:TPU:1, one launch (start us, length us, event | category | flops | bytes accessed | tf_op | source)
XLA Modules:
  0.0 193.8 jit_solution(14717788006701229789)
XLA Ops:
  0.0 0.7 reduce.6
  1.1 0.9 reshape.348
  2.0 0.7 reduce.7
  3.6 0.9 fusion.12
  4.5 1.0 broadcast_in_dim.87
  5.5 10.8 %all-to-all-start = ((bf16[8,400,128]{2,1,0:T(8,128)(2,1)}), bf16[8,400,128]{2,1,0:T(8,128)(2,1)S(1)}, u32[]{:S(2)}, u32[]{:S(2)}) async-start(bf16[8,400,128]{2,1,0:T(8,128)(2,1)} %broadcast_in_dim.87), calls=%async_computation | async-start | bytes 1638400 | tf_op jit(solution)/shard_map/all_to_all | solution.py:281
  16.3 4.6 %convolution_convert_fusion = bf16[64,4,512]{2,1,0:T(4,128)(2,1)S(1)} fusion(bf16[64,128,512]{2,1,0:T(8,128)(2,1)} %upk_hbm.3, bf16[4,1,8192]{2,0,1:T(4,128)(2,1)S(1)} %copy-done.6), kind=kOutput, calls=%fused_computation.4 | convolution fusion | flops 33685504 | bytes 8716288 | tf_op jit(solution)/shard_map/shn,hnl->hsl/dot_general | solution.py:213
  21.6 1.1 fusion
  22.7 0.6 copy.50
  23.3 2.4 %copy.51 = bf16[96,64,64]{2,1,0:T(8,128)(2,1)S(1)} copy(bf16[96,64,64]{0,2,1:T(8,128)(2,1)S(1)} %bitcast.73) | data formatting | bytes 1572864 | tf_op jit(solution)/shard_map/reshape | solution.py:350
  25.7 1.7 pad.9.keyrope_hbm
  27.4 5.3 %fusion.5 = f32[64,4,128]{2,1,0:T(4,128)} fusion(bf16[64,512,128]{2,1,0:T(8,128)(2,1)} %upv_hbm.3, bf16[64,4,512]{2,0,1:T(8,128)(2,1)S(1)} %copy-done.4), kind=kOutput, calls=%fused_computation.15 | convolution fusion | flops 33554432 | bytes 8781824 | tf_op jit(solution)/shard_map/hsl,hlv->hsv/dot_general | solution.py:230
  33.2 29.7 %all_to_all.30 = bf16[8,4,400,128]{3,2,1,0:T(8,128)(2,1)} all-to-all(bf16[8,4,400,128]{3,2,1,0:T(8,128)(2,1)S(1)} %broadcast_in_dim.91), channel_id=1, replica_groups={{0,2,8,10,32,34,40,42},{4,6,12,14,36,38,44,46},{16,18,24,26,48,50,56,58..., dimensions={0} | all-to-all | bytes 6553600 | tf_op jit(solution)/shard_map/all_to_all | solution.py:281
  62.9 2.1 %broadcast_in_dim.92 = bf16[8,4,400,128]{3,2,1,0:T(8,128)(2,1)} broadcast(bf16[4,400,128]{2,1,0:T(8,128)(2,1)S(1)} %get-tuple-element.21), dimensions={1,2,3} | broadcast | bytes 3686400 | tf_op jit(solution)/shard_map/broadcast_in_dim | solution.py:287
  65.0 10.2 %all-to-all-start.2 = ((bf16[8,4,400,128]{3,2,1,0:T(8,128)(2,1)}), bf16[8,4,400,128]{3,2,1,0:T(8,128)(2,1)S(1)}, u32[]{:S(2)}, u32[]{:S(2)}) async-start(bf16[8,4,400,128]{3,2,1,0:T(8,128)(2,1)} %broadcast_in_dim.92), calls=%async_computation.2 | async-start | bytes 6553600 | tf_op jit(solution)/shard_map/all_to_all | solution.py:281
  75.2 1.5 slice.40
  76.6 1.0 copy.55
  78.4 21.9 %attention.2 = bf16[32,272,128]{2,1,0:T(8,128)(2,1)} custom-call(s32[32,16]{1,0:T(8,128)} %bitcast_convert_fusion.1.lists_ref, bf16[32,400,128]{2,1,0:T(8,128)(2,1)} %bitcast.77, bf16[64,128,512]{2,1,0:T(8,128)(2,1)} %upk_hbm.3, bf16[96,64,512]{2,1,0:T(8,128)(2,1)} %lat_hbm.3, bf16[96,64,128]{2,1,0:T(8,128)(2,1)} %pad.9.keyrope_hbm, ...), custom_call_target="tpu_custom_call" | custom-call | flops 10737418240 | bytes 134217728 | tf_op jit(solution)/shard_map/attention/pallas_call | solution.py:181
  100.3 1.7 copy-done.2
  102.0 9.0 %all-to-all-start.3 = ((bf16[8,4,272,128]{3,2,1,0:T(8,128)(2,1)}), bf16[8,4,272,128]{3,2,1,0:T(8,128)(2,1)S(1)}, u32[]{:S(2)}, u32[]{:S(2)}) async-start(bf16[8,4,272,128]{3,2,1,0:T(8,128)(2,1)} %bitcast.79), calls=%async_computation.3 | async-start | bytes 4456448 | tf_op jit(solution)/shard_map/all_to_all | solution.py:281
  111.0 0.8 slice.43
  112.8 22.6 %attention.3 = bf16[32,272,128]{2,1,0:T(8,128)(2,1)} custom-call(s32[32,16]{1,0:T(8,128)} %bitcast_convert_fusion.lists_ref, bf16[32,400,128]{2,1,0:T(8,128)(2,1)} %bitcast.75, bf16[64,128,512]{2,1,0:T(8,128)(2,1)} %upk_hbm.3, bf16[96,64,512]{2,1,0:T(8,128)(2,1)} %lat_hbm.3, bf16[96,64,128]{2,1,0:T(8,128)(2,1)} %pad.9.keyrope_hbm, bf16[64,512,128]{2,1,0:T(8,128)(2,1)} %upv_hbm.3), custom_call_target="tpu_custom_call" | custom-call | flops 10737418240 | bytes 134217728 | tf_op jit(solution)/shard_map/attention/pallas_call | solution.py:181
  135.4 1.4 copy-done.1
  136.8 8.3 %all-to-all-start.4 = ((bf16[8,4,272,128]{3,2,1,0:T(8,128)(2,1)}), bf16[8,4,272,128]{3,2,1,0:T(8,128)(2,1)S(1)}, u32[]{:S(2)}, u32[]{:S(2)}) async-start(bf16[8,4,272,128]{3,2,1,0:T(8,128)(2,1)} %bitcast.78), calls=%async_computation.4 | async-start | bytes 4456448 | tf_op jit(solution)/shard_map/all_to_all | solution.py:281
  145.1 0.8 slice_convert_fusion
  146.2 3.2 %multiply_reduce_fusion.1 = bf16[4,256,128]{2,1,0:T(8,128)(2,1)S(1)} fusion(bf16[8,4,272,128]{3,2,1,0:T(8,128)(2,1)} %copy-done.1, f32[8,4,256]{2,1,0:T(4,128)S(1)} %bitcast.91), kind=kLoop, calls=%fused_computation.1 | loop fusion | flops 3014656 | bytes 2392064 | tf_op jit(solution)/shard_map/reduce_sum | solution.py:303
  149.8 9.4 %all-to-all-done.4 = bf16[8,4,272,128]{3,2,1,0:T(8,128)(2,1)S(1)} async-done(((bf16[8,4,272,128]{3,2,1,0:T(8,128)(2,1)}), bf16[8,4,272,128]{3,2,1,0:T(8,128)(2,1)S(1)}, u32[]{:S(2)}, u32[]{:S(2)}) %all-to-all-start.4) | async-done | bytes 2228256 | tf_op jit(solution)/shard_map/all_to_all | solution.py:281
  159.5 1.3 multiply_reduce_fusion
  161.1 0.8 pad_maximum_fusion
  162.0 18.2 %all-to-all-start.5 = ((bf16[8,272,128]{2,1,0:T(8,128)(2,1)}), bf16[8,272,128]{2,1,0:T(8,128)(2,1)S(1)}, u32[]{:S(2)}, u32[]{:S(2)}) async-start(bf16[8,272,128]{2,1,0:T(8,128)(2,1)} %pad_maximum_fusion), calls=%async_computation.5 | async-start | bytes 1114112 | tf_op jit(solution)/shard_map/all_to_all | solution.py:281
  180.4 12.2 %all-to-all-done.5 = bf16[8,272,128]{2,1,0:T(8,128)(2,1)S(1)} async-done(((bf16[8,272,128]{2,1,0:T(8,128)(2,1)}), bf16[8,272,128]{2,1,0:T(8,128)(2,1)S(1)}, u32[]{:S(2)}, u32[]{:S(2)}) %all-to-all-start.5) | async-done | bytes 557088 | tf_op jit(solution)/shard_map/all_to_all | solution.py:281
  193.2 0.7 reshape.368
  (85 shorter events, 5.9 us)
Async XLA Ops:
  0.0 21.1 %copy-start = (bf16[4,1,512]{2,0,1:T(4,128)(2,1)S(1)}, bf16[4,1,512]{2,0,1:T(4,128)(2,1)}, u32[]{:S(2)}) copy-start(bf16[4,1,512]{2,0,1:T(4,128)(2,1)} %param.16) | copy-start | bytes 12292
  0.0 16.3 %copy-start.6 = (bf16[4,1,8192]{2,0,1:T(4,128)(2,1)S(1)}, bf16[4,1,8192]{2,0,1:T(4,128)(2,1)}, u32[]{:S(2)}) copy-start(bf16[4,1,8192]{2,0,1:T(4,128)(2,1)} %param.10) | copy-start | bytes 196612
  5.5 27.2 %all-to-all-start = ((bf16[8,400,128]{2,1,0:T(8,128)(2,1)}), bf16[8,400,128]{2,1,0:T(8,128)(2,1)S(1)}, u32[]{:S(2)}, u32[]{:S(2)}) async-start(bf16[8,400,128]{2,1,0:T(8,128)(2,1)} %broadcast_in_dim.87), calls=%async_computation | async-start | bytes 1638400 | tf_op jit(solution)/shard_map/all_to_all | solution.py:281
  16.3 4.7 %copy-start.7 = (bf16[1,256]{1,0:T(2,128)(2,1)S(1)}, bf16[1,256]{1,0:T(2,128)(2,1)}, u32[]{:S(2)}) copy-start(bf16[1,256]{1,0:T(2,128)(2,1)} %param.17) | copy-start | bytes 1540
  16.3 6.3 %copy-start.5 = (bf16[96,4096]{1,0:T(8,128)(2,1)S(1)}, bf16[96,4096]{1,0:T(8,128)(2,1)}, u32[]{:S(2)}) copy-start(bf16[96,4096]{1,0:T(8,128)(2,1)} %param.15) | copy-start | bytes 2359300
  25.7 1.7 copy-start.4
  65.0 35.3 %all-to-all-start.2 = ((bf16[8,4,400,128]{3,2,1,0:T(8,128)(2,1)}), bf16[8,4,400,128]{3,2,1,0:T(8,128)(2,1)S(1)}, u32[]{:S(2)}, u32[]{:S(2)}) async-start(bf16[8,4,400,128]{3,2,1,0:T(8,128)(2,1)} %broadcast_in_dim.92), calls=%async_computation.2 | async-start | bytes 6553600 | tf_op jit(solution)/shard_map/all_to_all | solution.py:281
  100.3 1.7 copy-start.2
  102.0 33.4 %all-to-all-start.3 = ((bf16[8,4,272,128]{3,2,1,0:T(8,128)(2,1)}), bf16[8,4,272,128]{3,2,1,0:T(8,128)(2,1)S(1)}, u32[]{:S(2)}, u32[]{:S(2)}) async-start(bf16[8,4,272,128]{3,2,1,0:T(8,128)(2,1)} %bitcast.79), calls=%async_computation.3 | async-start | bytes 4456448 | tf_op jit(solution)/shard_map/all_to_all | solution.py:281
  135.4 1.4 copy-start.1
  136.8 22.4 %all-to-all-start.4 = ((bf16[8,4,272,128]{3,2,1,0:T(8,128)(2,1)}), bf16[8,4,272,128]{3,2,1,0:T(8,128)(2,1)S(1)}, u32[]{:S(2)}, u32[]{:S(2)}) async-start(bf16[8,4,272,128]{3,2,1,0:T(8,128)(2,1)} %bitcast.78), calls=%async_computation.4 | async-start | bytes 4456448 | tf_op jit(solution)/shard_map/all_to_all | solution.py:281
  159.3 33.8 %copy-start.3 = (f32[64,4,128]{2,1,0:T(4,128)S(1)}, f32[64,4,128]{2,1,0:T(4,128)}, u32[]{:S(2)}) copy-start(f32[64,4,128]{2,1,0:T(4,128)} %fusion.5) | copy-start | bytes 393220
  162.0 30.6 %all-to-all-start.5 = ((bf16[8,272,128]{2,1,0:T(8,128)(2,1)}), bf16[8,272,128]{2,1,0:T(8,128)(2,1)S(1)}, u32[]{:S(2)}, u32[]{:S(2)}) async-start(bf16[8,272,128]{2,1,0:T(8,128)(2,1)} %pad_maximum_fusion), calls=%async_computation.5 | async-start | bytes 1114112 | tf_op jit(solution)/shard_map/all_to_all | solution.py:281

commit v7 on v6

--- a/solution.py
+++ b/solution.py
@@ -10,7 +10,7 @@
 
 MAX_PAGES = 10
 NEG = -1e30
-VMEM_BYTES = 54 * 1024 * 1024
+VMEM_BYTES = 60 * 1024 * 1024
 PER = 4
 PIECES = 4
 NT = (((1,), (1,)), ((), ()))
@@ -49,10 +49,10 @@
         halves.append(jnp.where(first, out[:, :, :value], out[:, :, value:]))
     packed[:, sixteen(at), :] = jnp.concatenate(halves, axis=1).astype(jnp.bfloat16)
 
-def attend_step(scale, at, lists_ref, packed_ref, lat_ref, keyrope_ref, held, keys, rotated, tops, totals):
+def attend_step(scale, at, lists_ref, shift, packed_ref, lat_ref, keyrope_ref, held, keys, rotated, tops, totals):
     queries, latent = held.shape[1:]
     page = lat_ref.shape[1]
-    counts = [lists_ref[at * PER + i, 0] for i in range(PER)]
+    counts = [lists_ref[at * PER + i, shift] for i in range(PER)]
     most = functools.reduce(jnp.maximum, counts)
 
     def run(pages):
@@ -63,7 +63,7 @@
         for i in range(PER):
             r = at * PER + i
             for k in range(pages):
-                slot = lists_ref[r, 1 + k]
+                slot = lists_ref[r, shift + 1 + k]
                 keys[i, k * page : (k + 1) * page, :] = lat_ref[slot]
                 rotated[i, k * page : (k + 1) * page, :] = keyrope_ref[slot]
             packed = packed_ref[r, queries : queries + queries // 2, :]
@@ -106,7 +106,7 @@
             out = jnp.where(row == level * per + c, part, out)
     packed[:, queries : queries + 16, :] = jnp.concatenate([out, jnp.zeros_like(out)], axis=1).astype(jnp.bfloat16)
 
-def body(scale, lists_ref, packed_hbm, upk_hbm, lat_hbm, keyrope_hbm, upv_hbm, out_hbm,
+def body(scale, lists_ref, place_ref, packed_hbm, upk_hbm, lat_hbm, keyrope_hbm, upv_hbm, out_hbm,
          packed, upk, lat, keyrope, upv, held, keys, rotated, tops, totals, in_sems, key_sems, value_sems, out_sems):
     heads = upk.shape[0]
     queries = held.shape[1]
@@ -148,8 +148,13 @@
         piece(upv_hbm, upv, value_sems, k).start()
 
     def attend(at, _):
-        attend_step(scale, at, lists_ref, packed, lat, keyrope, held, keys, rotated, tops, totals)
+        @pl.when(at != place_ref[0])
+        def _():
+            attend_step(
+                scale, at, lists_ref, place_ref[1], packed, lat, keyrope, held, keys, rotated, tops, totals
+            )
         return 0
+
     lax.fori_loop(0, held.shape[0] // PER, attend, 0)
 
     share_step(scale, tops, totals, packed)
@@ -169,7 +174,7 @@
         return 0
     lax.fori_loop(0, groups + 1, drain, 0)
 
-def attention(lists, packed, up_key, up_value, pool_latent, pool_rope, scale):
+def attention(lists, place, packed, up_key, up_value, pool_latent, pool_rope, scale):
     rows = packed.shape[0]
     heads, nope, latent = up_key.shape
     value = up_value.shape[2]
@@ -181,7 +186,7 @@
     return pl.pallas_call(
         functools.partial(body, scale),
         out_shape=jax.ShapeDtypeStruct((rows, queries + 16, value), jnp.bfloat16),
-        in_specs=[scalars] + [anywhere] * 5,
+        in_specs=[scalars] * 2 + [anywhere] * 5,
         out_specs=anywhere,
         scratch_shapes=[
             pltpu.VMEM((rows, queries + queries // 2, nope), jnp.bfloat16),
@@ -204,7 +209,7 @@
             flops=rows * queries * 640 * 4 * latent, bytes_accessed=1 << 27, transcendentals=0
         ),
         name="attention",
-    )(lists, packed, up_key, pool_latent, pool_rope, up_value)
+    )(lists, place, packed, up_key, pool_latent, pool_rope, up_value)
 
 
 def fresh_part(q_nope, q_rope, up_key, up_value, new_latent, new_rope, scale):
@@ -283,8 +288,14 @@
     )
 
 
-def spread(x, key):
-    return exchange(jnp.broadcast_to(x[None], (8,) + x.shape), key)
+def repeat(x):
+    return jnp.broadcast_to(x[None], (8,) + x.shape)
+
+
+def block_position():
+    i, core = lax.axis_index("batch"), lax.axis_index("head")
+    at = (i // (SIDE * SIDE), i // SIDE % SIDE, i % SIDE)
+    return corner_index([(v + SIDE - core) % 2 for v in at]).astype(jnp.int32)
 
 
 def mix(parts, queries, fresh=None):
@@ -345,7 +356,7 @@
     queries = heads * steps
     length = queries + queries // 2
 
-    near = spread(own, sublattice)
+    near = exchange(repeat(own), sublattice)
     count = 8 // HALVES
     pool_rope = pool_rope.reshape(slots_total, page, rope)
     pool_rope = jnp.pad(pool_rope, ((0, 0), (0, 0), (0, 128 - rope)))
@@ -354,19 +365,30 @@
     )
     near, pool_rope, fresh = lax.optimization_barrier((near, pool_rope, fresh))
     me = lax.axis_index("batch")
-    gathered = [
-        spread(near[k * count : (k + 1) * count], block) for k in range(HALVES)
-    ]
+
+    def attend_rows(packed, skip):
+        at_row = length + me // (nope // wide)
+        lists = lax.dynamic_index_in_dim(packed, at_row, 1, keepdims=False).astype(jnp.int32)
+        place = jnp.stack([jnp.int32(skip), me % (nope // wide) * wide]).astype(jnp.int32)
+        return attention(lists, place, packed, up_key, up_value, pool_latent, pool_rope, scale)
+
+    position = block_position()
+    halves = [near[k * count : (k + 1) * count] for k in range(HALVES)]
+    gathered = [exchange(repeat(halves[0]), block), repeat(halves[1])]
+    beside = attend_rows(near, -1)
+    *gathered, beside = lax.optimization_barrier((*gathered, beside))
+    gathered[1] = exchange(gathered[1], block)
     returned = []
     for k in range(HALVES):
-        packed = gathered[k].reshape(8 * count, own.shape[0], nope)
-        lists = packed[:, length : length + shards * wide // nope]
-        lists = lists.reshape(8 * count, shards, wide)
-        lists = lax.dynamic_index_in_dim(lists, me, 1, keepdims=False).astype(jnp.int32)
-        parts = attention(lists, packed, up_key, up_value, pool_latent, pool_rope, scale)
+        parts = attend_rows(gathered[k].reshape(8 * count, own.shape[0], nope), position)
         if k + 1 < HALVES:
             parts, gathered[k + 1] = lax.optimization_barrier((parts, gathered[k + 1]))
+        else:
+            parts, returned[0] = lax.optimization_barrier((parts, returned[0]))
         parts = exchange(parts.reshape(8, count, queries + 16, value), block)
+        parts = lax.dynamic_update_slice_in_dim(
+            parts, beside[None, k * count : (k + 1) * count], position, 0
+        )
         returned.append(parts)
     mixed = pack(*mix(returned[0], queries))
     mixed, second = lax.optimization_barrier((mixed, returned[1]))

time: 195 us -> 194 us (level)
  Pallas kernels: 44.5 us -> 74.5 us
  blocking collectives: 29.7 us -> 0 us
  starting transfers between devices: 56.5 us -> 50.2 us
  waiting for transfers between devices: 21.6 us -> 25.4 us
  other arithmetic: 11.5 us -> 15 us
    pallas_call x2 -> x3, Pallas kernels: 44.5 us -> 74.5 us  [attention(): pl.pallas_call(functools.partial(body, scale), out_shape=jax.ShapeDtypeSt...]
    all_to_all x1 -> x0, blocking collectives: 29.7 us -> none  [exchange(): lax.all_to_all(x, ('batch', 'head'), split_axis=0, concat_axis=0, tiled=T...]
    all_to_all x5 -> x6, starting transfers between devices: 56.5 us -> 50.2 us  [exchange(): lax.all_to_all(x, ('batch', 'head'), split_axis=0, concat_axis=0, tiled=T...]
    all_to_all x5 -> x6, waiting for transfers between devices: 21.6 us -> 25.4 us  [exchange(): lax.all_to_all(x, ('batch', 'head'), split_axis=0, concat_axis=0, tiled=T...]
    slice x5 -> x1, local copies, waits for them, and re-layouts: 3.57 us -> 0.05 us  [per_device(): halves = [near[k * count:(k + 1) * count] for k in range(HALVES)]]
    convert_element_type x2 -> x3, other arithmetic: 1.23 us -> 3.54 us  [attend_rows(): lax.dynamic_index_in_dim(packed, at_row, 1, keepdims=False)]
    unnamed x23 -> x24, local copies, waits for them, and re-layouts: 3.92 us -> 4.61 us
  transfers between devices with their start and end apart: 5 -> 6, of which waited for: 2 -> 4; matrix products, arithmetic and copies ran while one was open for 13% -> 14% of each run, Pallas kernels for 23% -> 38%
where the time goes in v7:
time: 194 us
  Pallas kernels  74.5 us (38%)
  starting transfers between devices  50.2 us (26%)
  waiting for transfers between devices  25.4 us (13%)
  local copies, waits for them, and re-layouts  18.1 us (9%)
  other arithmetic  15 us (8%)
  matrix products  10.7 us (6%)
    pallas_call x3, Pallas kernels, attention(): pl.pallas_call(functools.partial(body, scale), out_shape=jax.ShapeDtypeSt...  74.5 us
    all_to_all x6, starting transfers between devices, exchange(): lax.all_to_all(x, ('batch', 'head'), split_axis=0, concat_axis=0, tiled=T...  50.2 us
    all_to_all x6, waiting for transfers between devices, exchange(): lax.all_to_all(x, ('batch', 'head'), split_axis=0, concat_axis=0, tiled=T...  25.4 us
    reduce_sum x3, other arithmetic, mix(): jnp.sum(parts[:, :, :queries].astype(jnp.float32) * (share / total)[...,...  5.56 us
    broadcast_in_dim x3, local copies, waits for them, and re-layouts, repeat(): return jnp.broadcast_to(x[None], (8,) + x.shape)  5.27 us
    dot_general x1, matrix products, fresh_part(): jnp.einsum('shn,hnl->hsl', q_nope, up_key, preferred_element_type=jnp.flo...  4.65 us
    dot_general x1, matrix products, fresh_part(): jnp.einsum('hsl,hlv->hsv', mixed, up_value, preferred_element_type=jnp.fl...  4.62 us
    unnamed x24, local copies, waits for them, and re-layouts  4.61 us
  transfers between devices with their start and end apart: 6, of which 4 were waited for; matrix products, arithmetic and copies ran while one was open for 14% of the time, Pallas kernels for 38%

profile of v7, /device:TPU:1, one launch (start us, length us, event | category | flops | bytes accessed | tf_op | source)
XLA Modules:
  0.0 194.2 jit_solution(2869254377651279298)
XLA Ops:
  0.0 0.7 reduce.6
  1.1 0.9 reshape.344
  3.6 0.9 copy.55
  4.6 1.0 broadcast_in_dim.93
  5.6 10.8 %all-to-all-start = ((bf16[8,400,128]{2,1,0:T(8,128)(2,1)}), bf16[8,400,128]{2,1,0:T(8,128)(2,1)S(1)}, u32[]{:S(2)}, u32[]{:S(2)}) async-start(bf16[8,400,128]{2,1,0:T(8,128)(2,1)} %broadcast_in_dim.93), calls=%async_computation | async-start | bytes 1638400 | tf_op jit(solution)/shard_map/all_to_all | solution.py:286
  16.4 4.6 %convolution_convert_fusion = bf16[64,4,512]{2,1,0:T(4,128)(2,1)S(1)} fusion(bf16[64,128,512]{2,1,0:T(8,128)(2,1)} %upk_hbm.5, bf16[4,1,8192]{2,0,1:T(4,128)(2,1)S(1)} %copy-done.7), kind=kOutput, calls=%fused_computation.4 | convolution fusion | flops 33685504 | bytes 8716288 | tf_op jit(solution)/shard_map/shn,hnl->hsl/dot_general | solution.py:218
  21.7 1.1 fusion
  23.4 2.4 %copy.42 = bf16[96,64,64]{2,1,0:T(8,128)(2,1)S(1)} copy(bf16[96,64,64]{0,2,1:T(8,128)(2,1)S(1)} %bitcast.79) | data formatting | bytes 1572864 | tf_op jit(solution)/shard_map/reshape | solution.py:361
  25.8 1.7 pad.9.keyrope_hbm
  27.5 4.6 %fusion.5 = f32[64,4,128]{2,1,0:T(4,128)S(1)} fusion(bf16[64,512,128]{2,1,0:T(8,128)(2,1)} %upv_hbm.5, bf16[64,4,512]{2,0,1:T(8,128)(2,1)S(1)} %copy-done.5), kind=kOutput, calls=%fused_computation.17 | convolution fusion | flops 33554432 | bytes 8781824 | tf_op jit(solution)/shard_map/hsl,hlv->hsv/dot_general | solution.py:235
  32.7 2.1 %broadcast_in_dim.97 = bf16[8,4,400,128]{3,2,1,0:T(8,128)(2,1)} broadcast(bf16[4,400,128]{2,1,0:T(8,128)(2,1)S(1)} %get-tuple-element.32), dimensions={1,2,3} | broadcast | bytes 3686400 | tf_op jit(solution)/shard_map/broadcast_in_dim | solution.py:292
  34.8 11.3 %all-to-all-start.1 = ((bf16[8,4,400,128]{3,2,1,0:T(8,128)(2,1)}), bf16[8,4,400,128]{3,2,1,0:T(8,128)(2,1)}, u32[]{:S(2)}, u32[]{:S(2)}) async-start(bf16[8,4,400,128]{3,2,1,0:T(8,128)(2,1)} %broadcast_in_dim.97), calls=%async_computation.1 | async-start | bytes 6553600 | tf_op jit(solution)/shard_map/all_to_all | solution.py:286
  47.4 14.7 %attention.3 = bf16[8,272,128]{2,1,0:T(8,128)(2,1)} custom-call(s32[8,128]{1,0:T(8,128)} %bitcast.102, s32[2]{0:T(128)} %pad_add_fusion.place_ref, bf16[8,400,128]{2,1,0:T(8,128)(2,1)} %copy-done.2, bf16[64,128,512]{2,1,0:T(8,128)(2,1)} %upk_hbm.5, bf16[96,64,512]{2,1,0:T(8,128)(2,1)} %lat_hbm.5, bf16[96,64,128]{2,1,0:T(8,128)(2,1)} %pad.9.keyrope_hbm, ...), custom_call_target="tpu_custom_call" | custom-call | flops 2684354560 | bytes 134217728 | tf_op jit(solution)/shard_map/attention/pallas_call | solution.py:186
  62.1 5.3 %all-to-all-done.1 = bf16[8,4,400,128]{3,2,1,0:T(8,128)(2,1)} async-done(((bf16[8,4,400,128]{3,2,1,0:T(8,128)(2,1)}), bf16[8,4,400,128]{3,2,1,0:T(8,128)(2,1)}, u32[]{:S(2)}, u32[]{:S(2)}) %all-to-all-start.1) | async-done | bytes 3276832 | tf_op jit(solution)/shard_map/all_to_all | solution.py:286
  67.4 2.1 %broadcast_in_dim.98 = bf16[8,4,400,128]{3,2,1,0:T(8,128)(2,1)} broadcast(bf16[4,400,128]{2,1,0:T(8,128)(2,1)S(1)} %get-tuple-element.31), dimensions={1,2,3} | broadcast | bytes 3686400 | tf_op jit(solution)/shard_map/broadcast_in_dim | solution.py:292
  69.5 8.2 %all-to-all-start.2 = ((bf16[8,4,400,128]{3,2,1,0:T(8,128)(2,1)}), bf16[8,4,400,128]{3,2,1,0:T(8,128)(2,1)S(1)}, u32[]{:S(2)}, u32[]{:S(2)}) async-start(bf16[8,4,400,128]{3,2,1,0:T(8,128)(2,1)} %broadcast_in_dim.98), calls=%async_computation.2 | async-start | bytes 6553600 | tf_op jit(solution)/shard_map/all_to_all | solution.py:286
  78.4 1.5 dynamic-slice_convert_fusion.1
  79.9 29.8 %attention.4 = bf16[32,272,128]{2,1,0:T(8,128)(2,1)} custom-call(s32[32,128]{1,0:T(8,128)} %bitcast.104, s32[2]{0:T(128)} %pad_add_fusion.1.place_ref, bf16[32,400,128]{2,1,0:T(8,128)(2,1)} %bitcast.14.packed_hbm, bf16[64,128,512]{2,1,0:T(8,128)(2,1)} %upk_hbm.5, bf16[96,64,512]{2,1,0:T(8,128)(2,1)} %lat_hbm.5, bf16[96,64,128]{2,1,0:T(8,128)(2,1)} %pad.9.keyrope_hbm, ...), custom_call_target="tpu_custom_call" | custom-call | flops 10737418240 | bytes 134217728 | tf_op jit(solution)/shard_map/attention/pallas_call | solution.py:186
  109.7 1.7 copy-done.3
  111.4 8.2 %all-to-all-start.3 = ((bf16[8,4,272,128]{3,2,1,0:T(8,128)(2,1)}), bf16[8,4,272,128]{3,2,1,0:T(8,128)(2,1)S(1)}, u32[]{:S(2)}, u32[]{:S(2)}) async-start(bf16[8,4,272,128]{3,2,1,0:T(8,128)(2,1)} %bitcast.83), calls=%async_computation.3 | async-start | bytes 4456448 | tf_op jit(solution)/shard_map/all_to_all | solution.py:286
  119.6 1.5 dynamic-slice_convert_fusion
  121.0 30.0 %attention.5 = bf16[32,272,128]{2,1,0:T(8,128)(2,1)} custom-call(s32[32,128]{1,0:T(8,128)} %bitcast.103, s32[2]{0:T(128)} %pad_add_fusion.1.place_ref, bf16[32,400,128]{2,1,0:T(8,128)(2,1)} %bitcast.81, bf16[64,128,512]{2,1,0:T(8,128)(2,1)} %upk_hbm.5, bf16[96,64,512]{2,1,0:T(8,128)(2,1)} %lat_hbm.5, bf16[96,64,128]{2,1,0:T(8,128)(2,1)} %pad.9.keyrope_hbm, ...), custom_call_target="tpu_custom_call" | custom-call | flops 10737418240 | bytes 134217728 | tf_op jit(solution)/shard_map/attention/pallas_call | solution.py:186
  151.1 1.4 copy-done.1
  152.5 8.2 %all-to-all-start.4 = ((bf16[8,4,272,128]{3,2,1,0:T(8,128)(2,1)}), bf16[8,4,272,128]{3,2,1,0:T(8,128)(2,1)S(1)}, u32[]{:S(2)}, u32[]{:S(2)}) async-start(bf16[8,4,272,128]{3,2,1,0:T(8,128)(2,1)} %bitcast.82), calls=%async_computation.4 | async-start | bytes 4456448 | tf_op jit(solution)/shard_map/all_to_all | solution.py:286
  160.7 0.8 slice_convert_fusion.1
  161.8 3.9 %multiply_reduce_fusion.1 = bf16[4,256,128]{2,1,0:T(8,128)(2,1)} fusion(f32[8,4,256]{2,1,0:T(4,128)S(1)} %bitcast.95, bf16[8,4,272,128]{3,2,1,0:T(8,128)(2,1)} %copy-done.1), kind=kLoop, calls=%fused_computation.1 | loop fusion | flops 3014656 | bytes 2392064 | tf_op jit(solution)/shard_map/reduce_sum | solution.py:314
  165.7 1.2 concatenate.20
  166.9 7.9 %all-to-all-done.4 = bf16[8,4,272,128]{3,2,1,0:T(8,128)(2,1)S(1)} async-done(((bf16[8,4,272,128]{3,2,1,0:T(8,128)(2,1)}), bf16[8,4,272,128]{3,2,1,0:T(8,128)(2,1)S(1)}, u32[]{:S(2)}, u32[]{:S(2)}) %all-to-all-start.4) | async-done | bytes 2228256 | tf_op jit(solution)/shard_map/all_to_all | solution.py:286
  175.2 1.3 multiply_reduce_fusion
  176.7 0.8 pad_maximum_fusion
  177.6 3.5 %all-to-all-start.5 = ((bf16[8,272,128]{2,1,0:T(8,128)(2,1)}), bf16[8,272,128]{2,1,0:T(8,128)(2,1)S(1)}, u32[]{:S(2)}, u32[]{:S(2)}) async-start(bf16[8,272,128]{2,1,0:T(8,128)(2,1)} %pad_maximum_fusion), calls=%async_computation.5 | async-start | bytes 1114112 | tf_op jit(solution)/shard_map/all_to_all | solution.py:286
  181.3 11.6 %all-to-all-done.5 = bf16[8,272,128]{2,1,0:T(8,128)(2,1)S(1)} async-done(((bf16[8,272,128]{2,1,0:T(8,128)(2,1)}), bf16[8,272,128]{2,1,0:T(8,128)(2,1)S(1)}, u32[]{:S(2)}, u32[]{:S(2)}) %all-to-all-start.5) | async-done | bytes 557088 | tf_op jit(solution)/shard_map/all_to_all | solution.py:286
  (88 shorter events, 8.1 us)
Async XLA Ops:
  0.0 21.2 %copy-start = (bf16[4,1,512]{2,0,1:T(4,128)(2,1)S(1)}, bf16[4,1,512]{2,0,1:T(4,128)(2,1)}, u32[]{:S(2)}) copy-start(bf16[4,1,512]{2,0,1:T(4,128)(2,1)} %param.16) | copy-start | bytes 12292
  0.0 16.4 %copy-start.7 = (bf16[4,1,8192]{2,0,1:T(4,128)(2,1)S(1)}, bf16[4,1,8192]{2,0,1:T(4,128)(2,1)}, u32[]{:S(2)}) copy-start(bf16[4,1,8192]{2,0,1:T(4,128)(2,1)} %param.10) | copy-start | bytes 196612
  5.6 27.0 %all-to-all-start = ((bf16[8,400,128]{2,1,0:T(8,128)(2,1)}), bf16[8,400,128]{2,1,0:T(8,128)(2,1)S(1)}, u32[]{:S(2)}, u32[]{:S(2)}) async-start(bf16[8,400,128]{2,1,0:T(8,128)(2,1)} %broadcast_in_dim.93), calls=%async_computation | async-start | bytes 1638400 | tf_op jit(solution)/shard_map/all_to_all | solution.py:286
  16.4 4.7 %copy-start.8 = (bf16[1,256]{1,0:T(2,128)(2,1)S(1)}, bf16[1,256]{1,0:T(2,128)(2,1)}, u32[]{:S(2)}) copy-start(bf16[1,256]{1,0:T(2,128)(2,1)} %param.17) | copy-start | bytes 1540
  16.4 6.3 %copy-start.6 = (bf16[96,4096]{1,0:T(8,128)(2,1)S(1)}, bf16[96,4096]{1,0:T(8,128)(2,1)}, u32[]{:S(2)}) copy-start(bf16[96,4096]{1,0:T(8,128)(2,1)} %param.15) | copy-start | bytes 2359300
  25.8 1.7 copy-start.5
  32.6 14.2 %copy-start.2 = (bf16[8,400,128]{2,1,0:T(8,128)(2,1)}, bf16[8,400,128]{2,1,0:T(8,128)(2,1)S(1)}, u32[]{:S(2)}) copy-start(bf16[8,400,128]{2,1,0:T(8,128)(2,1)S(1)} %all-to-all-done.packed_hbm) | copy-start | bytes 2457604
  34.8 32.6 %all-to-all-start.1 = ((bf16[8,4,400,128]{3,2,1,0:T(8,128)(2,1)}), bf16[8,4,400,128]{3,2,1,0:T(8,128)(2,1)}, u32[]{:S(2)}, u32[]{:S(2)}) async-start(bf16[8,4,400,128]{3,2,1,0:T(8,128)(2,1)} %broadcast_in_dim.97), calls=%async_computation.1 | async-start | bytes 6553600 | tf_op jit(solution)/shard_map/all_to_all | solution.py:286
  69.5 40.1 %all-to-all-start.2 = ((bf16[8,4,400,128]{3,2,1,0:T(8,128)(2,1)}), bf16[8,4,400,128]{3,2,1,0:T(8,128)(2,1)S(1)}, u32[]{:S(2)}, u32[]{:S(2)}) async-start(bf16[8,4,400,128]{3,2,1,0:T(8,128)(2,1)} %broadcast_in_dim.98), calls=%async_computation.2 | async-start | bytes 6553600 | tf_op jit(solution)/shard_map/all_to_all | solution.py:286
  109.7 1.7 copy-start.3
  111.4 39.7 %all-to-all-start.3 = ((bf16[8,4,272,128]{3,2,1,0:T(8,128)(2,1)}), bf16[8,4,272,128]{3,2,1,0:T(8,128)(2,1)S(1)}, u32[]{:S(2)}, u32[]{:S(2)}) async-start(bf16[8,4,272,128]{3,2,1,0:T(8,128)(2,1)} %bitcast.83), calls=%async_computation.3 | async-start | bytes 4456448 | tf_op jit(solution)/shard_map/all_to_all | solution.py:286
  121.0 30.0 %copy-start.4 = (bf16[8,272,128]{2,1,0:T(8,128)(2,1)S(1)}, bf16[8,272,128]{2,1,0:T(8,128)(2,1)}, u32[]{:S(2)}) copy-start(bf16[8,272,128]{2,1,0:T(8,128)(2,1)} %attention.3) | copy-start | bytes 1671172
  151.1 1.4 copy-start.1
  152.5 22.3 %all-to-all-start.4 = ((bf16[8,4,272,128]{3,2,1,0:T(8,128)(2,1)}), bf16[8,4,272,128]{3,2,1,0:T(8,128)(2,1)S(1)}, u32[]{:S(2)}, u32[]{:S(2)}) async-start(bf16[8,4,272,128]{3,2,1,0:T(8,128)(2,1)} %bitcast.82), calls=%async_computation.4 | async-start | bytes 4456448 | tf_op jit(solution)/shard_map/all_to_all | solution.py:286
  177.6 15.4 %all-to-all-start.5 = ((bf16[8,272,128]{2,1,0:T(8,128)(2,1)}), bf16[8,272,128]{2,1,0:T(8,128)(2,1)S(1)}, u32[]{:S(2)}, u32[]{:S(2)}) async-start(bf16[8,272,128]{2,1,0:T(8,128)(2,1)} %pad_maximum_fusion), calls=%async_computation.5 | async-start | bytes 1114112 | tf_op jit(solution)/shard_map/all_to_all | solution.py:286

commit v8 on v7

--- a/solution.py
+++ b/solution.py
@@ -10,7 +10,7 @@
 
 MAX_PAGES = 10
 NEG = -1e30
-VMEM_BYTES = 60 * 1024 * 1024
+VMEM_BYTES = 52 * 1024 * 1024
 PER = 4
 PIECES = 4
 NT = (((1,), (1,)), ((), ()))
@@ -106,8 +106,13 @@
             out = jnp.where(row == level * per + c, part, out)
     packed[:, queries : queries + 16, :] = jnp.concatenate([out, jnp.zeros_like(out)], axis=1).astype(jnp.bfloat16)
 
-def body(scale, lists_ref, place_ref, packed_hbm, upk_hbm, lat_hbm, keyrope_hbm, upv_hbm, out_hbm,
-         packed, upk, lat, keyrope, upv, held, keys, rotated, tops, totals, in_sems, key_sems, value_sems, out_sems):
+def body(scale, repeats, lists_ref, place_ref, packed_hbm, upk_hbm, lat_hbm, keyrope_hbm, upv_hbm, out_hbm,
+         *refs):
+    repeated = None
+    if repeats:
+        repeated, *refs = refs
+    packed, upk, lat, keyrope, upv, held, keys, rotated, tops, totals, *sems = refs
+    in_sems, key_sems, value_sems, out_sems, repeat_sems = sems
     heads = upk.shape[0]
     queries = held.shape[1]
     groups = heads // 4
@@ -116,6 +121,12 @@
     def piece(hbm, vmem, sems, k):
         span = pl.ds(k * chunk, chunk)
         return pltpu.make_async_copy(hbm.at[span], vmem.at[span], sems.at[k])
+
+    def repeat_copy(k):
+        half = packed_hbm.shape[0] // 2
+        return pltpu.make_async_copy(
+            packed_hbm.at[pl.ds(half, half)], repeated.at[k], repeat_sems.at[k]
+        )
 
     def out_copy(at):
         return pltpu.make_async_copy(packed.at[:, sixteen(at), :], out_hbm.at[:, sixteen(at), :], out_sems.at[at])
@@ -146,6 +157,8 @@
     load_rope.wait()
     for k in range(PIECES):
         piece(upv_hbm, upv, value_sems, k).start()
+    for k in range(repeats):
+        repeat_copy(k).start()
 
     def attend(at, _):
         @pl.when(at != place_ref[0])
@@ -173,8 +186,10 @@
         out_copy(at).wait()
         return 0
     lax.fori_loop(0, groups + 1, drain, 0)
-
-def attention(lists, place, packed, up_key, up_value, pool_latent, pool_rope, scale):
+    for k in range(repeats):
+        repeat_copy(k).wait()
+
+def attention(lists, place, packed, up_key, up_value, pool_latent, pool_rope, scale, repeats=0):
     rows = packed.shape[0]
     heads, nope, latent = up_key.shape
     value = up_value.shape[2]
@@ -182,12 +197,15 @@
     page = pool_latent.shape[1]
     rope = pool_rope.shape[2]
     anywhere = pl.BlockSpec(memory_space=pl.ANY)
+    outs = [jax.ShapeDtypeStruct((rows, queries + 16, value), jnp.bfloat16)]
+    if repeats:
+        outs.append(jax.ShapeDtypeStruct((repeats, rows // 2) + packed.shape[1:], jnp.bfloat16))
     scalars = pl.BlockSpec(memory_space=pltpu.SMEM)
     return pl.pallas_call(
-        functools.partial(body, scale),
-        out_shape=jax.ShapeDtypeStruct((rows, queries + 16, value), jnp.bfloat16),
+        functools.partial(body, scale, repeats),
+        out_shape=outs if repeats else outs[0],
         in_specs=[scalars] * 2 + [anywhere] * 5,
-        out_specs=anywhere,
+        out_specs=[anywhere] * len(outs) if repeats else anywhere,
         scratch_shapes=[
             pltpu.VMEM((rows, queries + queries // 2, nope), jnp.bfloat16),
             pltpu.VMEM(up_key.shape, jnp.bfloat16),
@@ -203,6 +221,7 @@
             pltpu.SemaphoreType.DMA((PIECES,)),
             pltpu.SemaphoreType.DMA((PIECES,)),
             pltpu.SemaphoreType.DMA((heads // 4 + 1,)),
+            pltpu.SemaphoreType.DMA((8,)),
         ],
         compiler_params=pltpu.CompilerParams(vmem_limit_bytes=VMEM_BYTES),
         cost_estimate=pl.CostEstimate(
@@ -366,17 +385,19 @@
     near, pool_rope, fresh = lax.optimization_barrier((near, pool_rope, fresh))
     me = lax.axis_index("batch")
 
-    def attend_rows(packed, skip):
+    def attend_rows(packed, skip, repeats=0):
         at_row = length + me // (nope // wide)
         lists = lax.dynamic_index_in_dim(packed, at_row, 1, keepdims=False).astype(jnp.int32)
         place = jnp.stack([jnp.int32(skip), me % (nope // wide) * wide]).astype(jnp.int32)
-        return attention(lists, place, packed, up_key, up_value, pool_latent, pool_rope, scale)
+        return attention(
+            lists, place, packed, up_key, up_value, pool_latent, pool_rope, scale, repeats
+        )
 
     position = block_position()
-    halves = [near[k * count : (k + 1) * count] for k in range(HALVES)]
-    gathered = [exchange(repeat(halves[0]), block), repeat(halves[1])]
-    beside = attend_rows(near, -1)
-    *gathered, beside = lax.optimization_barrier((*gathered, beside))
+    first = exchange(repeat(near[:count]), block)
+    beside, second = attend_rows(near, -1, 8)
+    first, second, beside = lax.optimization_barrier((first, second, beside))
+    gathered = [first, second]
     gathered[1] = exchange(gathered[1], block)
     returned = []
     for k in range(HALVES):

time: 194 us -> 188 us (0.969)
  Pallas kernels: 74.5 us -> 58.8 us
  starting transfers between devices: 50.2 us -> 61.6 us
  waiting for transfers between devices: 25.4 us -> 31 us
  local copies, waits for them, and re-layouts: 18.1 us -> 14.3 us
  other arithmetic: 15 us -> 11.3 us
    pallas_call x3, Pallas kernels: 74.5 us -> 58.8 us  [attention(): pl.pallas_call(functools.partial(body, scale, repeats), out_shape=outs if...]
    all_to_all x6, starting transfers between devices: 50.2 us -> 61.6 us  [exchange(): lax.all_to_all(x, ('batch', 'head'), split_axis=0, concat_axis=0, tiled=T...]
    all_to_all x6, waiting for transfers between devices: 25.4 us -> 31 us  [exchange(): lax.all_to_all(x, ('batch', 'head'), split_axis=0, concat_axis=0, tiled=T...]
    unnamed x24 -> x16, local copies, waits for them, and re-layouts: 4.61 us -> 2.21 us
    broadcast_in_dim x3 -> x2, local copies, waits for them, and re-layouts: 5.27 us -> 3.14 us  [repeat(): return jnp.broadcast_to(x[None], (8,) + x.shape)]
  transfers between devices with their start and end apart: 6 -> 6, of which waited for: 4 -> 3; matrix products, arithmetic and copies ran while one was open for 14% -> 12% of each run, Pallas kernels for 38% -> 31%
where the time goes in v8:
time: 188 us; the launch traced here: 187 us
  starting transfers between devices  61.6 us (33%)
  Pallas kernels  58.8 us (31%)
  waiting for transfers between devices  31 us (16%)
  local copies, waits for them, and re-layouts  14.3 us (8%)
  other arithmetic  11.3 us (6%)
  matrix products  9.96 us (5%)
    all_to_all x6, starting transfers between devices, exchange(): lax.all_to_all(x, ('batch', 'head'), split_axis=0, concat_axis=0, tiled=T...  61.6 us
    pallas_call x3, Pallas kernels, attention(): pl.pallas_call(functools.partial(body, scale, repeats), out_shape=outs if...  58.8 us
    all_to_all x6, waiting for transfers between devices, exchange(): lax.all_to_all(x, ('batch', 'head'), split_axis=0, concat_axis=0, tiled=T...  31 us
    reduce_sum x3, other arithmetic, mix(): jnp.sum(parts[:, :, :queries].astype(jnp.float32) * (share / total)[...,...  4.86 us
    dot_general x1, matrix products, fresh_part(): jnp.einsum('hsl,hlv->hsv', mixed, up_value, preferred_element_type=jnp.fl...  4.62 us
    dot_general x1, matrix products, fresh_part(): jnp.einsum('shn,hnl->hsl', q_nope, up_key, preferred_element_type=jnp.flo...  4.59 us
  transfers between devices with their start and end apart: 6, of which 3 were waited for; matrix products, arithmetic and copies ran while one was open for 12% of the time, Pallas kernels for 31%

profile of v8, /device:TPU:1, one launch (start us, length us, event | category | flops | bytes accessed | tf_op | source)
XLA Modules:
  0.0 187.3 jit_solution(14473300231184648862)
XLA Ops:
  0.0 0.8 reduce.6
  1.1 0.7 reduce.7
  2.5 0.9 reshape.343
  3.7 0.9 copy.55
  4.6 1.0 broadcast_in_dim.87
  5.7 10.8 %all-to-all-start = ((bf16[8,400,128]{2,1,0:T(8,128)(2,1)}), bf16[8,400,128]{2,1,0:T(8,128)(2,1)S(1)}, u32[]{:S(2)}, u32[]{:S(2)}) async-start(bf16[8,400,128]{2,1,0:T(8,128)(2,1)} %broadcast_in_dim.87), calls=%async_computation | async-start | bytes 1638400 | tf_op jit(solution)/shard_map/all_to_all | solution.py:305
  16.5 1.3 copy.41
  17.8 3.3 %copy.42 = bf16[96,64,64]{2,1,0:T(8,128)(2,1)S(1)} copy(bf16[96,64,64]{0,2,1:T(8,128)(2,1)} %bitcast.82) | data formatting | bytes 1572864 | tf_op jit(solution)/shard_map/reshape | solution.py:380
  21.1 1.6 pad.9.keyrope_hbm
  22.8 4.6 %convolution_convert_fusion = bf16[64,4,512]{2,1,0:T(4,128)(2,1)S(1)} fusion(bf16[64,128,512]{2,1,0:T(8,128)(2,1)} %upk_hbm.5, bf16[4,1,8192]{2,0,1:T(4,128)(2,1)S(1)} %copy-done.3), kind=kOutput, calls=%fused_computation.4 | convolution fusion | flops 33685504 | bytes 8716288 | tf_op jit(solution)/shard_map/shn,hnl->hsl/dot_general | solution.py:237
  28.0 0.3 fusion
  28.3 4.6 %fusion.5 = f32[64,4,128]{2,1,0:T(4,128)S(1)} fusion(bf16[64,512,128]{2,1,0:T(8,128)(2,1)} %upv_hbm.5, bf16[64,4,512]{2,0,1:T(8,128)(2,1)S(1)} %fusion), kind=kOutput, calls=%fused_computation.17 | convolution fusion | flops 33554432 | bytes 8781824 | tf_op jit(solution)/shard_map/hsl,hlv->hsv/dot_general | solution.py:254
  33.0 2.1 %broadcast_in_dim.91 = bf16[8,4,400,128]{3,2,1,0:T(8,128)(2,1)} broadcast(bf16[4,400,128]{2,1,0:T(8,128)(2,1)S(1)} %slice.27), dimensions={1,2,3} | broadcast | bytes 3686400 | tf_op jit(solution)/shard_map/broadcast_in_dim | solution.py:311
  35.1 11.9 %all-to-all-start.1 = ((bf16[8,4,400,128]{3,2,1,0:T(8,128)(2,1)}), bf16[8,4,400,128]{3,2,1,0:T(8,128)(2,1)}, u32[]{:S(2)}, u32[]{:S(2)}) async-start(bf16[8,4,400,128]{3,2,1,0:T(8,128)(2,1)} %broadcast_in_dim.91), calls=%async_computation.1 | async-start | bytes 6553600 | tf_op jit(solution)/shard_map/all_to_all | solution.py:305
  47.1 13.8 %attention.3 = (bf16[8,272,128]{2,1,0:T(8,128)(2,1)S(1)}, bf16[8,4,400,128]{3,2,1,0:T(8,128)(2,1)}) custom-call(s32[8,128]{1,0:T(8,128)S(1)} %bitcast.79, s32[2]{0:T(128)S(1)} %pad_add_fusion.place_ref, bf16[8,400,128]{2,1,0:T(8,128)(2,1)S(1)} %all-to-all-done.packed_hbm, bf16[64,128,512]{2,1,0:T(8,128)(2,1)} %upk_hbm.5, bf16[96,64,512]{2,1,0:T(8,128)(2,1)} %lat_hbm.5, ...), custom_call_target="tpu_custom_call" | custom-call | flops 2684354560 | bytes 134217728 | tf_op jit(solution)/shard_map/attention/pallas_call | solution.py:204
  60.8 7.4 %all-to-all-done.1 = bf16[8,4,400,128]{3,2,1,0:T(8,128)(2,1)} async-done(((bf16[8,4,400,128]{3,2,1,0:T(8,128)(2,1)}), bf16[8,4,400,128]{3,2,1,0:T(8,128)(2,1)}, u32[]{:S(2)}, u32[]{:S(2)}) %all-to-all-start.1) | async-done | bytes 3276832 | tf_op jit(solution)/shard_map/all_to_all | solution.py:305
  68.2 9.0 %all-to-all-start.2 = ((bf16[8,4,400,128]{3,2,1,0:T(8,128)(2,1)}), bf16[8,4,400,128]{3,2,1,0:T(8,128)(2,1)}, u32[]{:S(2)}, u32[]{:S(2)}) async-start(bf16[8,4,400,128]{3,2,1,0:T(8,128)(2,1)} %get-tuple-element.25), calls=%async_computation.2 | async-start | bytes 6553600 | tf_op jit(solution)/shard_map/all_to_all | solution.py:305
  77.3 0.9 dynamic-slice_convert_fusion.1
  78.2 22.7 %attention.4 = bf16[32,272,128]{2,1,0:T(8,128)(2,1)} custom-call(s32[32,128]{1,0:T(8,128)S(1)} %bitcast.81, s32[2]{0:T(128)S(1)} %pad_add_fusion.1.place_ref, bf16[32,400,128]{2,1,0:T(8,128)(2,1)} %bitcast.14.packed_hbm, bf16[64,128,512]{2,1,0:T(8,128)(2,1)} %upk_hbm.5, bf16[96,64,512]{2,1,0:T(8,128)(2,1)} %lat_hbm.5, bf16[96,64,128]{2,1,0:T(8,128)(2,1)S(1)} %copy-done.1, ...), custom_call_target="tpu_custom_call" | custom-call | flops 10737418240 | bytes 134217728 | tf_op jit(solution)/shard_map/attention/pallas_call | solution.py:204
  100.9 11.0 %all-to-all-start.3 = ((bf16[8,4,272,128]{3,2,1,0:T(8,128)(2,1)}), bf16[8,4,272,128]{3,2,1,0:T(8,128)(2,1)}, u32[]{:S(2)}, u32[]{:S(2)}) async-start(bf16[8,4,272,128]{3,2,1,0:T(8,128)(2,1)} %bitcast.84), calls=%async_computation.3 | async-start | bytes 4456448 | tf_op jit(solution)/shard_map/all_to_all | solution.py:305
  111.8 0.9 dynamic-slice_convert_fusion
  112.7 22.3 %attention.5 = bf16[32,272,128]{2,1,0:T(8,128)(2,1)} custom-call(s32[32,128]{1,0:T(8,128)S(1)} %bitcast.80, s32[2]{0:T(128)S(1)} %pad_add_fusion.1.place_ref, bf16[32,400,128]{2,1,0:T(8,128)(2,1)} %bitcast.17.packed_hbm, bf16[64,128,512]{2,1,0:T(8,128)(2,1)} %upk_hbm.5, bf16[96,64,512]{2,1,0:T(8,128)(2,1)} %lat_hbm.5, bf16[96,64,128]{2,1,0:T(8,128)(2,1)S(1)} %copy-done.1, ...), custom_call_target="tpu_custom_call" | custom-call | flops 10737418240 | bytes 134217728 | tf_op jit(solution)/shard_map/attention/pallas_call | solution.py:204
  135.0 0.7 bitcast_dynamic-update-slice_fusion.1
  135.8 10.6 %all-to-all-start.4 = ((bf16[8,4,272,128]{3,2,1,0:T(8,128)(2,1)}), bf16[8,4,272,128]{3,2,1,0:T(8,128)(2,1)S(1)}, u32[]{:S(2)}, u32[]{:S(2)}) async-start(bf16[8,4,272,128]{3,2,1,0:T(8,128)(2,1)} %bitcast.83), calls=%async_computation.4 | async-start | bytes 4456448 | tf_op jit(solution)/shard_map/all_to_all | solution.py:305
  146.3 0.8 slice_convert_fusion.1
  147.5 3.2 %multiply_reduce_fusion.1 = bf16[4,256,128]{2,1,0:T(8,128)(2,1)S(1)} fusion(f32[8,4,256]{2,1,0:T(4,128)S(1)} %bitcast.96, bf16[8,4,272,128]{3,2,1,0:T(8,128)(2,1)} %bitcast_dynamic-update-slice_fusion.1), kind=kLoop, calls=%fused_computation.1 | loop fusion | flops 3014656 | bytes 2392064 | tf_op jit(solution)/shard_map/reduce_sum | solution.py:333
  151.0 9.4 %all-to-all-done.4 = bf16[8,4,272,128]{3,2,1,0:T(8,128)(2,1)S(1)} async-done(((bf16[8,4,272,128]{3,2,1,0:T(8,128)(2,1)}), bf16[8,4,272,128]{3,2,1,0:T(8,128)(2,1)S(1)}, u32[]{:S(2)}, u32[]{:S(2)}) %all-to-all-start.4) | async-done | bytes 2228256 | tf_op jit(solution)/shard_map/all_to_all | solution.py:305
  160.8 1.3 multiply_reduce_fusion
  162.4 0.8 pad_maximum_fusion
  163.3 8.4 %all-to-all-start.5 = ((bf16[8,272,128]{2,1,0:T(8,128)(2,1)}), bf16[8,272,128]{2,1,0:T(8,128)(2,1)S(1)}, u32[]{:S(2)}, u32[]{:S(2)}) async-start(bf16[8,272,128]{2,1,0:T(8,128)(2,1)} %pad_maximum_fusion), calls=%async_computation.5 | async-start | bytes 1114112 | tf_op jit(solution)/shard_map/all_to_all | solution.py:305
  171.9 14.1 %all-to-all-done.5 = bf16[8,272,128]{2,1,0:T(8,128)(2,1)S(1)} async-done(((bf16[8,272,128]{2,1,0:T(8,128)(2,1)}), bf16[8,272,128]{2,1,0:T(8,128)(2,1)S(1)}, u32[]{:S(2)}, u32[]{:S(2)}) %all-to-all-start.5) | async-done | bytes 557088 | tf_op jit(solution)/shard_map/all_to_all | solution.py:305
  186.6 0.7 reshape.361
  (79 shorter events, 4.1 us)
Async XLA Ops:
  0.0 27.5 %copy-start = (bf16[4,1,512]{2,0,1:T(4,128)(2,1)S(1)}, bf16[4,1,512]{2,0,1:T(4,128)(2,1)}, u32[]{:S(2)}) copy-start(bf16[4,1,512]{2,0,1:T(4,128)(2,1)} %param.16) | copy-start | bytes 12292
  0.0 16.5 %copy-start.2 = (bf16[96,4096]{1,0:T(8,128)(2,1)S(1)}, bf16[96,4096]{1,0:T(8,128)(2,1)}, u32[]{:S(2)}) copy-start(bf16[96,4096]{1,0:T(8,128)(2,1)} %param.15) | copy-start | bytes 2359300
  5.7 27.3 %all-to-all-start = ((bf16[8,400,128]{2,1,0:T(8,128)(2,1)}), bf16[8,400,128]{2,1,0:T(8,128)(2,1)S(1)}, u32[]{:S(2)}, u32[]{:S(2)}) async-start(bf16[8,400,128]{2,1,0:T(8,128)(2,1)} %broadcast_in_dim.87), calls=%async_computation | async-start | bytes 1638400 | tf_op jit(solution)/shard_map/all_to_all | solution.py:305
  17.8 5.0 %copy-start.3 = (bf16[4,1,8192]{2,0,1:T(4,128)(2,1)S(1)}, bf16[4,1,8192]{2,0,1:T(4,128)(2,1)}, u32[]{:S(2)}) copy-start(bf16[4,1,8192]{2,0,1:T(4,128)(2,1)} %param.10) | copy-start | bytes 196612
  22.8 4.6 %copy-start.4 = (bf16[1,256]{1,0:T(2,128)(2,1)S(1)}, bf16[1,256]{1,0:T(2,128)(2,1)}, u32[]{:S(2)}) copy-start(bf16[1,256]{1,0:T(2,128)(2,1)} %param.17) | copy-start | bytes 1540
  35.1 33.1 %all-to-all-start.1 = ((bf16[8,4,400,128]{3,2,1,0:T(8,128)(2,1)}), bf16[8,4,400,128]{3,2,1,0:T(8,128)(2,1)}, u32[]{:S(2)}, u32[]{:S(2)}) async-start(bf16[8,4,400,128]{3,2,1,0:T(8,128)(2,1)} %broadcast_in_dim.91), calls=%async_computation.1 | async-start | bytes 6553600 | tf_op jit(solution)/shard_map/all_to_all | solution.py:305
  68.2 9.9 %copy-start.1 = (bf16[96,64,128]{2,1,0:T(8,128)(2,1)S(1)}, bf16[96,64,128]{2,1,0:T(8,128)(2,1)}, u32[]{:S(2)}) copy-start(bf16[96,64,128]{2,1,0:T(8,128)(2,1)} %pad.9.keyrope_hbm) | copy-start | bytes 4718596
  68.2 32.6 %all-to-all-start.2 = ((bf16[8,4,400,128]{3,2,1,0:T(8,128)(2,1)}), bf16[8,4,400,128]{3,2,1,0:T(8,128)(2,1)}, u32[]{:S(2)}, u32[]{:S(2)}) async-start(bf16[8,4,400,128]{3,2,1,0:T(8,128)(2,1)} %get-tuple-element.25), calls=%async_computation.2 | async-start | bytes 6553600 | tf_op jit(solution)/shard_map/all_to_all | solution.py:305
  100.9 34.2 %all-to-all-start.3 = ((bf16[8,4,272,128]{3,2,1,0:T(8,128)(2,1)}), bf16[8,4,272,128]{3,2,1,0:T(8,128)(2,1)}, u32[]{:S(2)}, u32[]{:S(2)}) async-start(bf16[8,4,272,128]{3,2,1,0:T(8,128)(2,1)} %bitcast.84), calls=%async_computation.3 | async-start | bytes 4456448 | tf_op jit(solution)/shard_map/all_to_all | solution.py:305
  135.8 24.7 %all-to-all-start.4 = ((bf16[8,4,272,128]{3,2,1,0:T(8,128)(2,1)}), bf16[8,4,272,128]{3,2,1,0:T(8,128)(2,1)S(1)}, u32[]{:S(2)}, u32[]{:S(2)}) async-start(bf16[8,4,272,128]{3,2,1,0:T(8,128)(2,1)} %bitcast.83), calls=%async_computation.4 | async-start | bytes 4456448 | tf_op jit(solution)/shard_map/all_to_all | solution.py:305
  163.3 22.7 %all-to-all-start.5 = ((bf16[8,272,128]{2,1,0:T(8,128)(2,1)}), bf16[8,272,128]{2,1,0:T(8,128)(2,1)S(1)}, u32[]{:S(2)}, u32[]{:S(2)}) async-start(bf16[8,272,128]{2,1,0:T(8,128)(2,1)} %pad_maximum_fusion), calls=%async_computation.5 | async-start | bytes 1114112 | tf_op jit(solution)/shard_map/all_to_all | solution.py:305

commit v9 on v8

--- a/solution.py
+++ b/solution.py
@@ -407,12 +407,14 @@
         else:
             parts, returned[0] = lax.optimization_barrier((parts, returned[0]))
         parts = exchange(parts.reshape(8, count, queries + 16, value), block)
-        parts = lax.dynamic_update_slice_in_dim(
-            parts, beside[None, k * count : (k + 1) * count], position, 0
-        )
         returned.append(parts)
-    mixed = pack(*mix(returned[0], queries))
+    def with_own(parts, k):
+        own_part = beside[None, k * count : (k + 1) * count]
+        return lax.dynamic_update_slice_in_dim(parts, own_part, position, 0)
+
+    mixed = pack(*mix(with_own(returned[0], 0), queries))
     mixed, second = lax.optimization_barrier((mixed, returned[1]))
+    second = with_own(second, 1)
     rows = jnp.concatenate([mixed, pack(*mix(second, queries))], axis=0)
     rows = exchange(rows, sublattice)
     fresh = (fresh[0].reshape(1, queries, value), fresh[1].reshape(1, queries))

time: 188 us -> 185 us (0.984)
  Pallas kernels: 58.8 us -> 53.7 us
  starting transfers between devices: 61.6 us -> 66.6 us
  waiting for transfers between devices: 31 us -> 28.7 us
    pallas_call x3, Pallas kernels: 58.8 us -> 53.7 us  [attention(): pl.pallas_call(functools.partial(body, scale, repeats), out_shape=outs if...]
    all_to_all x6, starting transfers between devices: 61.6 us -> 66.6 us  [exchange(): lax.all_to_all(x, ('batch', 'head'), split_axis=0, concat_axis=0, tiled=T...]
    all_to_all x6, waiting for transfers between devices: 31 us -> 28.7 us  [exchange(): lax.all_to_all(x, ('batch', 'head'), split_axis=0, concat_axis=0, tiled=T...]
  transfers between devices with their start and end apart: 6 -> 6, of which waited for: 3 -> 3; matrix products, arithmetic and copies ran while one was open for 12% -> 13% of each run, Pallas kernels for 31% -> 29%
where the time goes in v9:
time: 185 us
  starting transfers between devices  66.6 us (36%)
  Pallas kernels  53.7 us (29%)
  waiting for transfers between devices  28.7 us (16%)
  local copies, waits for them, and re-layouts  14.3 us (8%)
  other arithmetic  11.3 us (6%)
  matrix products  9.96 us (5%)
    all_to_all x6, starting transfers between devices, exchange(): lax.all_to_all(x, ('batch', 'head'), split_axis=0, concat_axis=0, tiled=T...  66.6 us
    pallas_call x3, Pallas kernels, attention(): pl.pallas_call(functools.partial(body, scale, repeats), out_shape=outs if...  53.7 us
    all_to_all x6, waiting for transfers between devices, exchange(): lax.all_to_all(x, ('batch', 'head'), split_axis=0, concat_axis=0, tiled=T...  28.7 us
    reduce_sum x3, other arithmetic, mix(): jnp.sum(parts[:, :, :queries].astype(jnp.float32) * (share / total)[...,...  4.86 us
    dot_general x1, matrix products, fresh_part(): jnp.einsum('hsl,hlv->hsv', mixed, up_value, preferred_element_type=jnp.fl...  4.62 us
    dot_general x1, matrix products, fresh_part(): jnp.einsum('shn,hnl->hsl', q_nope, up_key, preferred_element_type=jnp.flo...  4.59 us
  transfers between devices with their start and end apart: 6, of which 3 were waited for; matrix products, arithmetic and copies ran while one was open for 13% of the time, Pallas kernels for 29%

profile of v9, /device:TPU:1, one launch (start us, length us, event | category | flops | bytes accessed | tf_op | source)
XLA Modules:
  0.0 185.0 jit_solution(12778661515357363061)
XLA Ops:
  0.0 0.8 reduce.6
  1.1 0.7 reduce.7
  2.5 0.9 reshape.343
  3.7 0.9 copy.55
  4.6 1.0 broadcast_in_dim.87
  5.7 10.8 %all-to-all-start = ((bf16[8,400,128]{2,1,0:T(8,128)(2,1)}), bf16[8,400,128]{2,1,0:T(8,128)(2,1)S(1)}, u32[]{:S(2)}, u32[]{:S(2)}) async-start(bf16[8,400,128]{2,1,0:T(8,128)(2,1)} %broadcast_in_dim.87), calls=%async_computation | async-start | bytes 1638400 | tf_op jit(solution)/shard_map/all_to_all | solution.py:305
  16.5 1.3 copy.41
  17.8 3.3 %copy.42 = bf16[96,64,64]{2,1,0:T(8,128)(2,1)S(1)} copy(bf16[96,64,64]{0,2,1:T(8,128)(2,1)} %bitcast.82) | data formatting | bytes 1572864 | tf_op jit(solution)/shard_map/reshape | solution.py:380
  21.1 1.6 pad.9.keyrope_hbm
  22.8 4.6 %convolution_convert_fusion = bf16[64,4,512]{2,1,0:T(4,128)(2,1)S(1)} fusion(bf16[64,128,512]{2,1,0:T(8,128)(2,1)} %upk_hbm.5, bf16[4,1,8192]{2,0,1:T(4,128)(2,1)S(1)} %copy-done.3), kind=kOutput, calls=%fused_computation.4 | convolution fusion | flops 33685504 | bytes 8716288 | tf_op jit(solution)/shard_map/shn,hnl->hsl/dot_general | solution.py:237
  28.0 0.3 fusion
  28.3 4.6 %fusion.5 = f32[64,4,128]{2,1,0:T(4,128)S(1)} fusion(bf16[64,512,128]{2,1,0:T(8,128)(2,1)} %upv_hbm.5, bf16[64,4,512]{2,0,1:T(8,128)(2,1)S(1)} %fusion), kind=kOutput, calls=%fused_computation.17 | convolution fusion | flops 33554432 | bytes 8781824 | tf_op jit(solution)/shard_map/hsl,hlv->hsv/dot_general | solution.py:254
  33.0 2.1 %broadcast_in_dim.91 = bf16[8,4,400,128]{3,2,1,0:T(8,128)(2,1)} broadcast(bf16[4,400,128]{2,1,0:T(8,128)(2,1)S(1)} %slice.27), dimensions={1,2,3} | broadcast | bytes 3686400 | tf_op jit(solution)/shard_map/broadcast_in_dim | solution.py:311
  35.1 11.9 %all-to-all-start.1 = ((bf16[8,4,400,128]{3,2,1,0:T(8,128)(2,1)}), bf16[8,4,400,128]{3,2,1,0:T(8,128)(2,1)}, u32[]{:S(2)}, u32[]{:S(2)}) async-start(bf16[8,4,400,128]{3,2,1,0:T(8,128)(2,1)} %broadcast_in_dim.91), calls=%async_computation.1 | async-start | bytes 6553600 | tf_op jit(solution)/shard_map/all_to_all | solution.py:305
  47.1 13.6 %attention.3 = (bf16[8,272,128]{2,1,0:T(8,128)(2,1)S(1)}, bf16[8,4,400,128]{3,2,1,0:T(8,128)(2,1)}) custom-call(s32[8,128]{1,0:T(8,128)S(1)} %bitcast.79, s32[2]{0:T(128)S(1)} %pad_add_fusion.place_ref, bf16[8,400,128]{2,1,0:T(8,128)(2,1)S(1)} %all-to-all-done.packed_hbm, bf16[64,128,512]{2,1,0:T(8,128)(2,1)} %upk_hbm.5, bf16[96,64,512]{2,1,0:T(8,128)(2,1)} %lat_hbm.5, ...), custom_call_target="tpu_custom_call" | custom-call | flops 2684354560 | bytes 134217728 | tf_op jit(solution)/shard_map/attention/pallas_call | solution.py:204
  60.7 7.5 %all-to-all-done.1 = bf16[8,4,400,128]{3,2,1,0:T(8,128)(2,1)} async-done(((bf16[8,4,400,128]{3,2,1,0:T(8,128)(2,1)}), bf16[8,4,400,128]{3,2,1,0:T(8,128)(2,1)}, u32[]{:S(2)}, u32[]{:S(2)}) %all-to-all-start.1) | async-done | bytes 3276832 | tf_op jit(solution)/shard_map/all_to_all | solution.py:305
  68.2 9.0 %all-to-all-start.2 = ((bf16[8,4,400,128]{3,2,1,0:T(8,128)(2,1)}), bf16[8,4,400,128]{3,2,1,0:T(8,128)(2,1)}, u32[]{:S(2)}, u32[]{:S(2)}) async-start(bf16[8,4,400,128]{3,2,1,0:T(8,128)(2,1)} %get-tuple-element.25), calls=%async_computation.2 | async-start | bytes 6553600 | tf_op jit(solution)/shard_map/all_to_all | solution.py:305
  77.3 0.9 dynamic-slice_convert_fusion.1
  78.2 20.9 %attention.4 = bf16[32,272,128]{2,1,0:T(8,128)(2,1)} custom-call(s32[32,128]{1,0:T(8,128)S(1)} %bitcast.81, s32[2]{0:T(128)S(1)} %pad_add_fusion.1.place_ref, bf16[32,400,128]{2,1,0:T(8,128)(2,1)} %bitcast.14.packed_hbm, bf16[64,128,512]{2,1,0:T(8,128)(2,1)} %upk_hbm.5, bf16[96,64,512]{2,1,0:T(8,128)(2,1)} %lat_hbm.5, bf16[96,64,128]{2,1,0:T(8,128)(2,1)S(1)} %copy-done.1, ...), custom_call_target="tpu_custom_call" | custom-call | flops 10737418240 | bytes 134217728 | tf_op jit(solution)/shard_map/attention/pallas_call | solution.py:204
  99.1 14.1 %all-to-all-start.3 = ((bf16[8,4,272,128]{3,2,1,0:T(8,128)(2,1)}), bf16[8,4,272,128]{3,2,1,0:T(8,128)(2,1)}, u32[]{:S(2)}, u32[]{:S(2)}) async-start(bf16[8,4,272,128]{3,2,1,0:T(8,128)(2,1)} %bitcast.84), calls=%async_computation.3 | async-start | bytes 4456448 | tf_op jit(solution)/shard_map/all_to_all | solution.py:305
  113.2 0.9 dynamic-slice_convert_fusion
  114.1 19.2 %attention.5 = bf16[32,272,128]{2,1,0:T(8,128)(2,1)} custom-call(s32[32,128]{1,0:T(8,128)S(1)} %bitcast.80, s32[2]{0:T(128)S(1)} %pad_add_fusion.1.place_ref, bf16[32,400,128]{2,1,0:T(8,128)(2,1)} %bitcast.17.packed_hbm, bf16[64,128,512]{2,1,0:T(8,128)(2,1)} %upk_hbm.5, bf16[96,64,512]{2,1,0:T(8,128)(2,1)} %lat_hbm.5, bf16[96,64,128]{2,1,0:T(8,128)(2,1)S(1)} %copy-done.1, ...), custom_call_target="tpu_custom_call" | custom-call | flops 10737418240 | bytes 134217728 | tf_op jit(solution)/shard_map/attention/pallas_call | solution.py:204
  133.3 16.0 %all-to-all-start.4 = ((bf16[8,4,272,128]{3,2,1,0:T(8,128)(2,1)}), bf16[8,4,272,128]{3,2,1,0:T(8,128)(2,1)S(1)}, u32[]{:S(2)}, u32[]{:S(2)}) async-start(bf16[8,4,272,128]{3,2,1,0:T(8,128)(2,1)} %bitcast.83), calls=%async_computation.4 | async-start | bytes 4456448 | tf_op jit(solution)/shard_map/all_to_all | solution.py:305
  149.2 0.7 bitcast_dynamic-update-slice_fusion.1
  150.0 0.8 slice_convert_fusion.1
  151.1 3.2 %multiply_reduce_fusion.1 = bf16[4,256,128]{2,1,0:T(8,128)(2,1)S(1)} fusion(bf16[8,4,272,128]{3,2,1,0:T(8,128)(2,1)} %bitcast_dynamic-update-slice_fusion.1, f32[8,4,256]{2,1,0:T(4,128)S(1)} %bitcast.96), kind=kLoop, calls=%fused_computation.1 | loop fusion | flops 3014656 | bytes 2392064 | tf_op jit(solution)/shard_map/reduce_sum | solution.py:333
  154.7 8.7 %all-to-all-done.4 = bf16[8,4,272,128]{3,2,1,0:T(8,128)(2,1)S(1)} async-done(((bf16[8,4,272,128]{3,2,1,0:T(8,128)(2,1)}), bf16[8,4,272,128]{3,2,1,0:T(8,128)(2,1)S(1)}, u32[]{:S(2)}, u32[]{:S(2)}) %all-to-all-start.4) | async-done | bytes 2228256 | tf_op jit(solution)/shard_map/all_to_all | solution.py:305
  163.7 1.3 multiply_reduce_fusion
  165.3 0.8 pad_maximum_fusion
  166.2 4.8 %all-to-all-start.5 = ((bf16[8,272,128]{2,1,0:T(8,128)(2,1)}), bf16[8,272,128]{2,1,0:T(8,128)(2,1)S(1)}, u32[]{:S(2)}, u32[]{:S(2)}) async-start(bf16[8,272,128]{2,1,0:T(8,128)(2,1)} %pad_maximum_fusion), calls=%async_computation.5 | async-start | bytes 1114112 | tf_op jit(solution)/shard_map/all_to_all | solution.py:305
  171.2 12.5 %all-to-all-done.5 = bf16[8,272,128]{2,1,0:T(8,128)(2,1)S(1)} async-done(((bf16[8,272,128]{2,1,0:T(8,128)(2,1)}), bf16[8,272,128]{2,1,0:T(8,128)(2,1)S(1)}, u32[]{:S(2)}, u32[]{:S(2)}) %all-to-all-start.5) | async-done | bytes 557088 | tf_op jit(solution)/shard_map/all_to_all | solution.py:305
  184.3 0.7 reshape.361
  (79 shorter events, 4.1 us)
Async XLA Ops:
  0.0 27.5 %copy-start = (bf16[4,1,512]{2,0,1:T(4,128)(2,1)S(1)}, bf16[4,1,512]{2,0,1:T(4,128)(2,1)}, u32[]{:S(2)}) copy-start(bf16[4,1,512]{2,0,1:T(4,128)(2,1)} %param.16) | copy-start | bytes 12292
  0.0 16.5 %copy-start.2 = (bf16[96,4096]{1,0:T(8,128)(2,1)S(1)}, bf16[96,4096]{1,0:T(8,128)(2,1)}, u32[]{:S(2)}) copy-start(bf16[96,4096]{1,0:T(8,128)(2,1)} %param.15) | copy-start | bytes 2359300
  5.7 27.3 %all-to-all-start = ((bf16[8,400,128]{2,1,0:T(8,128)(2,1)}), bf16[8,400,128]{2,1,0:T(8,128)(2,1)S(1)}, u32[]{:S(2)}, u32[]{:S(2)}) async-start(bf16[8,400,128]{2,1,0:T(8,128)(2,1)} %broadcast_in_dim.87), calls=%async_computation | async-start | bytes 1638400 | tf_op jit(solution)/shard_map/all_to_all | solution.py:305
  17.8 5.0 %copy-start.3 = (bf16[4,1,8192]{2,0,1:T(4,128)(2,1)S(1)}, bf16[4,1,8192]{2,0,1:T(4,128)(2,1)}, u32[]{:S(2)}) copy-start(bf16[4,1,8192]{2,0,1:T(4,128)(2,1)} %param.10) | copy-start | bytes 196612
  22.8 4.6 %copy-start.4 = (bf16[1,256]{1,0:T(2,128)(2,1)S(1)}, bf16[1,256]{1,0:T(2,128)(2,1)}, u32[]{:S(2)}) copy-start(bf16[1,256]{1,0:T(2,128)(2,1)} %param.17) | copy-start | bytes 1540
  35.1 33.1 %all-to-all-start.1 = ((bf16[8,4,400,128]{3,2,1,0:T(8,128)(2,1)}), bf16[8,4,400,128]{3,2,1,0:T(8,128)(2,1)}, u32[]{:S(2)}, u32[]{:S(2)}) async-start(bf16[8,4,400,128]{3,2,1,0:T(8,128)(2,1)} %broadcast_in_dim.91), calls=%async_computation.1 | async-start | bytes 6553600 | tf_op jit(solution)/shard_map/all_to_all | solution.py:305
  68.2 9.9 %copy-start.1 = (bf16[96,64,128]{2,1,0:T(8,128)(2,1)S(1)}, bf16[96,64,128]{2,1,0:T(8,128)(2,1)}, u32[]{:S(2)}) copy-start(bf16[96,64,128]{2,1,0:T(8,128)(2,1)} %pad.9.keyrope_hbm) | copy-start | bytes 4718596
  68.2 30.9 %all-to-all-start.2 = ((bf16[8,4,400,128]{3,2,1,0:T(8,128)(2,1)}), bf16[8,4,400,128]{3,2,1,0:T(8,128)(2,1)}, u32[]{:S(2)}, u32[]{:S(2)}) async-start(bf16[8,4,400,128]{3,2,1,0:T(8,128)(2,1)} %get-tuple-element.25), calls=%async_computation.2 | async-start | bytes 6553600 | tf_op jit(solution)/shard_map/all_to_all | solution.py:305
  99.1 34.1 %all-to-all-start.3 = ((bf16[8,4,272,128]{3,2,1,0:T(8,128)(2,1)}), bf16[8,4,272,128]{3,2,1,0:T(8,128)(2,1)}, u32[]{:S(2)}, u32[]{:S(2)}) async-start(bf16[8,4,272,128]{3,2,1,0:T(8,128)(2,1)} %bitcast.84), calls=%async_computation.3 | async-start | bytes 4456448 | tf_op jit(solution)/shard_map/all_to_all | solution.py:305
  133.3 30.1 %all-to-all-start.4 = ((bf16[8,4,272,128]{3,2,1,0:T(8,128)(2,1)}), bf16[8,4,272,128]{3,2,1,0:T(8,128)(2,1)S(1)}, u32[]{:S(2)}, u32[]{:S(2)}) async-start(bf16[8,4,272,128]{3,2,1,0:T(8,128)(2,1)} %bitcast.83), calls=%async_computation.4 | async-start | bytes 4456448 | tf_op jit(solution)/shard_map/all_to_all | solution.py:305
  166.2 17.5 %all-to-all-start.5 = ((bf16[8,272,128]{2,1,0:T(8,128)(2,1)}), bf16[8,272,128]{2,1,0:T(8,128)(2,1)S(1)}, u32[]{:S(2)}, u32[]{:S(2)}) async-start(bf16[8,272,128]{2,1,0:T(8,128)(2,1)} %pad_maximum_fusion), calls=%async_computation.5 | async-start | bytes 1114112 | tf_op jit(solution)/shard_map/all_to_all | solution.py:305
